TPU v7x, 32 devices: a whole 2x2x4 slice. The times are simulated.
32 devices in a mesh: section: 4 (over y, x), batch: 8 (over z, core).
Axes of the slice: x: 2, y: 2, z: 4, core: 2. Of those that a mesh axis runs over, the one named last changes fastest.
Arguments:
- tokens: bfloat16 [32, 416, 384], P(('section', 'batch')), may hold values from -6 to 6
- levels: int32 [32], P(('section', 'batch')), may hold values from 5 to 13, as said below
- lead: int32 [32], P(('section', 'batch')), may hold values from 0 to 39
- w_qkv: bfloat16 [4, 384, 1152], P('section', 'batch'), may hold values from -0.3125 to 0.3125
- w_o: bfloat16 [4, 384, 384], P('section', 'batch'), may hold values from -2 to 2
- b_o: bfloat16 [4, 384], P('section', 'batch'), may hold values from -1.796875 to 1.796875
- w_up: bfloat16 [4, 384, 1536], P('section', 'batch'), may hold values from -0.3125 to 0.3125
- b_up: bfloat16 [4, 1536], P('section', 'batch'), may hold values from -1.796875 to 1.796875
- w_down: bfloat16 [4, 1536, 384], P('section', 'batch'), may hold values from -0.15625 to 0.15625
- b_down: bfloat16 [4, 384], P('section', 'batch'), may hold values from -1.796875 to 1.796875
- w_ada: bfloat16 [4, 384, 2304], P('section', 'batch'), may hold values from -0.625 to 0.625
- b_ada: bfloat16 [4, 2304], P('section', 'batch'), may hold values from -1.796875 to 1.796875
- cotangent: bfloat16 [32, 416, 384], P(('section', 'batch')), may hold values from -6 to 6
Outputs:
- result: bfloat16 [32, 416, 384], P(('section', 'batch'))
- grad_tokens: bfloat16 [32, 416, 384], P(('section', 'batch'))
- grad_w_qkv: float32 [4, 384, 1152], P('section', 'batch')
- grad_w_o: float32 [4, 384, 384], P('section', 'batch')
- grad_b_o: float32 [4, 384], P('section', 'batch')
- grad_w_up: float32 [4, 384, 1536], P('section', 'batch')
- grad_b_up: float32 [4, 1536], P('section', 'batch')
- grad_w_down: float32 [4, 1536, 384], P('section', 'batch')
- grad_b_down: float32 [4, 384], P('section', 'batch')
- grad_w_ada: float32 [4, 384, 2304], P('section', 'batch')
- grad_b_ada: float32 [4, 2304], P('section', 'batch')
Inputs may be any that keep to these rules, and one draw needn't show every extreme that they name: Count of pressure levels present in each item; keys of levels at or above it are masked. Some item has 13 and some has 5.
All inputs are finite; a program needn't handle non-finite values.
Results may differ from a plain program's by a relative error of at most 0.019.
Values may be sent and summed in bfloat16 or wider, within the bound.
No kernel may reach another device: no remote copies, remote signals or barrier semaphores. Data moves between devices by JAX's collectives and lax.ppermute only.
A program may use at most 320 MiB of HBM per device.

v0:
```python
import math

import jax
import jax.numpy as jnp
from jax import lax
from jax.sharding import PartitionSpec as P

HEADS = 6
LEVELS = 13


EPS = 1e-06
NEG = -1e30
HIGH = lax.Precision.HIGHEST


def shifted(array, axis, by):
    devices = lax.axis_size(axis)
    pairs = [(i, i + by) for i in range(devices) if 0 <= i + by < devices]
    return lax.ppermute(array, axis, pairs)


def normalize(value):
    centered = value - jnp.mean(value, -1, keepdims=True)
    rstd = lax.rsqrt(jnp.mean(centered * centered, -1, keepdims=True) + EPS)
    return (centered * rstd, rstd)


def normalize_back(grad, normed, rstd):
    return rstd * (
        grad
        - jnp.mean(grad, -1, keepdims=True)
        - normed * jnp.mean(grad * normed, -1, keepdims=True)
    )


def contract_rows(left, right):
    return lax.dot_general(
        left, right, (((0,), (0,)), ((), ())), preferred_element_type=jnp.float32
    )


def contract_cols(left, right):
    return lax.dot_general(
        left, right, (((1,), (1,)), ((), ())), preferred_element_type=jnp.float32
    )


def embed_lead(steps, width):
    half = width // 2
    freq = jnp.exp(-math.log(10000.0) * jnp.arange(half, dtype=jnp.float32) / half)
    angle = 6.0 * steps.astype(jnp.float32)[:, None] * freq[None, :]
    return jnp.concatenate([jnp.sin(angle), jnp.cos(angle)], -1)


def head_probs(query, keys, key_ok, factor):
    raw = jnp.einsum("qe,ke->qk", query, keys, preferred_element_type=jnp.float32) * factor
    return jax.nn.softmax(jnp.where(key_ok[None, :], raw, NEG), -1)


def head_cols(qkv16, part, head, width):
    size = width // HEADS
    return qkv16[:, part * width + head * size : part * width + (head + 1) * size]


def layer_forward(value16, mod, key_ok, weights):
    w_qkv, w_o, b_o, w_up, b_up, w_down, b_down = weights
    width = value16.shape[1]
    factor = (width // HEADS) ** (-0.5)
    shift_a, scale_a, gate_a, shift_b, scale_b, gate_b = jnp.split(mod, 6)
    inputs = value16.astype(jnp.float32)
    normed_a, rstd_a = normalize(inputs)
    hidden_a = (normed_a * (1.0 + scale_a) + shift_a).astype(jnp.bfloat16)
    qkv16 = jnp.dot(hidden_a, w_qkv, preferred_element_type=jnp.float32).astype(jnp.bfloat16)
    pieces = []
    for head in range(HEADS):
        probs = head_probs(
            head_cols(qkv16, 0, head, width), head_cols(qkv16, 1, head, width), key_ok, factor
        )
        pieces.append(
            jnp.dot(
                probs.astype(jnp.bfloat16),
                head_cols(qkv16, 2, head, width),
                preferred_element_type=jnp.float32,
            )
        )
    mixed16 = jnp.concatenate(pieces, -1).astype(jnp.bfloat16)
    branch_a = jnp.dot(mixed16, w_o, preferred_element_type=jnp.float32) + b_o.astype(jnp.float32)
    middle = inputs + gate_a * branch_a
    normed_b, rstd_b = normalize(middle)
    hidden_b = (normed_b * (1.0 + scale_b) + shift_b).astype(jnp.bfloat16)
    pre = jnp.dot(hidden_b, w_up, preferred_element_type=jnp.float32) + b_up.astype(jnp.float32)
    act, act_back = jax.vjp(jax.nn.gelu, pre)
    act16 = act.astype(jnp.bfloat16)
    branch_b = jnp.dot(act16, w_down, preferred_element_type=jnp.float32) + b_down.astype(
        jnp.float32
    )
    result = middle + gate_b * branch_b
    saved = (
        normed_a,
        rstd_a,
        hidden_a,
        qkv16,
        mixed16,
        branch_a,
        normed_b,
        rstd_b,
        hidden_b,
        act_back,
        act16,
        branch_b,
    )
    return (result, saved)


def layer_backward(value16, grad16, mod, cond_row, key_ok, weights):
    w_qkv, w_o, b_o, w_up, b_up, w_down, b_down = weights
    width = value16.shape[1]
    factor = (width // HEADS) ** (-0.5)
    shift_a, scale_a, gate_a, shift_b, scale_b, gate_b = jnp.split(mod, 6)
    result, saved = layer_forward(value16, mod, key_ok, weights)
    (
        normed_a,
        rstd_a,
        hidden_a,
        qkv16,
        mixed16,
        branch_a,
        normed_b,
        rstd_b,
        hidden_b,
        act_back,
        act16,
        branch_b,
    ) = saved
    grad_out = grad16.astype(jnp.float32)
    grad_gate_b = jnp.sum(grad_out * branch_b, 0)
    grad_bb = (grad_out * gate_b).astype(jnp.bfloat16)
    g_w_down = contract_rows(act16, grad_bb)
    g_b_down = jnp.sum(grad_bb.astype(jnp.float32), 0)
    grad_act = contract_cols(grad_bb, w_down)
    grad_pre = act_back(grad_act)[0].astype(jnp.bfloat16)
    g_w_up = contract_rows(hidden_b, grad_pre)
    g_b_up = jnp.sum(grad_pre.astype(jnp.float32), 0)
    grad_hb = contract_cols(grad_pre, w_up)
    grad_shift_b = jnp.sum(grad_hb, 0)
    grad_scale_b = jnp.sum(grad_hb * normed_b, 0)
    grad_middle = grad_out + normalize_back(grad_hb * (1.0 + scale_b), normed_b, rstd_b)
    grad_gate_a = jnp.sum(grad_middle * branch_a, 0)
    grad_ba = (grad_middle * gate_a).astype(jnp.bfloat16)
    g_w_o = contract_rows(mixed16, grad_ba)
    g_b_o = jnp.sum(grad_ba.astype(jnp.float32), 0)
    grad_mixed = contract_cols(grad_ba, w_o).astype(jnp.bfloat16)
    size = width // HEADS
    query_parts, key_parts, value_parts = ([], [], [])
    for head in range(HEADS):
        query = head_cols(qkv16, 0, head, width)
        keys = head_cols(qkv16, 1, head, width)
        values = head_cols(qkv16, 2, head, width)
        grad_head = grad_mixed[:, head * size : (head + 1) * size]
        probs = head_probs(query, keys, key_ok, factor)
        value_parts.append(contract_rows(probs.astype(jnp.bfloat16), grad_head))
        grad_probs = jnp.einsum("qe,ke->qk", grad_head, values, preferred_element_type=jnp.float32)
        grad_raw = (
            probs * (grad_probs - jnp.sum(grad_probs * probs, -1, keepdims=True)) * factor
        ).astype(jnp.bfloat16)
        query_parts.append(jnp.dot(grad_raw, keys, preferred_element_type=jnp.float32))
        key_parts.append(contract_rows(grad_raw, query))
    grad_qkv = jnp.concatenate(query_parts + key_parts + value_parts, -1).astype(jnp.bfloat16)
    g_w_qkv = contract_rows(hidden_a, grad_qkv)
    grad_ha = contract_cols(grad_qkv, w_qkv)
    grad_shift_a = jnp.sum(grad_ha, 0)
    grad_scale_a = jnp.sum(grad_ha * normed_a, 0)
    grad_inputs = grad_middle + normalize_back(grad_ha * (1.0 + scale_a), normed_a, rstd_a)
    grad_mod = jnp.concatenate(
        [grad_shift_a, grad_scale_a, grad_gate_a, grad_shift_b, grad_scale_b, grad_gate_b]
    )
    g_w_ada = cond_row[:, None] * grad_mod[None, :]
    grads = (g_w_qkv, g_w_o, g_b_o, g_w_up, g_b_up, g_w_down, g_b_down, g_w_ada, grad_mod)
    return (grad_inputs.astype(jnp.bfloat16), grads)


def guarded(valid, work, blank):
    return lax.cond(valid, work, blank)


def body(
    tokens, levels, lead, w_qkv, w_o, b_o, w_up, b_up, w_down, b_down, w_ada, b_ada, cotangent
):
    section = lax.axis_index("section")
    sections = lax.axis_size("section")
    token_list = []
    cotan_list = []
    for anchor in range(sections):
        if anchor == 0:
            token_list.append(tokens)
        else:
            token_list.append(shifted(tokens, "section", -anchor))
        if anchor == sections - 1:
            cotan_list.append(cotangent)
        else:
            cotan_list.append(shifted(cotangent, "section", sections - 1 - anchor))
    items = jnp.concatenate(token_list, 0)
    cotangents = jnp.concatenate(cotan_list, 0)
    level_all, lead_all = (
        lax.all_gather(levels, "section", axis=0, tiled=True),
        lax.all_gather(lead, "section", axis=0, tiled=True),
    )
    gathered = (
        lax.all_gather(w_qkv, "batch", axis=1, tiled=True),
        lax.all_gather(w_o, "batch", axis=1, tiled=True),
        lax.all_gather(b_o, "batch", axis=1, tiled=True),
        lax.all_gather(w_up, "batch", axis=1, tiled=True),
        lax.all_gather(b_up, "batch", axis=1, tiled=True),
        lax.all_gather(w_down, "batch", axis=1, tiled=True),
        lax.all_gather(b_down, "batch", axis=1, tiled=True),
        lax.all_gather(w_ada, "batch", axis=1, tiled=True),
        lax.all_gather(b_ada, "batch", axis=1, tiled=True),
    )
    weights = tuple((piece[0] for piece in gathered))
    micro, seq_len, width = items.shape
    cond_all = jax.nn.silu(embed_lead(lead_all, width))
    mods = jnp.dot(cond_all, weights[7].astype(jnp.float32), precision=HIGH) + weights[8].astype(
        jnp.float32
    )
    patch = seq_len // LEVELS
    key_table = (jnp.arange(seq_len) // patch)[None, :] < level_all[:, None]
    slots = jnp.arange(micro)
    ticks = micro + sections - 1
    forward_weights = weights[:7]

    def blank_act():
        return jnp.zeros((seq_len, width), jnp.bfloat16)

    receive = jnp.zeros((seq_len, width), jnp.bfloat16)
    kept = jnp.zeros((micro, seq_len, width), jnp.bfloat16)
    finals = jnp.zeros((micro, seq_len, width), jnp.bfloat16)
    for tick in range(ticks):
        index = tick - section
        valid = (index >= 0) & (index < micro)
        pick = jnp.clip(index, 0, micro - 1)
        entering = jnp.where(section == 0, items[min(tick, micro - 1)], receive)
        leaving = guarded(
            valid,
            lambda: layer_forward(entering, mods[pick], key_table[pick], forward_weights)[0].astype(
                jnp.bfloat16
            ),
            blank_act,
        )
        hit = (valid & (slots == index))[:, None, None]
        kept = jnp.where(hit, entering[None], kept)
        finals = jnp.where(hit, leaving[None], finals)
        if tick < ticks - 1:
            receive = shifted(leaving, "section", 1)
    totals = tuple((jnp.zeros(piece.shape, jnp.float32) for piece in weights))
    shards = tuple(
        (
            jnp.zeros(piece.shape, jnp.float32)
            for piece in (w_qkv, w_o, b_o, w_up, b_up, w_down, b_down, w_ada, b_ada)
        )
    )

    def blank_back():
        return (
            jnp.zeros((seq_len, width), jnp.bfloat16),
            tuple((jnp.zeros(piece.shape, jnp.float32) for piece in weights)),
        )

    receive = jnp.zeros((seq_len, width), jnp.bfloat16)
    input_grads = jnp.zeros((micro, seq_len, width), jnp.bfloat16)
    for tick in range(ticks):
        index = tick - (sections - 1 - section)
        valid = (index >= 0) & (index < micro)
        pick = jnp.clip(index, 0, micro - 1)
        entering = jnp.where(section == sections - 1, cotangents[min(tick, micro - 1)], receive)
        saved_in = kept[pick]
        grad_in, grads = guarded(
            valid,
            lambda: layer_backward(
                saved_in, entering, mods[pick], cond_all[pick], key_table[pick], forward_weights
            ),
            blank_back,
        )
        hit = (valid & (slots == index))[:, None, None]
        input_grads = jnp.where(hit, grad_in[None], input_grads)
        totals = tuple((left + right for left, right in zip(totals, grads)))
        if tick < ticks - 1:
            receive = shifted(grad_in, "section", -1)
    t_qkv, t_o, t_bo, t_up, t_bup, t_down, t_bdown, t_ada, t_bada = totals
    shards = (
        lax.psum_scatter(t_qkv[None], "batch", scatter_dimension=1, tiled=True),
        lax.psum_scatter(t_o[None], "batch", scatter_dimension=1, tiled=True),
        lax.psum_scatter(t_bo[None], "batch", scatter_dimension=1, tiled=True),
        lax.psum_scatter(t_up[None], "batch", scatter_dimension=1, tiled=True),
        lax.psum_scatter(t_bup[None], "batch", scatter_dimension=1, tiled=True),
        lax.psum_scatter(t_down[None], "batch", scatter_dimension=1, tiled=True),
        lax.psum_scatter(t_bdown[None], "batch", scatter_dimension=1, tiled=True),
        lax.psum_scatter(t_ada[None], "batch", scatter_dimension=1, tiled=True),
        lax.psum_scatter(t_bada[None], "batch", scatter_dimension=1, tiled=True),
    )
    share = micro // sections
    result = jnp.zeros((share, seq_len, width), jnp.bfloat16)
    grad_tokens = jnp.zeros((share, seq_len, width), jnp.bfloat16)
    for target in range(sections):
        out_piece = finals[target * share : (target + 1) * share]
        grad_piece = input_grads[target * share : (target + 1) * share]
        if target != sections - 1:
            out_piece = shifted(out_piece, "section", target - (sections - 1))
        if target != 0:
            grad_piece = shifted(grad_piece, "section", target)
        result = jnp.where(section == target, out_piece, result)
        grad_tokens = jnp.where(section == target, grad_piece, grad_tokens)
    s_qkv, s_o, s_bo, s_up, s_bup, s_down, s_bdown, s_ada, s_bada = shards
    return (result, grad_tokens, s_qkv, s_o, s_bo, s_up, s_bup, s_down, s_bdown, s_ada, s_bada)


def solution(mesh):
    in_specs = (
        P(("section", "batch"), None, None),
        P(("section", "batch")),
        P(("section", "batch")),
        P("section", "batch", None),
        P("section", "batch", None),
        P("section", "batch"),
        P("section", "batch", None),
        P("section", "batch"),
        P("section", "batch", None),
        P("section", "batch"),
        P("section", "batch", None),
        P("section", "batch"),
        P(("section", "batch"), None, None),
    )
    out_specs = (
        P(("section", "batch"), None, None),
        P(("section", "batch"), None, None),
        P("section", "batch", None),
        P("section", "batch", None),
        P("section", "batch"),
        P("section", "batch", None),
        P("section", "batch"),
        P("section", "batch", None),
        P("section", "batch"),
        P("section", "batch", None),
        P("section", "batch"),
    )
    return jax.shard_map(body, mesh=mesh, in_specs=in_specs, out_specs=out_specs, check_vma=False)
```

profile of v0, /device:TPU:0, one launch (start us, length us, event | category | flops | bytes accessed | tf_op | source)
XLA Modules:
  0.0 1129.0 jit_solution(15874289195323046690)
XLA Ops:
  14.8 14.7 %all-reduce.6 = (s32[4]{0:T(128)S(1)}, s32[4]{0:T(128)S(1)}) all-reduce(s32[4]{0:T(128)S(1)} %dynamic-update-slice, s32[4]{0:T(128)S(1)} %dynamic-update-slice.2), channel_id=1, replica_groups=mesh['section'=4,'batch'=8] {'section'}, use_global_device_ids=true, to_apply=%add | all-reduce | flops 8 | bytes 64
  36.3 28.0 %all-reduce.7 = (bf16[2304]{0:T(1024)(128)(2,1)S(1)}, bf16[384]{0:T(512)(128)(2,1)S(1)}, bf16[1536]{0:T(1024)(128)(2,1)S(1)}, bf16[384]{0:T(512)(128)(2,1)S(1)}) all-reduce(bf16[2304]{0:T(1024)(128)(2,1)S(1)} %dynamic-update-slice.1, bf16[384]{0:T(512)(128)(2,1)S(1)} %dynamic-update-slice.3, ...), channel_id=1, replica_groups=mesh['section'=4,'batch'=8] {'batch'}, use_global_device_ids=true, to_apply=%add.1 | all-reduce | flops 4608 | bytes 18432
  64.5 15.0 %all_gather.38 = bf16[1,384,384]{2,1,0:T(8,128)(2,1)S(1)} all-gather(bf16[1,48,384]{2,1,0:T(8,128)(2,1)} %param.45), channel_id=1, replica_groups=mesh['section'=4,'batch'=8] {'batch'}, dimensions={1}, use_global_device_ids=true | all-gather | bytes 331776 | tf_op jit(solution)/shard_map/all_gather | solution.py:211
  79.6 17.3 %all_gather.37 = bf16[1,384,1152]{2,1,0:T(8,128)(2,1)S(1)} all-gather(bf16[1,48,1152]{2,1,0:T(8,128)(2,1)} %param.44), channel_id=1, replica_groups=mesh['section'=4,'batch'=8] {'batch'}, dimensions={1}, use_global_device_ids=true | all-gather | bytes 995328 | tf_op jit(solution)/shard_map/all_gather | solution.py:210
  100.4 24.7 %conditional.14 = (bf16[416,384]{1,0:T(8,128)(2,1)S(1)}) conditional(s32[]{:T(128)} %convert_element_type.1496, () %tuple.140, (bf16[1,416,384]{2,1,0:T(8,128)(2,1)S(1)}, pred[416,384]{1,0:T(8,128)(4,1)S(1)}, bf16[416,384]{1,0:T(8,128)(2,1)}, s32[]{:T(128)}, f32[4,2304]{1,0:T(4,128)S(1)}, /*index=5*/pred[4,416]{1,0:T(4,128)(4,1)S(1)}, ...), branch_computations={%region_0.1_spmd, %region_1.18_spmd} | conditional | flops 1758141440 | bytes 24599416 | solution.py:184
  121.7 3.3 fusion.18
  127.7 6.2 collective-permute-done.3
  134.0 24.4 %conditional.15 = (bf16[416,384]{1,0:T(8,128)(2,1)S(1)}) conditional(s32[]{:T(128)} %convert_element_type.1495, () %tuple.139, (bf16[416,384]{1,0:T(8,128)(2,1)S(1)}, s32[]{:T(128)}, f32[4,2304]{1,0:T(4,128)S(1)}, pred[4,416]{1,0:T(4,128)(4,1)S(1)}, bf16[384,1152]{1,0:T(8,128)(2,1)}, /*index=5*/bf16[384,384]{1,0:T(8,128)(2,1)S(1)}, ...), branch_computations={%region_18.19_spmd, %region_19.36_spmd} | conditional | flops 1757981696 | bytes 23800696 | solution.py:184
  158.5 4.4 collective-permute-start.4
  164.2 5.4 collective-permute-done.4
  169.6 24.5 %conditional.16 = (bf16[416,384]{1,0:T(8,128)(2,1)S(1)}) conditional(s32[]{:T(128)} %convert_element_type.1494, () %tuple.138, (bf16[416,384]{1,0:T(8,128)(2,1)S(1)}, s32[]{:T(128)}, f32[4,2304]{1,0:T(4,128)S(1)}, pred[4,416]{1,0:T(4,128)(4,1)S(1)}, bf16[384,1152]{1,0:T(8,128)(2,1)}, /*index=5*/bf16[384,384]{1,0:T(8,128)(2,1)S(1)}, ...), branch_computations={%region_36.37_spmd, %region_37.54_spmd} | conditional | flops 1757981696 | bytes 23800696 | solution.py:184
  190.8 3.3 fusion.154
  194.2 4.7 collective-permute-start.5
  198.8 5.5 collective-permute-done.5
  204.4 24.3 %conditional.17 = (bf16[416,384]{1,0:T(8,128)(2,1)S(1)}) conditional(s32[]{:T(128)} %convert_element_type.1493, () %tuple.137, (bf16[416,384]{1,0:T(8,128)(2,1)S(1)}, s32[]{:T(128)}, f32[4,2304]{1,0:T(4,128)S(1)}, pred[4,416]{1,0:T(4,128)(4,1)S(1)}, bf16[384,1152]{1,0:T(8,128)(2,1)}, /*index=5*/bf16[384,384]{1,0:T(8,128)(2,1)S(1)}, ...), branch_computations={%region_54.55_spmd, %region_55.72_spmd} | conditional | flops 1757981696 | bytes 23800696 | solution.py:184
  225.4 3.3 fusion.222
  228.7 4.4 collective-permute-start.6
  242.4 30.2 %collective-permute-start.7 = (bf16[416,384]{1,0:T(8,128)(2,1)}, bf16[416,384]{1,0:T(8,128)(2,1)S(1)}, u32[]{:S(2)}, u32[]{:S(2)}) collective-permute-start(bf16[416,384]{1,0:T(8,128)(2,1)} %get-tuple-element.1929), channel_id=1, source_target_pairs={{0,8},{8,16},{16,24},{1,9},{9,17},{17,25},{2,10},{10,18},{18,26},{... | collective-permute-start | bytes 958472 | tf_op jit(solution)/shard_map/ppermute | solution.py:20
  272.6 4.7 collective-permute-done.7
  278.3 4.3 collective-permute-start.8
  283.7 3.7 collective-permute-done.8
  288.3 16.8 %conditional.21 = (bf16[416,384]{1,0:T(8,128)(2,1)}, f32[384,1152]{1,0:T(8,128)S(1)}, f32[384,384]{1,0:T(8,128)}, f32[384]{0:T(512)}, f32[384,1536]{1,0:T(8,128)...) conditional(s32[]{:T(128)} %convert_element_type.1504, ...), branch_computations={%region_126.127_spmd, %region_127.163_spmd} | conditional | flops 5279537152 | bytes 118788120 | solution.py:184
  306.5 32.7 %collective-permute-start.12 = (bf16[1,416,384]{2,1,0:T(8,128)(2,1)}, bf16[1,416,384]{2,1,0:T(8,128)(2,1)}, u32[]{:S(2)}, u32[]{:S(2)}) collective-permute-start(bf16[1,416,384]{2,1,0:T(8,128)(2,1)} %param.53), channel_id=1, source_target_pairs={{0,8},{8,16},{16,24},{1,9},{9,17},{17,25},{2,10},{10,18},{18,26},{... | collective-permute-start | bytes 958472 | tf_op jit(solution)/shard_map/ppermute | solution.py:20
  339.1 5.2 collective-permute-done.15
  344.3 17.1 %conditional.22 = (bf16[416,384]{1,0:T(8,128)(2,1)}, f32[384,1152]{1,0:T(8,128)}, f32[384,384]{1,0:T(8,128)}, f32[384]{0:T(512)S(1)}, f32[384,1536]{1,0:T(8,128)...) conditional(s32[]{:T(128)} %convert_element_type.1503, ...), branch_computations={%region_163.164_spmd, %region_164.200_spmd} | conditional | flops 5279537152 | bytes 118757504 | solution.py:184
  363.3 7.8 collective-permute-done.16
  371.1 16.1 %conditional.23 = (bf16[416,384]{1,0:T(8,128)(2,1)}, f32[384,1152]{1,0:T(8,128)S(1)}, f32[384,384]{1,0:T(8,128)}, f32[384]{0:T(512)}, f32[384,1536]{1,0:T(8,128)...) conditional(s32[]{:T(128)} %convert_element_type.1502, ...), branch_computations={%region_200.201_spmd, %region_201.237_spmd} | conditional | flops 5279537152 | bytes 120066104 | solution.py:184
  388.4 139.1 %collective-permute-done.17 = bf16[416,384]{1,0:T(8,128)(2,1)} collective-permute-done((bf16[416,384]{1,0:T(8,128)(2,1)}, bf16[416,384]{1,0:T(8,128)(2,1)}, u32[]{:S(2)}, u32[]{:S(2)}) %collective-permute-start.17) | collective-permute-done | bytes 319520 | tf_op jit(solution)/shard_map/ppermute | solution.py:20
  527.5 61.7 %conditional.24 = (bf16[416,384]{1,0:T(8,128)(2,1)}, f32[384,1152]{1,0:T(8,128)}, f32[384,384]{1,0:T(8,128)}, f32[384]{0:T(512)S(1)}, f32[384,1536]{1,0:T(8,128)...) conditional(s32[]{:T(128)} %convert_element_type.1501, ...), branch_computations={%region_237.238_spmd, %region_238.274_spmd} | conditional | flops 5279537152 | bytes 118757504 | solution.py:184
  591.1 8.7 collective-permute-done.18
  599.8 62.1 %conditional.25 = (bf16[416,384]{1,0:T(8,128)(2,1)}, f32[384,1152]{1,0:T(8,128)S(1)}, f32[384,384]{1,0:T(8,128)}, f32[384]{0:T(512)}, f32[384,1536]{1,0:T(8,128)...) conditional(s32[]{:T(128)} %convert_element_type.1500, ...), branch_computations={%region_274.275_spmd, %region_275.311_spmd} | conditional | flops 5279537152 | bytes 120066104 | solution.py:184
  663.3 8.8 collective-permute-done.19
  672.1 61.7 %conditional.26 = (bf16[416,384]{1,0:T(8,128)(2,1)}, f32[384,1152]{1,0:T(8,128)}, f32[384,384]{1,0:T(8,128)}, f32[384]{0:T(512)S(1)}, f32[384,1536]{1,0:T(8,128)...) conditional(s32[]{:T(128)} %convert_element_type.1499, ...), branch_computations={%region_311.312_spmd, %region_312.348_spmd} | conditional | flops 5279537152 | bytes 118757504 | solution.py:184
  735.7 8.7 collective-permute-done.20
  744.4 62.0 %conditional.27 = (bf16[416,384]{1,0:T(8,128)(2,1)}, f32[384,1152]{1,0:T(8,128)S(1)}, f32[384,384]{1,0:T(8,128)S(1)}, f32[384]{0:T(512)S(1)}, f32[384,1536]{1,0:...) conditional(s32[]{:T(128)} %convert_element_type.1498, ...), branch_computations={%region_348.349_spmd, %region_349.385_spmd} | conditional | flops 5279537152 | bytes 122425304 | solution.py:184
  817.7 5.9 add_bitcast_fusion.3
  823.7 9.2 add_bitcast_fusion.2
  833.0 7.9 add_bitcast_fusion.1
  841.0 11.5 %add_bitcast_fusion = f32[1,384,2304]{2,1,0:T(8,128)} fusion(f32[384,2304]{1,0:T(8,128)} %get-tuple-element.1253, f32[384,2304]{1,0:T(8,128)} %get-tuple-element.1252, f32[384,2304]{1,0:T(8,128)} %get-tuple-element.1251, f32[384,2304]{1,0:T(8,128)} %get-tuple-element.1250, f32[384,2304]{1,0:T(8,128)} %get-tuple-element.1249, ...), kind=kLoop, calls=%fused_computation.2405 | loop fusion | flops 5308416 | bytes 28311552 | tf_op jit(solution)/shard_map/broadcast_in_dim | solution.py:298
  864.7 4.6 collective-permute-start.23
  869.3 6.0 collective-permute-start.22
  881.8 16.8 %reduce-scatter.30.cloned.1.call-done = f32[192,1]{1,0:T(8,128)} async-done(((f32[1536,1]{1,0:T(8,128)}), f32[192,1]{1,0:T(8,128)}) %reduce-scatter.30.cloned.1.call-update) | async-done | bytes 784
  900.1 31.9 %reduce-scatter.34.cloned.1.call-done = f32[288,1]{1,0:T(8,128)} async-done(((f32[2304,1]{1,0:T(8,128)}), f32[288,1]{1,0:T(8,128)}) %reduce-scatter.34.cloned.1.call-update) | async-done | bytes 1168
  934.4 29.9 %reduce-scatter.20.cloned.1.call-done = f32[1,48,384]{2,1,0:T(8,128)} async-done(((f32[1,384,384]{2,1,0:T(8,128)}), f32[1,48,384]{2,1,0:T(8,128)}) %reduce-scatter.20.cloned.1.call-update) | async-done | bytes 73744 | tf_op jit(solution)/shard_map/reduce_scatter | solution.py:292
  964.3 36.2 %reduce-scatter.18.cloned.1.call-done = f32[1,48,1152]{2,1,0:T(8,128)} async-done(((f32[1,384,1152]{2,1,0:T(8,128)}), f32[1,48,1152]{2,1,0:T(8,128)}) %reduce-scatter.18.cloned.1.call-update) | async-done | bytes 221200 | tf_op jit(solution)/shard_map/reduce_scatter | solution.py:291
  1000.4 37.1 %reduce-scatter.22.cloned.1.call-done = f32[1,48,1536]{2,1,0:T(8,128)} async-done(((f32[1,384,1536]{2,1,0:T(8,128)}), f32[1,48,1536]{2,1,0:T(8,128)}) %reduce-scatter.22.cloned.1.call-update) | async-done | bytes 294928 | tf_op jit(solution)/shard_map/reduce_scatter | solution.py:294
  1037.6 38.4 %reduce-scatter.24.cloned.1.call-done = f32[1,192,384]{2,1,0:T(8,128)} async-done(((f32[1,1536,384]{2,1,0:T(8,128)}), f32[1,192,384]{2,1,0:T(8,128)}) %reduce-scatter.24.cloned.1.call-update) | async-done | bytes 294928 | tf_op jit(solution)/shard_map/reduce_scatter | solution.py:296
  1076.0 45.9 %reduce-scatter.26.cloned.1.call-done = f32[1,48,2304]{2,1,0:T(8,128)} async-done(((f32[1,384,2304]{2,1,0:T(8,128)}), f32[1,48,2304]{2,1,0:T(8,128)}) %reduce-scatter.26.cloned.1.call-update) | async-done | bytes 442384 | tf_op jit(solution)/shard_map/reduce_scatter | solution.py:298
  (791 shorter events, 436.5 us)
Async XLA Ops:
  7.2 89.7 %all-gather.4.cloned.1.call-start = ((), (), s32[]{:S(2)}) async-start(), calls=%async_computation.9 | async-start | bytes 1990656 | tf_op jit(solution)/shard_map/all_gather | solution.py:217
  7.9 91.7 %all-gather.6.cloned.1.call-start = ((), (), s32[]{:S(2)}) async-start(), calls=%async_computation.10 | async-start | bytes 1327104 | tf_op jit(solution)/shard_map/all_gather | solution.py:213
  8.7 90.9 %all-gather.8.cloned.1.call-start = ((), (), s32[]{:S(2)}) async-start(), calls=%async_computation.11 | async-start | bytes 1327104 | tf_op jit(solution)/shard_map/all_gather | solution.py:215
  9.4 869.7 %reduce-scatter.28.cloned.1.call-start = ((), (), s32[]{:S(2)}) async-start(), calls=%async_computation.17 | async-start | bytes 221184
  13.5 114.2 %collective-permute-start.2 = (bf16[1,416,384]{2,1,0:T(8,128)(2,1)}, bf16[1,416,384]{2,1,0:T(8,128)(2,1)S(1)}, u32[]{:S(2)}, u32[]{:S(2)}) collective-permute-start(bf16[1,416,384]{2,1,0:T(8,128)(2,1)} %param.41), channel_id=1, source_target_pairs={{8,0},{16,8},{24,16},{9,1},{17,9},{25,17},{10,2},{18,10},{26,18},{... | collective-permute-start | bytes 958472 | tf_op jit(solution)/shard_map/ppermute | solution.py:20
  64.5 35.0 %copy-start.42 = (f32[4,384]{1,0:T(4,128)}, f32[4,384]{1,0:T(4,128)S(1)}, u32[]{:S(2)}) copy-start(f32[4,384]{1,0:T(4,128)S(1)} %divide_multiply_fusion) | copy-start | bytes 18436
  125.1 8.9 collective-permute-start.3
  126.4 37.8 %collective-permute-start.1 = (bf16[1,416,384]{2,1,0:T(8,128)(2,1)S(1)}, bf16[1,416,384]{2,1,0:T(8,128)(2,1)S(1)}, u32[]{:S(2)}, u32[]{:S(2)}) collective-permute-start(bf16[1,416,384]{2,1,0:T(8,128)(2,1)S(1)} %copy-done.15), channel_id=1, source_target_pairs={{16,0},{24,8},{17,1},{25,9},{18,2},{26,10},{19,3},{27,11},{20,4},{... | collective-permute-start | bytes 958472 | tf_op jit(solution)/shard_map/ppermute | solution.py:20
  158.5 11.1 collective-permute-start.4
  162.9 36.0 %collective-permute-start = (bf16[1,416,384]{2,1,0:T(8,128)(2,1)S(1)}, bf16[1,416,384]{2,1,0:T(8,128)(2,1)S(1)}, u32[]{:S(2)}, u32[]{:S(2)}) collective-permute-start(bf16[1,416,384]{2,1,0:T(8,128)(2,1)S(1)} %copy-done.15), channel_id=1, source_target_pairs={{24,0},{25,1},{26,2},{27,3},{28,4},{29,5},{30,6},{31,7}} | collective-permute-start | bytes 958472 | tf_op jit(solution)/shard_map/ppermute | solution.py:20
  194.2 10.2 collective-permute-start.5
  228.7 12.4 %collective-permute-start.6 = (bf16[416,384]{1,0:T(8,128)(2,1)S(1)}, bf16[416,384]{1,0:T(8,128)(2,1)S(1)}, u32[]{:S(2)}, u32[]{:S(2)}) collective-permute-start(bf16[416,384]{1,0:T(8,128)(2,1)S(1)} %get-tuple-element.1928), channel_id=1, source_target_pairs={{0,8},{8,16},{16,24},{1,9},{9,17},{17,25},{2,10},{10,18},{18,26},{... | collective-permute-start | bytes 958472 | tf_op jit(solution)/shard_map/ppermute | solution.py:20
  233.1 55.1 %collective-permute-start.14 = (bf16[1,416,384]{2,1,0:T(8,128)(2,1)}, bf16[1,416,384]{2,1,0:T(8,128)(2,1)}, u32[]{:S(2)}, u32[]{:S(2)}) collective-permute-start(bf16[1,416,384]{2,1,0:T(8,128)(2,1)} %param.53), channel_id=1, source_target_pairs={{0,24},{1,25},{2,26},{3,27},{4,28},{5,29},{6,30},{7,31}} | collective-permute-start | bytes 958472 | tf_op jit(solution)/shard_map/ppermute | solution.py:20
  235.2 104.0 %collective-permute-start.13 = (bf16[1,416,384]{2,1,0:T(8,128)(2,1)}, bf16[1,416,384]{2,1,0:T(8,128)(2,1)}, u32[]{:S(2)}, u32[]{:S(2)}) collective-permute-start(bf16[1,416,384]{2,1,0:T(8,128)(2,1)} %param.53), channel_id=1, source_target_pairs={{0,16},{8,24},{1,17},{9,25},{2,18},{10,26},{3,19},{11,27},{4,20},{... | collective-permute-start | bytes 958472 | tf_op jit(solution)/shard_map/ppermute | solution.py:20
  238.1 49.4 %copy-start.82 = (pred[4]{0:T(512)(128)(4,1)}, pred[4]{0:T(512)(128)(4,1)S(1)}, u32[]{:S(2)}) copy-start(pred[4]{0:T(512)(128)(4,1)S(1)} %compare_and_fusion.11) | copy-start | bytes 16
  242.4 35.0 %collective-permute-start.7 = (bf16[416,384]{1,0:T(8,128)(2,1)}, bf16[416,384]{1,0:T(8,128)(2,1)S(1)}, u32[]{:S(2)}, u32[]{:S(2)}) collective-permute-start(bf16[416,384]{1,0:T(8,128)(2,1)} %get-tuple-element.1929), channel_id=1, source_target_pairs={{0,8},{8,16},{16,24},{1,9},{9,17},{17,25},{2,10},{10,18},{18,26},{... | collective-permute-start | bytes 958472 | tf_op jit(solution)/shard_map/ppermute | solution.py:20
  272.6 14.9 %copy-start.84 = (pred[4]{0:T(512)(128)(4,1)}, pred[4]{0:T(512)(128)(4,1)S(1)}, u32[]{:S(2)}) copy-start(pred[4]{0:T(512)(128)(4,1)S(1)} %compare_and_fusion.7) | copy-start | bytes 16
  272.6 14.9 %copy-start.74 = (pred[4]{0:T(512)(128)(4,1)}, pred[4]{0:T(512)(128)(4,1)S(1)}, u32[]{:S(2)}) copy-start(pred[4]{0:T(512)(128)(4,1)S(1)} %get-tuple-element.1783) | copy-start | bytes 16
  272.6 14.9 %copy-start.76 = (pred[4]{0:T(512)(128)(4,1)}, pred[4]{0:T(512)(128)(4,1)S(1)}, u32[]{:S(2)}) copy-start(pred[4]{0:T(512)(128)(4,1)S(1)} %get-tuple-element.1784) | copy-start | bytes 16
  278.3 9.1 collective-permute-start.8
  305.1 39.2 %copy-start.2 = (f32[384,1152]{1,0:T(8,128)}, f32[384,1152]{1,0:T(8,128)S(1)}, u32[]{:S(2)}) copy-start(f32[384,1152]{1,0:T(8,128)S(1)} %get-tuple-element.1198) | copy-start | bytes 5308420
  305.2 39.2 %collective-permute-start.15 = (bf16[416,384]{1,0:T(8,128)(2,1)}, bf16[416,384]{1,0:T(8,128)(2,1)}, u32[]{:S(2)}, u32[]{:S(2)}) collective-permute-start(bf16[416,384]{1,0:T(8,128)(2,1)} %get-tuple-element.1191), channel_id=1, source_target_pairs={{8,0},{16,8},{24,16},{9,1},{17,9},{25,17},{10,2},{18,10},{26,18},{... | collective-permute-start | bytes 958472 | tf_op jit(solution)/shard_map/ppermute | solution.py:20
  306.5 56.8 %collective-permute-start.12 = (bf16[1,416,384]{2,1,0:T(8,128)(2,1)}, bf16[1,416,384]{2,1,0:T(8,128)(2,1)}, u32[]{:S(2)}, u32[]{:S(2)}) collective-permute-start(bf16[1,416,384]{2,1,0:T(8,128)(2,1)} %param.53), channel_id=1, source_target_pairs={{0,8},{8,16},{16,24},{1,9},{9,17},{17,25},{2,10},{10,18},{18,26},{... | collective-permute-start | bytes 958472 | tf_op jit(solution)/shard_map/ppermute | solution.py:20
  362.0 9.1 collective-permute-start.16
  387.1 140.4 %copy-start.4 = (f32[384,1152]{1,0:T(8,128)}, f32[384,1152]{1,0:T(8,128)S(1)}, u32[]{:S(2)}) copy-start(f32[384,1152]{1,0:T(8,128)S(1)} %get-tuple-element.1200) | copy-start | bytes 5308420
  387.1 140.4 %collective-permute-start.17 = (bf16[416,384]{1,0:T(8,128)(2,1)}, bf16[416,384]{1,0:T(8,128)(2,1)}, u32[]{:S(2)}, u32[]{:S(2)}) collective-permute-start(bf16[416,384]{1,0:T(8,128)(2,1)} %get-tuple-element.1193), channel_id=1, source_target_pairs={{8,0},{16,8},{24,16},{9,1},{17,9},{25,17},{10,2},{18,10},{26,18},{... | collective-permute-start | bytes 958472 | tf_op jit(solution)/shard_map/ppermute | solution.py:20
  589.8 10.0 collective-permute-start.18
  601.5 54.7 %copy-start.45 = (f32[416]{0:T(512)}, f32[416]{0:T(512)S(1)}, u32[]{:S(2)}) copy-start(f32[416]{0:T(512)S(1)} %broadcast_multiply_fusion.48) | copy-start | bytes 4996 | tf_op jit(solution)/shard_map/cond
  601.6 54.5 %copy-start.49 = (f32[384]{0:T(512)}, f32[384]{0:T(512)S(1)}, u32[]{:S(2)}) copy-start(f32[384]{0:T(512)S(1)} %get-tuple-element.1370) | copy-start | bytes 4612 | tf_op jit(solution)/shard_map/cond
  603.6 52.5 %copy-start.53 = (f32[416]{0:T(512)}, f32[416]{0:T(512)S(1)}, u32[]{:S(2)}) copy-start(f32[416]{0:T(512)S(1)} %add_rsqrt_fusion.23) | copy-start | bytes 4996 | tf_op jit(solution)/shard_map/cond
  662.0 10.1 collective-permute-start.19
  734.4 10.0 collective-permute-start.20
  746.0 54.7 %copy-start.46 = (f32[416]{0:T(512)}, f32[416]{0:T(512)S(1)}, u32[]{:S(2)}) copy-start(f32[416]{0:T(512)S(1)} %broadcast_multiply_fusion.62) | copy-start | bytes 4996 | tf_op jit(solution)/shard_map/cond
  746.1 54.6 %copy-start.50 = (f32[384]{0:T(512)}, f32[384]{0:T(512)S(1)}, u32[]{:S(2)}) copy-start(f32[384]{0:T(512)S(1)} %get-tuple-element.1398) | copy-start | bytes 4612 | tf_op jit(solution)/shard_map/cond
  808.5 71.9 %reduce-scatter.32.cloned.1.call-start = ((), (), s32[]{:S(2)}) async-start(), calls=%async_computation.19 | async-start | bytes 221184
  810.1 88.4 %reduce-scatter.30.cloned.1.call-start = ((), (), s32[]{:S(2)}) async-start(), calls=%async_computation.18 | async-start | bytes 884736
  812.2 119.8 %reduce-scatter.34.cloned.1.call-start = ((), (), s32[]{:S(2)}) async-start(), calls=%async_computation.20 | async-start | bytes 1327104
  814.4 149.8 %reduce-scatter.20.cloned.1.call-start = ((), (), s32[]{:S(2)}) async-start(), calls=%async_computation.13 | async-start | bytes 663552 | tf_op jit(solution)/shard_map/reduce_scatter | solution.py:292
  817.7 182.8 %reduce-scatter.18.cloned.1.call-start = ((), (), s32[]{:S(2)}) async-start(), calls=%async_computation.12 | async-start | bytes 1990656 | tf_op jit(solution)/shard_map/reduce_scatter | solution.py:291
  823.7 213.9 %reduce-scatter.22.cloned.1.call-start = ((), (), s32[]{:S(2)}) async-start(), calls=%async_computation.14 | async-start | bytes 2654208 | tf_op jit(solution)/shard_map/reduce_scatter | solution.py:294
  833.0 243.0 %reduce-scatter.24.cloned.1.call-start = ((), (), s32[]{:S(2)}) async-start(), calls=%async_computation.15 | async-start | bytes 2654208 | tf_op jit(solution)/shard_map/reduce_scatter | solution.py:296
  841.0 280.9 %reduce-scatter.26.cloned.1.call-start = ((), (), s32[]{:S(2)}) async-start(), calls=%async_computation.16 | async-start | bytes 3981312 | tf_op jit(solution)/shard_map/reduce_scatter | solution.py:298
  857.9 17.4 %collective-permute-start.11 = (bf16[1,416,384]{2,1,0:T(8,128)(2,1)S(1)}, bf16[1,416,384]{2,1,0:T(8,128)(2,1)}, u32[]{:S(2)}, u32[]{:S(2)}) collective-permute-start(bf16[1,416,384]{2,1,0:T(8,128)(2,1)S(1)} %get-tuple-element.1776), channel_id=1, source_target_pairs={{24,0},{25,1},{26,2},{27,3},{28,4},{29,5},{30,6},{31,7}} | collective-permute-start | bytes 958472 | tf_op jit(solution)/shard_map/ppermute | solution.py:20
  859.2 18.1 %collective-permute-start.10 = (bf16[1,416,384]{2,1,0:T(8,128)(2,1)}, bf16[1,416,384]{2,1,0:T(8,128)(2,1)}, u32[]{:S(2)}, u32[]{:S(2)}) collective-permute-start(bf16[1,416,384]{2,1,0:T(8,128)(2,1)} %get-tuple-element.1777), channel_id=1, source_target_pairs={{16,0},{24,8},{17,1},{25,9},{18,2},{26,10},{19,3},{27,11},{20,4},{... | collective-permute-start | bytes 958472 | tf_op jit(solution)/shard_map/ppermute | solution.py:20
  860.5 16.8 %collective-permute-start.9 = (bf16[1,416,384]{2,1,0:T(8,128)(2,1)}, bf16[1,416,384]{2,1,0:T(8,128)(2,1)}, u32[]{:S(2)}, u32[]{:S(2)}) collective-permute-start(bf16[1,416,384]{2,1,0:T(8,128)(2,1)} %get-tuple-element.1778), channel_id=1, source_target_pairs={{8,0},{16,8},{24,16},{9,1},{17,9},{25,17},{10,2},{18,10},{26,18},{... | collective-permute-start | bytes 958472 | tf_op jit(solution)/shard_map/ppermute | solution.py:20
  864.7 68.8 %collective-permute-start.23 = (bf16[1,416,384]{2,1,0:T(8,128)(2,1)}, bf16[1,416,384]{2,1,0:T(8,128)(2,1)S(1)}, u32[]{:S(2)}, u32[]{:S(2)}) collective-permute-start(bf16[1,416,384]{2,1,0:T(8,128)(2,1)} %get-tuple-element.1773), channel_id=1, source_target_pairs={{0,8},{8,16},{16,24},{1,9},{9,17},{17,25},{2,10},{10,18},{18,26},{... | collective-permute-start | bytes 958472 | tf_op jit(solution)/shard_map/ppermute | solution.py:20
  869.3 64.3 %collective-permute-start.22 = (bf16[1,416,384]{2,1,0:T(8,128)(2,1)}, bf16[1,416,384]{2,1,0:T(8,128)(2,1)S(1)}, u32[]{:S(2)}, u32[]{:S(2)}) collective-permute-start(bf16[1,416,384]{2,1,0:T(8,128)(2,1)} %get-tuple-element.1774), channel_id=1, source_target_pairs={{0,16},{8,24},{1,17},{9,25},{2,18},{10,26},{3,19},{11,27},{4,20},{... | collective-permute-start | bytes 958472 | tf_op jit(solution)/shard_map/ppermute | solution.py:20
  875.3 58.3 %collective-permute-start.21 = (bf16[1,416,384]{2,1,0:T(8,128)(2,1)}, bf16[1,416,384]{2,1,0:T(8,128)(2,1)}, u32[]{:S(2)}, u32[]{:S(2)}) collective-permute-start(bf16[1,416,384]{2,1,0:T(8,128)(2,1)} %get-tuple-element.1775), channel_id=1, source_target_pairs={{0,24},{1,25},{2,26},{3,27},{4,28},{5,29},{6,30},{7,31}} | collective-permute-start | bytes 958472 | tf_op jit(solution)/shard_map/ppermute | solution.py:20
  (61 other events, 197.6 us)
Sparse Core Ops, SparseCore 0:
  9.7 29.0 all-gather.3
  40.4 22.4 all-gather.5
  64.6 25.5 all-gather.7
  808.6 27.3 reduce-scatter.27
  838.2 28.4 reduce-scatter.31
  868.8 29.6 reduce-scatter.29
  900.9 31.0 reduce-scatter.33
  934.9 29.2 reduce-scatter.19
  967.3 33.1 reduce-scatter.17
  1003.3 34.2 reduce-scatter.21
  1040.6 35.3 reduce-scatter.23
  1078.8 43.0 reduce-scatter.25
where the time goes:
time: 1140 us; the launch traced here: 1130 us
  waiting for transfers between devices  445 us (39%)
  matrix products  257 us (23%)
  starting transfers between devices  115 us (10%)
  other arithmetic  98.7 us (9%)
  local copies, waits for them, and re-layouts  93.9 us (8%)
  blocking collectives  75 us (7%)
  loops' own time  25.6 us (2%)
  between operations  18.6 us (2%)
    ppermute x24, waiting for transfers between devices, shifted(): return lax.ppermute(array, axis, pairs)  207 us
    ppermute x24, starting transfers between devices, shifted(): return lax.ppermute(array, axis, pairs)  115 us
    dot_general x48, matrix products, head_probs(): jnp.einsum('qe,ke->qk', query, keys, preferred_element_type=jnp.float32)  62.9 us
    unnamed x16, waiting for transfers between devices  50.9 us
    dot_general x64, matrix products, contract_rows(): lax.dot_general(left, right, (((0,), (0,)), ((), ())), preferred_element_...  47.8 us
    reduce_scatter x1, waiting for transfers between devices, body(): lax.psum_scatter(t_ada[None], 'batch', scatter_dimension=1, tiled=True)  45.9 us
    unnamed x2, blocking collectives  42.7 us
    reduce_scatter x1, waiting for transfers between devices, body(): lax.psum_scatter(t_down[None], 'batch', scatter_dimension=1, tiled=True)  38.4 us
  transfers between devices with their start and end apart: 36, of which 19 were waited for; matrix products, arithmetic and copies ran while one was open for 15% of the time, Pallas kernels for 0%

commit v1 on v0

--- a/solution.py
+++ b/solution.py
@@ -180,138 +180,96 @@
     return (grad_inputs.astype(jnp.bfloat16), grads)
 
 
-def guarded(valid, work, blank):
-    return lax.cond(valid, work, blank)
+BOTH = ("section", "batch")
 
 
 def body(
     tokens, levels, lead, w_qkv, w_o, b_o, w_up, b_up, w_down, b_down, w_ada, b_ada, cotangent
 ):
-    section = lax.axis_index("section")
-    sections = lax.axis_size("section")
-    token_list = []
-    cotan_list = []
-    for anchor in range(sections):
-        if anchor == 0:
-            token_list.append(tokens)
-        else:
-            token_list.append(shifted(tokens, "section", -anchor))
-        if anchor == sections - 1:
-            cotan_list.append(cotangent)
-        else:
-            cotan_list.append(shifted(cotangent, "section", sections - 1 - anchor))
-    items = jnp.concatenate(token_list, 0)
-    cotangents = jnp.concatenate(cotan_list, 0)
-    level_all, lead_all = (
-        lax.all_gather(levels, "section", axis=0, tiled=True),
-        lax.all_gather(lead, "section", axis=0, tiled=True),
-    )
-    gathered = (
-        lax.all_gather(w_qkv, "batch", axis=1, tiled=True),
-        lax.all_gather(w_o, "batch", axis=1, tiled=True),
-        lax.all_gather(b_o, "batch", axis=1, tiled=True),
-        lax.all_gather(w_up, "batch", axis=1, tiled=True),
-        lax.all_gather(b_up, "batch", axis=1, tiled=True),
-        lax.all_gather(w_down, "batch", axis=1, tiled=True),
-        lax.all_gather(b_down, "batch", axis=1, tiled=True),
-        lax.all_gather(w_ada, "batch", axis=1, tiled=True),
-        lax.all_gather(b_ada, "batch", axis=1, tiled=True),
-    )
-    weights = tuple((piece[0] for piece in gathered))
-    micro, seq_len, width = items.shape
-    cond_all = jax.nn.silu(embed_lead(lead_all, width))
-    mods = jnp.dot(cond_all, weights[7].astype(jnp.float32), precision=HIGH) + weights[8].astype(
-        jnp.float32
-    )
+    batch = lax.axis_index("batch")
+    sections, batches = lax.axis_size("section"), lax.axis_size("batch")
+    width, seq_len = tokens.shape[2], tokens.shape[1]
+    rows = width // batches
+
+    def whole(piece):
+        full = lax.all_gather(piece, "batch", axis=1, tiled=True)
+        return lax.all_gather(full, "section", axis=0, tiled=True)
+
+    def blocks_of(piece):
+        return jnp.stack(jnp.split(piece, piece.shape[1] // width, axis=1))
+
+    shard = jnp.concatenate(
+        [
+            blocks_of(w_qkv[0]),
+            w_o,
+            blocks_of(w_up[0]),
+            w_down[0].reshape(4, rows, width),
+        ]
+    )
+    shards = lax.all_gather(shard, BOTH, axis=0, tiled=False)
+    shards = shards.reshape(sections, batches, 12, rows, width)
+    front = jnp.swapaxes(shards[:, :, :8], 1, 2).reshape(sections, 8, width, width)
+    downs = shards[:, :, 8:].reshape(sections, 4 * width, width)
+    small = jnp.concatenate([b_o[0], b_up[0], b_down[0]])
+    smalls = lax.all_gather(small, BOTH, axis=0, tiled=False).reshape(sections, batches, -1)
+    bias_o = smalls[:, :, :rows].reshape(sections, width)
+    bias_up = smalls[:, :, rows : 5 * rows].reshape(sections, 4 * width)
+    bias_down = smalls[:, :, 5 * rows :].reshape(sections, width)
+
+    leads = lax.all_gather(lead, BOTH, axis=0, tiled=True)
+    conds = jax.nn.silu(embed_lead(leads, width))
+    mine = lax.dynamic_slice_in_dim(conds, batch * rows, rows, axis=1)
+    part = jnp.dot(mine, w_ada[0].astype(jnp.float32), precision=HIGH)
+    bias = jnp.zeros((6 * width,), jnp.float32)
+    bias = lax.dynamic_update_slice_in_dim(
+        bias, b_ada[0].astype(jnp.float32), batch * 6 * rows, axis=0
+    )
+    part = (part + bias).reshape(sections, batches, 6 * width)
+    part = lax.psum_scatter(part, "batch", scatter_dimension=1, tiled=True)
+    mods = lax.all_to_all(part[:, 0], "section", 0, 0, tiled=True)
+
     patch = seq_len // LEVELS
-    key_table = (jnp.arange(seq_len) // patch)[None, :] < level_all[:, None]
-    slots = jnp.arange(micro)
-    ticks = micro + sections - 1
-    forward_weights = weights[:7]
-
-    def blank_act():
-        return jnp.zeros((seq_len, width), jnp.bfloat16)
-
-    receive = jnp.zeros((seq_len, width), jnp.bfloat16)
-    kept = jnp.zeros((micro, seq_len, width), jnp.bfloat16)
-    finals = jnp.zeros((micro, seq_len, width), jnp.bfloat16)
-    for tick in range(ticks):
-        index = tick - section
-        valid = (index >= 0) & (index < micro)
-        pick = jnp.clip(index, 0, micro - 1)
-        entering = jnp.where(section == 0, items[min(tick, micro - 1)], receive)
-        leaving = guarded(
-            valid,
-            lambda: layer_forward(entering, mods[pick], key_table[pick], forward_weights)[0].astype(
-                jnp.bfloat16
-            ),
-            blank_act,
+    key_ok = (jnp.arange(seq_len) // patch) < levels[0]
+    cond_row = jnp.zeros((1,), jnp.float32)
+
+    def weights_of(layer):
+        return (
+            jnp.concatenate([front[layer, 0], front[layer, 1], front[layer, 2]], axis=1),
+            front[layer, 3],
+            bias_o[layer],
+            jnp.concatenate([front[layer, 4 + j] for j in range(4)], axis=1),
+            bias_up[layer],
+            downs[layer],
+            bias_down[layer],
         )
-        hit = (valid & (slots == index))[:, None, None]
-        kept = jnp.where(hit, entering[None], kept)
-        finals = jnp.where(hit, leaving[None], finals)
-        if tick < ticks - 1:
-            receive = shifted(leaving, "section", 1)
-    totals = tuple((jnp.zeros(piece.shape, jnp.float32) for piece in weights))
-    shards = tuple(
-        (
-            jnp.zeros(piece.shape, jnp.float32)
-            for piece in (w_qkv, w_o, b_o, w_up, b_up, w_down, b_down, w_ada, b_ada)
+
+    value = tokens[0]
+    kept = []
+    for layer in range(sections):
+        kept.append(value)
+        value = layer_forward(value, mods[layer], key_ok, weights_of(layer))[0].astype(jnp.bfloat16)
+    result = value[None]
+    grad = cotangent[0]
+    all_grads = [None] * sections
+    for layer in reversed(range(sections)):
+        grad, all_grads[layer] = layer_backward(
+            kept[layer], grad, mods[layer], cond_row, key_ok, weights_of(layer)
         )
-    )
-
-    def blank_back():
-        return (
-            jnp.zeros((seq_len, width), jnp.bfloat16),
-            tuple((jnp.zeros(piece.shape, jnp.float32) for piece in weights)),
-        )
-
-    receive = jnp.zeros((seq_len, width), jnp.bfloat16)
-    input_grads = jnp.zeros((micro, seq_len, width), jnp.bfloat16)
-    for tick in range(ticks):
-        index = tick - (sections - 1 - section)
-        valid = (index >= 0) & (index < micro)
-        pick = jnp.clip(index, 0, micro - 1)
-        entering = jnp.where(section == sections - 1, cotangents[min(tick, micro - 1)], receive)
-        saved_in = kept[pick]
-        grad_in, grads = guarded(
-            valid,
-            lambda: layer_backward(
-                saved_in, entering, mods[pick], cond_all[pick], key_table[pick], forward_weights
-            ),
-            blank_back,
-        )
-        hit = (valid & (slots == index))[:, None, None]
-        input_grads = jnp.where(hit, grad_in[None], input_grads)
-        totals = tuple((left + right for left, right in zip(totals, grads)))
-        if tick < ticks - 1:
-            receive = shifted(grad_in, "section", -1)
-    t_qkv, t_o, t_bo, t_up, t_bup, t_down, t_bdown, t_ada, t_bada = totals
-    shards = (
-        lax.psum_scatter(t_qkv[None], "batch", scatter_dimension=1, tiled=True),
-        lax.psum_scatter(t_o[None], "batch", scatter_dimension=1, tiled=True),
-        lax.psum_scatter(t_bo[None], "batch", scatter_dimension=1, tiled=True),
-        lax.psum_scatter(t_up[None], "batch", scatter_dimension=1, tiled=True),
-        lax.psum_scatter(t_bup[None], "batch", scatter_dimension=1, tiled=True),
-        lax.psum_scatter(t_down[None], "batch", scatter_dimension=1, tiled=True),
-        lax.psum_scatter(t_bdown[None], "batch", scatter_dimension=1, tiled=True),
-        lax.psum_scatter(t_ada[None], "batch", scatter_dimension=1, tiled=True),
-        lax.psum_scatter(t_bada[None], "batch", scatter_dimension=1, tiled=True),
-    )
-    share = micro // sections
-    result = jnp.zeros((share, seq_len, width), jnp.bfloat16)
-    grad_tokens = jnp.zeros((share, seq_len, width), jnp.bfloat16)
-    for target in range(sections):
-        out_piece = finals[target * share : (target + 1) * share]
-        grad_piece = input_grads[target * share : (target + 1) * share]
-        if target != sections - 1:
-            out_piece = shifted(out_piece, "section", target - (sections - 1))
-        if target != 0:
-            grad_piece = shifted(grad_piece, "section", target)
-        result = jnp.where(section == target, out_piece, result)
-        grad_tokens = jnp.where(section == target, grad_piece, grad_tokens)
-    s_qkv, s_o, s_bo, s_up, s_bup, s_down, s_bdown, s_ada, s_bada = shards
-    return (result, grad_tokens, s_qkv, s_o, s_bo, s_up, s_bup, s_down, s_bdown, s_ada, s_bada)
+    outs = []
+    for k in range(7):
+        full = jnp.stack([grads[k] for grads in all_grads])
+        if full.ndim == 3:
+            full = full.astype(jnp.bfloat16)
+        total = lax.psum_scatter(full, "section", scatter_dimension=0, tiled=True)
+        total = lax.psum_scatter(total, "batch", scatter_dimension=1, tiled=True)
+        outs.append(total.astype(jnp.float32))
+    grad_mods = jnp.stack([grads[8] for grads in all_grads])
+    grad_mods = lax.all_to_all(grad_mods, "section", 0, 0, tiled=True)
+    every = lax.all_gather(grad_mods, "batch", axis=1, tiled=False)
+    every = every.reshape(sections * batches, 6 * width)
+    g_ada = jnp.dot(mine.T, every, precision=HIGH)[None]
+    g_bada = lax.dynamic_slice_in_dim(jnp.sum(every, 0), batch * 6 * rows, 6 * rows)[None]
+    return (result, grad[None], *outs, g_ada, g_bada)
 
 
 def solution(mesh):

time: 1140 us -> 753 us (0.66)
  matrix products: 257 us -> 120 us
  starting transfers between devices: 115 us -> 8.16 us
  other arithmetic: 98.7 us -> 33.5 us
  waiting for transfers between devices: 445 us -> 384 us
  blocking collectives: 75 us -> 115 us
  local copies, waits for them, and re-layouts: 93.9 us -> 66 us
  loops' own time: 25.6 us -> 0 us
    ppermute x24 -> x0, waiting for transfers between devices: 207 us -> none  [shifted(): return lax.ppermute(array, axis, pairs)]
    unnamed x16 -> x21, waiting for transfers between devices: 50.9 us -> 252 us
    ppermute x24 -> x0, starting transfers between devices: 115 us -> none  [shifted(): return lax.ppermute(array, axis, pairs)]
    reduce_scatter x5 -> x4, waiting for transfers between devices: 188 us -> 107 us  [body(): total = lax.psum_scatter(total, 'batch', scatter_dimension=1, tiled=True)]
    unnamed x2 -> x3, blocking collectives: 42.7 us -> 100 us
    dot_general x48 -> x24, matrix products: 62.9 us -> 8.89 us  [head_probs(): jnp.einsum('qe,ke->qk', query, keys, preferred_element_type=jnp.float32)]
    broadcast_in_dim x6 -> x1, other arithmetic: 38.7 us -> 1.03 us  [body(): return (result, grad[None], *outs, g_ada, g_bada)]
    another operation x34 -> x16, local copies, waits for them, and re-layouts: 31.2 us -> 0.08 us  [the longest x12 0.05 us: body(): full = jnp.stack([grads[k] for grads in all_grads])]
  transfers between devices with their start and end apart: 36 -> 15, of which waited for: 19 -> 13; matrix products, arithmetic and copies ran while one was open for 15% -> 8% of each run, Pallas kernels for 0% -> 0%
where the time goes in v1:
time: 753 us; the launch traced here: 748 us
  waiting for transfers between devices  384 us (51%)
  matrix products  120 us (16%)
  blocking collectives  115 us (15%)
  local copies, waits for them, and re-layouts  66 us (9%)
  other arithmetic  33.5 us (4%)
  between operations  21 us (3%)
  starting transfers between devices  8.16 us (1%)
    unnamed x21, waiting for transfers between devices  252 us
    reduce_scatter x4, waiting for transfers between devices, body(): total = lax.psum_scatter(total, 'batch', scatter_dimension=1, tiled=True)  107 us
    unnamed x3, blocking collectives  100 us
    unnamed x348, local copies, waits for them, and re-layouts  36.2 us
    dot_general x64, matrix products, contract_rows(): lax.dot_general(left, right, (((0,), (0,)), ((), ())), preferred_element_...  34.9 us
    dot_general x16, matrix products, contract_cols(): lax.dot_general(left, right, (((1,), (1,)), ((), ())), preferred_element_...  26 us
    all_gather x1, waiting for transfers between devices, body(): shards = lax.all_gather(shard, BOTH, axis=0, tiled=False)  21.5 us
    transpose x2, local copies, waits for them, and re-layouts, body(): jnp.swapaxes(shards[:, :, :8], 1, 2).reshape(sections, 8, width, width)  17.7 us
  transfers between devices with their start and end apart: 15, of which 13 were waited for; matrix products, arithmetic and copies ran while one was open for 8% of the time, Pallas kernels for 0%

profile of v1, /device:TPU:0, one launch (start us, length us, event | category | flops | bytes accessed | tf_op | source)
XLA Modules:
  0.0 748.0 jit_solution(12153756753524627169)
XLA Ops:
  9.2 42.0 %all-reduce = s32[32]{0:T(128)S(1)} all-reduce(s32[32]{0:T(128)S(1)} %dynamic-update-slice), channel_id=1, replica_groups=mesh['section'=4,'batch'=8] {'section','batch'}, use_global_device_ids=true, to_apply=%add | all-reduce | flops 32 | bytes 256
  58.0 41.0 %all-reduce.1 = bf16[9216]{0:T(1024)(128)(2,1)S(1)} all-reduce(bf16[9216]{0:T(1024)(128)(2,1)S(1)} %dynamic-update-slice.1), channel_id=3, replica_groups=mesh['section'=4,'batch'=8] {'section','batch'}, use_global_device_ids=true, to_apply=%add.1 | all-reduce | flops 9216 | bytes 36864
  100.3 29.5 %all-reduce.13.cloned.1.call-done = f32[4,8,2304]{2,0,1:T(4,128)} async-done(((f32[4,8,2304]{2,0,1:T(4,128)}), f32[4,8,2304]{2,0,1:T(4,128)}) %all-reduce.13.cloned.1.call-update) | async-done | bytes 294928
  131.9 3.9 all-to-all-start
  137.0 3.8 all-to-all-done
  141.5 21.5 %all-gather.4.cloned.1.call-done = bf16[384,48,384]{2,1,0:T(8,128)(2,1)} async-done(((bf16[12,48,384]{2,1,0:T(8,128)(2,1)}), bf16[384,48,384]{2,1,0:T(8,128)(2,1)}) %all-gather.4.cloned.1.call-update) | async-done | bytes 14155792 | tf_op jit(solution)/shard_map/all_gather | solution.py:209
  163.0 4.2 fusion.680
  167.2 8.8 %slice_bitcast_fusion = bf16[4,8,8,48,384]{4,3,1,2,0:T(8,128)(2,1)} fusion(bf16[4,8,12,48,384]{4,3,2,1,0:T(8,128)(2,1)} %bitcast.348), kind=kLoop, calls=%fused_computation | loop fusion | bytes 18874368 | tf_op jit(solution)/shard_map/transpose | solution.py:211
  176.0 8.9 %copy.30 = bf16[4,8,8,48,384]{4,3,2,1,0:T(8,128)(2,1)} copy(bf16[4,8,8,48,384]{4,3,1,2,0:T(8,128)(2,1)} %slice_bitcast_fusion) | data formatting | bytes 18874368 | tf_op jit(solution)/shard_map/transpose | solution.py:211
  184.9 2.0 slice_bitcast_fusion.28
  190.1 3.3 copy-done.2
  193.4 1.7 slice_bitcast_fusion.4
  202.9 1.4 convolution_convert_fusion.2
  229.5 2.4 convolution_add_fusion.1
  231.9 4.6 convert_reduce_fusion
  236.5 3.1 multiply_reduce_fusion.24
  239.7 3.9 fusion.279
  256.9 1.8 fusion.12
  260.6 2.8 convert_reduce_fusion.1
  276.0 1.8 fusion.11
  278.2 1.4 copy-done.147
  279.7 2.5 convert_reduce_fusion.2
  297.5 2.7 convert_reduce_fusion.3
  312.8 1.7 multiply_convert_fusion.9
  322.3 1.6 fusion.10
  328.5 2.0 pad_maximum_fusion.2
  331.6 2.3 fusion.4
  337.7 2.5 pad_maximum_fusion
  341.2 3.1 fusion.8
  349.3 2.6 pad_maximum_fusion.1
  353.3 17.3 %all-reduce.10 = (f32[4,384]{1,0:T(4,128)S(1)}, f32[4,1536]{1,0:T(4,128)S(1)}, f32[4,384]{1,0:T(4,128)S(1)}) all-reduce(f32[4,384]{1,0:T(4,128)S(1)} %pad_maximum_fusion.30, f32[4,1536]{1,0:T(4,128)S(1)} %pad_maximum_fusion.29, f32[4,384]{1,0:T(4,128)S(1)} %pad_maximum_fusion.31), channel_id=9, replica_groups=mesh['section'=4,'batch'=8] {'section'}, use_global_device_ids=true, to_apply=%region_113.114.clone | all-reduce | flops 9216 | bytes 73728
  376.4 15.5 %reduce-scatter.40.cloned.1.call-done = bf16[1,384,1152]{2,1,0:T(8,128)(2,1)} async-done(((bf16[4,384,1152]{2,1,0:T(8,128)(2,1)}), bf16[1,384,1152]{2,1,0:T(8,128)(2,1)}) %reduce-scatter.40.cloned.1.call-update) | async-done | bytes 884752
  392.0 60.2 %reduce-scatter.44.cloned.1.call-done = bf16[1,384,1536]{2,1,0:T(8,128)(2,1)} async-done(((bf16[4,384,1536]{2,1,0:T(8,128)(2,1)}), bf16[1,384,1536]{2,1,0:T(8,128)(2,1)}) %reduce-scatter.44.cloned.1.call-update) | async-done | bytes 1179664
  452.5 59.9 %reduce-scatter.46.cloned.1.call-done = bf16[1,1536,384]{2,1,0:T(8,128)(2,1)} async-done(((bf16[4,1536,384]{2,1,0:T(8,128)(2,1)}), bf16[1,1536,384]{2,1,0:T(8,128)(2,1)}) %reduce-scatter.46.cloned.1.call-update) | async-done | bytes 1179664
  512.5 2.4 fusion.276
  515.7 3.3 all-to-all-start.1
  520.1 25.4 %reduce-scatter.38.cloned.1.call-done = f32[48,1]{1,0:T(8,128)} async-done(((f32[384,1]{1,0:T(8,128)}), f32[48,1]{1,0:T(8,128)}) %reduce-scatter.38.cloned.1.call-update) | async-done | bytes 208
  546.8 30.0 %reduce-scatter.34.cloned.1.call-done = f32[48,1]{1,0:T(8,128)} async-done(((f32[384,1]{1,0:T(8,128)}), f32[48,1]{1,0:T(8,128)}) %reduce-scatter.34.cloned.1.call-update) | async-done | bytes 208
  578.1 30.9 %reduce-scatter.36.cloned.1.call-done = f32[192,1]{1,0:T(8,128)} async-done(((f32[1536,1]{1,0:T(8,128)}), f32[192,1]{1,0:T(8,128)}) %reduce-scatter.36.cloned.1.call-update) | async-done | bytes 784
  609.0 1.5 copy.36
  610.5 14.3 %all_gather.24 = f32[4,8,2304]{2,0,1:T(4,128)S(1)} all-gather(f32[4,1,2304]{2,0,1:T(4,128)S(1)} %copy.31), channel_id=1, replica_groups=mesh['section'=4,'batch'=8] {'batch'}, dimensions={1}, use_global_device_ids=true | all-gather | bytes 331776 | tf_op jit(solution)/shard_map/all_gather | solution.py:268
  626.9 13.0 %reduce-scatter.28.cloned.1.call-done = bf16[1,48,384]{2,1,0:T(8,128)(2,1)} async-done(((bf16[1,384,384]{2,1,0:T(8,128)(2,1)}), bf16[1,48,384]{2,1,0:T(8,128)(2,1)}) %reduce-scatter.28.cloned.1.call-update) | async-done | bytes 36880 | tf_op jit(solution)/shard_map/reduce_scatter | solution.py:264
  641.3 30.9 %reduce-scatter.26.cloned.1.call-done = bf16[1,48,1152]{2,1,0:T(8,128)(2,1)} async-done(((bf16[1,384,1152]{2,1,0:T(8,128)(2,1)}), bf16[1,48,1152]{2,1,0:T(8,128)(2,1)}) %reduce-scatter.26.cloned.1.call-update) | async-done | bytes 110608 | tf_op jit(solution)/shard_map/reduce_scatter | solution.py:264
  672.2 1.6 convert_element_type.697
  673.8 31.5 %reduce-scatter.30.cloned.1.call-done = bf16[1,48,1536]{2,1,0:T(8,128)(2,1)} async-done(((bf16[1,384,1536]{2,1,0:T(8,128)(2,1)}), bf16[1,48,1536]{2,1,0:T(8,128)(2,1)}) %reduce-scatter.30.cloned.1.call-update) | async-done | bytes 147472 | tf_op jit(solution)/shard_map/reduce_scatter | solution.py:264
  705.3 1.6 convert_element_type.703
  706.9 31.6 %reduce-scatter.32.cloned.1.call-done = bf16[1,192,384]{2,1,0:T(8,128)(2,1)} async-done(((bf16[1,1536,384]{2,1,0:T(8,128)(2,1)}), bf16[1,192,384]{2,1,0:T(8,128)(2,1)}) %reduce-scatter.32.cloned.1.call-update) | async-done | bytes 147472 | tf_op jit(solution)/shard_map/reduce_scatter | solution.py:264
  738.5 1.6 convert_element_type.709
  (717 shorter events, 139.6 us)
Async XLA Ops:
  8.0 44.4 %copy-start = (bf16[1,48,2304]{2,1,0:T(8,128)(2,1)S(1)}, bf16[1,48,2304]{2,1,0:T(8,128)(2,1)}, u32[]{:S(2)}) copy-start(bf16[1,48,2304]{2,1,0:T(8,128)(2,1)} %param.23) | copy-start | bytes 663556
  8.0 91.1 %copy-start.136 = (u32[32]{0:T(128)S(1)}, u32[32]{0:T(128)}, u32[]{:S(2)}) copy-start(u32[32]{0:T(128)} %constant.128) | copy-start | bytes 388
  8.0 48.0 %copy-start.87 = (bf16[1,48,384]{2,1,0:T(8,128)(2,1)S(1)}, bf16[1,48,384]{2,1,0:T(8,128)(2,1)}, u32[]{:S(2)}) copy-start(bf16[1,48,384]{2,1,0:T(8,128)(2,1)} %param.17) | copy-start | bytes 110596
  8.1 48.0 %copy-start.85 = (bf16[1,48,1536]{2,1,0:T(8,128)(2,1)S(1)}, bf16[1,48,1536]{2,1,0:T(8,128)(2,1)}, u32[]{:S(2)}) copy-start(bf16[1,48,1536]{2,1,0:T(8,128)(2,1)} %param.19) | copy-start | bytes 442372
  8.1 48.1 %copy-start.86 = (bf16[1,192,384]{2,1,0:T(8,128)(2,1)S(1)}, bf16[1,192,384]{2,1,0:T(8,128)(2,1)}, u32[]{:S(2)}) copy-start(bf16[1,192,384]{2,1,0:T(8,128)(2,1)} %param.21) | copy-start | bytes 442372
  8.1 49.5 %copy-start.126 = (bf16[1,192]{1,0:T(2,128)(2,1)S(1)}, bf16[1,192]{1,0:T(2,128)(2,1)}, u32[]{:S(2)}) copy-start(bf16[1,192]{1,0:T(2,128)(2,1)} %param.20) | copy-start | bytes 1156
  8.1 49.6 %copy-start.127 = (bf16[1,48]{1,0:T(2,128)(2,1)S(1)}, bf16[1,48]{1,0:T(2,128)(2,1)}, u32[]{:S(2)}) copy-start(bf16[1,48]{1,0:T(2,128)(2,1)} %param.22) | copy-start | bytes 292
  8.1 49.6 %copy-start.128 = (bf16[1,48]{1,0:T(2,128)(2,1)S(1)}, bf16[1,48]{1,0:T(2,128)(2,1)}, u32[]{:S(2)}) copy-start(bf16[1,48]{1,0:T(2,128)(2,1)} %param.18) | copy-start | bytes 292
  8.1 91.6 %copy-start.27 = (bf16[1,416,384]{2,1,0:T(8,128)(2,1)S(1)}, bf16[1,416,384]{2,1,0:T(8,128)(2,1)}, u32[]{:S(2)}) copy-start(bf16[1,416,384]{2,1,0:T(8,128)(2,1)} %param.13) | copy-start | bytes 958468
  8.1 121.7 %all-reduce.13.cloned.1.call-start = ((), (), s32[]{:S(2)}) async-start(), calls=%async_computation.21 | async-start | bytes 589824
  53.6 109.3 %all-gather.4.cloned.1.call-start = ((), (), s32[]{:S(2)}) async-start(), calls=%async_computation.17 | async-start | bytes 14598144 | tf_op jit(solution)/shard_map/all_gather | solution.py:209
  99.9 87.2 %copy-start.100 = (f32[416]{0:T(512)}, f32[416]{0:T(512)S(1)}, u32[]{:S(2)}) copy-start(f32[416]{0:T(512)S(1)} %broadcast_multiply_fusion.23) | copy-start | bytes 4996
  100.1 86.9 %copy-start.116 = (f32[416]{0:T(512)}, f32[416]{0:T(512)S(1)}, u32[]{:S(2)}) copy-start(f32[416]{0:T(512)S(1)} %add_rsqrt_fusion.7) | copy-start | bytes 4996
  131.9 8.9 %all-to-all-start = ((f32[4,1,2304]{2,1,0:T(1,128)}), f32[4,1,2304]{2,1,0:T(1,128)S(1)}, u32[]{:S(2)}, u32[]{:S(2)}) async-start(f32[4,1,2304]{2,1,0:T(1,128)} %copy.29), calls=%async_computation | async-start | bytes 73728 | tf_op jit(solution)/shard_map/all_to_all | solution.py:229
  135.9 239.8 %reduce-scatter.42.cloned.1.call-start = ((), (), s32[]{:S(2)}) async-start(), calls=%async_computation.23 | async-start | bytes 1474560
  141.5 45.5 %copy-start.118 = (f32[384]{0:T(512)}, f32[384]{0:T(512)S(1)}, u32[]{:S(2)}) copy-start(f32[384]{0:T(512)S(1)} %get-tuple-element.290) | copy-start | bytes 4612
  141.5 45.6 %copy-start.124 = (f32[384]{0:T(512)}, f32[384]{0:T(512)S(1)}, u32[]{:S(2)}) copy-start(f32[384]{0:T(512)S(1)} %get-tuple-element.291) | copy-start | bytes 4612
  141.5 57.1 %copy-start.102 = (f32[384]{0:T(512)}, f32[384]{0:T(512)S(1)}, u32[]{:S(2)}) copy-start(f32[384]{0:T(512)S(1)} %get-tuple-element.289) | copy-start | bytes 4612
  141.5 58.7 %copy-start.120 = (f32[384]{0:T(512)}, f32[384]{0:T(512)S(1)}, u32[]{:S(2)}) copy-start(f32[384]{0:T(512)S(1)} %get-tuple-element.293) | copy-start | bytes 4612
  141.5 69.0 %copy-start.122 = (f32[384]{0:T(512)}, f32[384]{0:T(512)S(1)}, u32[]{:S(2)}) copy-start(f32[384]{0:T(512)S(1)} %get-tuple-element.64) | copy-start | bytes 4612
  186.9 13.2 %copy-start.73 = (bf16[384,384]{1,0:T(8,128)(2,1)}, bf16[384,384]{1,0:T(8,128)(2,1)S(1)}, u32[]{:S(2)}) copy-start(bf16[384,384]{1,0:T(8,128)(2,1)S(1)} %get-tuple-element.134) | copy-start | bytes 884740
  187.0 13.2 %copy-start.75 = (bf16[384,384]{1,0:T(8,128)(2,1)}, bf16[384,384]{1,0:T(8,128)(2,1)S(1)}, u32[]{:S(2)}) copy-start(bf16[384,384]{1,0:T(8,128)(2,1)S(1)} %get-tuple-element.137) | copy-start | bytes 884740
  187.0 13.2 %copy-start.77 = (bf16[384,384]{1,0:T(8,128)(2,1)}, bf16[384,384]{1,0:T(8,128)(2,1)S(1)}, u32[]{:S(2)}) copy-start(bf16[384,384]{1,0:T(8,128)(2,1)S(1)} %get-tuple-element.138) | copy-start | bytes 884740
  187.0 13.2 %copy-start.79 = (bf16[384,384]{1,0:T(8,128)(2,1)}, bf16[384,384]{1,0:T(8,128)(2,1)S(1)}, u32[]{:S(2)}) copy-start(bf16[384,384]{1,0:T(8,128)(2,1)S(1)} %get-tuple-element.139) | copy-start | bytes 884740
  187.0 15.9 %copy-start.81 = (bf16[384,384]{1,0:T(8,128)(2,1)}, bf16[384,384]{1,0:T(8,128)(2,1)S(1)}, u32[]{:S(2)}) copy-start(bf16[384,384]{1,0:T(8,128)(2,1)S(1)} %get-tuple-element.135) | copy-start | bytes 884740
  187.0 15.9 %copy-start.83 = (bf16[384,384]{1,0:T(8,128)(2,1)}, bf16[384,384]{1,0:T(8,128)(2,1)S(1)}, u32[]{:S(2)}) copy-start(bf16[384,384]{1,0:T(8,128)(2,1)S(1)} %get-tuple-element.136) | copy-start | bytes 884740
  195.0 27.5 %copy-start.55 = (bf16[384,384]{1,0:T(8,128)(2,1)}, bf16[384,384]{1,0:T(8,128)(2,1)S(1)}, u32[]{:S(2)}) copy-start(bf16[384,384]{1,0:T(8,128)(2,1)S(1)} %get-tuple-element.120) | copy-start | bytes 884740
  195.0 27.5 %copy-start.57 = (bf16[384,384]{1,0:T(8,128)(2,1)}, bf16[384,384]{1,0:T(8,128)(2,1)S(1)}, u32[]{:S(2)}) copy-start(bf16[384,384]{1,0:T(8,128)(2,1)S(1)} %get-tuple-element.121) | copy-start | bytes 884740
  202.6 93.0 %copy-start.29 = (bf16[416,384]{1,0:T(8,128)(2,1)}, bf16[416,384]{1,0:T(8,128)(2,1)S(1)}, u32[]{:S(2)}) copy-start(bf16[416,384]{1,0:T(8,128)(2,1)S(1)} %get-tuple-element.108) | copy-start | bytes 958468
  210.2 73.1 %copy-start.21 = (f32[416,384]{1,0:T(8,128)}, f32[416,384]{1,0:T(8,128)S(1)}, u32[]{:S(2)}) copy-start(f32[416,384]{1,0:T(8,128)S(1)} %get-tuple-element.106) | copy-start | bytes 1916932
  219.5 45.0 %copy-start.23 = (f32[416,384]{1,0:T(8,128)}, f32[416,384]{1,0:T(8,128)S(1)}, u32[]{:S(2)}) copy-start(f32[416,384]{1,0:T(8,128)S(1)} %get-tuple-element.102) | copy-start | bytes 1916932
  312.8 79.2 %reduce-scatter.40.cloned.1.call-start = ((), (), s32[]{:S(2)}) async-start(), calls=%async_computation.22 | async-start | bytes 4423680
  330.5 121.6 %reduce-scatter.44.cloned.1.call-start = ((), (), s32[]{:S(2)}) async-start(), calls=%async_computation.24 | async-start | bytes 5898240
  340.2 172.2 %reduce-scatter.46.cloned.1.call-start = ((), (), s32[]{:S(2)}) async-start(), calls=%async_computation.25 | async-start | bytes 5898240
  351.9 193.6 %reduce-scatter.38.cloned.1.call-start = ((), (), s32[]{:S(2)}) async-start(), calls=%async_computation.20 | async-start | bytes 221184
  372.1 204.6 %reduce-scatter.34.cloned.1.call-start = ((), (), s32[]{:S(2)}) async-start(), calls=%async_computation.18 | async-start | bytes 221184
  373.7 235.3 %reduce-scatter.36.cloned.1.call-start = ((), (), s32[]{:S(2)}) async-start(), calls=%async_computation.19 | async-start | bytes 884736
  375.6 264.3 %reduce-scatter.28.cloned.1.call-start = ((), (), s32[]{:S(2)}) async-start(), calls=%async_computation.14 | async-start | bytes 331776 | tf_op jit(solution)/shard_map/reduce_scatter | solution.py:264
  376.3 136.1 %copy-start.68 = (bf16[384,384]{1,0:T(8,128)(2,1)S(1)}, bf16[384,384]{1,0:T(8,128)(2,1)}, u32[]{:S(2)}) copy-start(bf16[384,384]{1,0:T(8,128)(2,1)} %copy-done.67) | copy-start | bytes 884740
  376.3 136.1 %copy-start.70 = (bf16[384,384]{1,0:T(8,128)(2,1)S(1)}, bf16[384,384]{1,0:T(8,128)(2,1)}, u32[]{:S(2)}) copy-start(bf16[384,384]{1,0:T(8,128)(2,1)} %copy-done.69) | copy-start | bytes 884740
  376.3 136.1 %copy-start.72 = (bf16[384,384]{1,0:T(8,128)(2,1)S(1)}, bf16[384,384]{1,0:T(8,128)(2,1)}, u32[]{:S(2)}) copy-start(bf16[384,384]{1,0:T(8,128)(2,1)} %copy-done.71) | copy-start | bytes 884740
  376.4 295.9 %reduce-scatter.26.cloned.1.call-start = ((), (), s32[]{:S(2)}) async-start(), calls=%async_computation.13 | async-start | bytes 995328 | tf_op jit(solution)/shard_map/reduce_scatter | solution.py:264
  392.0 313.3 %reduce-scatter.30.cloned.1.call-start = ((), (), s32[]{:S(2)}) async-start(), calls=%async_computation.15 | async-start | bytes 1327104 | tf_op jit(solution)/shard_map/reduce_scatter | solution.py:264
  452.2 286.3 %reduce-scatter.32.cloned.1.call-start = ((), (), s32[]{:S(2)}) async-start(), calls=%async_computation.16 | async-start | bytes 1327104 | tf_op jit(solution)/shard_map/reduce_scatter | solution.py:264
  514.9 110.6 %copy-start.64 = (f32[32,192]{1,0:T(8,128)S(1)}, f32[32,192]{1,0:T(8,128)}, u32[]{:S(2)}) copy-start(f32[32,192]{1,0:T(8,128)} %copy-done.63) | copy-start | bytes 73732
  514.9 110.6 %copy-start.66 = (f32[32,192]{1,0:T(8,128)S(1)}, f32[32,192]{1,0:T(8,128)}, u32[]{:S(2)}) copy-start(f32[32,192]{1,0:T(8,128)} %copy-done.65) | copy-start | bytes 73732
  515.7 94.8 %all-to-all-start.1 = ((f32[4,1,2304]{2,1,0:T(1,128)}), f32[4,1,2304]{2,1,0:T(1,128)S(1)}, u32[]{:S(2)}, u32[]{:S(2)}) async-start(f32[4,1,2304]{2,1,0:T(1,128)} %all_to_all.11), calls=%async_computation.5 | async-start | bytes 73728 | tf_op jit(solution)/shard_map/all_to_all | solution.py:267
  519.0 221.1 %copy-start.1 = (bf16[1,48,2304]{2,1,0:T(8,128)(2,1)S(1)}, bf16[1,48,2304]{2,1,0:T(8,128)(2,1)}, u32[]{:S(2)}) copy-start(bf16[1,48,2304]{2,1,0:T(8,128)(2,1)} %param.23) | copy-start | bytes 663556
  (119 other events, 292.8 us)
Sparse Core Ops, SparseCore 0:
  53.7 76.0 all-reduce.12
  312.9 26.8 reduce-scatter.41
  343.2 48.7 reduce-scatter.39
  395.1 57.0 reduce-scatter.43
  455.3 57.0 reduce-scatter.45
  515.2 30.2 reduce-scatter.37
  548.3 28.4 reduce-scatter.33
  579.1 29.8 reduce-scatter.35
  611.2 28.6 reduce-scatter.27
  642.2 29.9 reduce-scatter.25
  674.5 30.7 reduce-scatter.29
  707.4 31.0 reduce-scatter.31
Sparse Core Ops, SparseCore 1:
  58.1 104.8 all-gather.3

commit v2 on v1

v2 whole, which is shorter than its diff:
```python
import functools
import math

import jax
import jax.numpy as jnp
from jax import lax
from jax.experimental import pallas as pl
from jax.experimental.pallas import tpu as pltpu
from jax.sharding import PartitionSpec as P

HEADS = 6
LEVELS = 13
BLOCKS = 12
SHARDS = 8
EPS = 1e-06
NEG = -1e30
BF = jnp.bfloat16
F32 = jnp.float32
HIGH = lax.Precision.HIGHEST
C0 = math.sqrt(2.0 / math.pi)
C1 = 0.044715
VMEM_LIMIT = 60 * 2**20


def dot(left, right, over=(1, 0)):
    return lax.dot_general(
        left, right, (((over[0],), (over[1],)), ((), ())), preferred_element_type=F32
    )


def standard(value):
    centered = value - jnp.mean(value, -1, keepdims=True)
    rstd = lax.rsqrt(jnp.mean(centered * centered, -1, keepdims=True) + EPS)
    return centered * rstd, rstd


def standard_back(grad, normed, rstd):
    return rstd * (
        grad
        - jnp.mean(grad, -1, keepdims=True)
        - normed * jnp.mean(grad * normed, -1, keepdims=True)
    )


def forward_kernel(plan, ids, tokens, mods, biases, *refs):
    count = len({part[0] for parts in plan.values() for part in parts})
    sources, refs = refs[:count], refs[count:]
    result, w_out, xs, qkv, probs, mixed, branch_a, act, slope, branch_b = refs[:10]
    value, hidden, acc, w, in_sem, out_sem = refs[10:]
    layer = pl.program_id(0)
    layers = pl.num_programs(0)
    seq, width = value.shape
    size = width // HEADS
    section, place, core = ids[0], ids[1], ids[2]

    @pl.when(layer == 0)
    def _():
        value[...] = tokens[0]

        @pl.loop(0, layers)
        def _(target):
            for away in range(4):

                @pl.when(jnp.bitwise_xor(section, target) == away)
                def _():
                    for (sx, zx, cx), parts in plan.items():
                        if sx != away:
                            continue
                        shard = 2 * jnp.bitwise_xor(place, zx) + jnp.bitwise_xor(core, cx)
                        for index, lead, low, high in parts:
                            ref = sources[index]
                            top = min(high, 8)
                            if low < top:
                                pltpu.make_async_copy(
                                    ref.at[pl.ds(lead, top - low)],
                                    w.at[target, pl.ds(low, top - low), shard],
                                    in_sem.at[target],
                                ).start()
                            if high > 8:
                                pltpu.make_async_copy(
                                    ref.at[pl.ds(lead + 8 - low, 4)],
                                    w.at[target, 8 + shard // 2, pl.ds(4 * (shard % 2), 4)],
                                    in_sem.at[target],
                                ).start()

    pltpu.make_async_copy(w.at[layer], w.at[layer], in_sem.at[layer]).wait()
    pltpu.make_async_copy(w.at[layer], w_out.at[layer], out_sem.at[layer]).start()

    def weight(j):
        return w[layer, j].reshape(width, width)

    here = jnp.bitwise_xor(section, layer)
    mod = mods[here]
    bias = biases[here]
    xs[0] = value[...]
    x = value[...].astype(F32)
    normed, _ = standard(x)
    hidden[...] = (normed * (1.0 + mod[1:2]) + mod[0:1]).astype(BF)
    for j in range(3):
        qkv[0, :, j * width : (j + 1) * width] = dot(hidden[...], weight(j)).astype(BF)
    limit = ids[3] * (seq // LEVELS)
    row = lax.broadcasted_iota(jnp.int32, (seq, 1), 0)
    mask = jnp.where(row < limit, 0.0, NEG)
    for h in range(HEADS):
        q = qkv[0, :, h * size : (h + 1) * size] * (size**-0.5)
        k = qkv[0, :, width + h * size : width + (h + 1) * size]
        v = qkv[0, :, 2 * width + h * size : 2 * width + (h + 1) * size]
        raw = dot(k, q, (1, 1)) + mask
        top = jnp.max(raw, axis=0, keepdims=True)
        e = jnp.exp(raw - top)
        p = (e * (1.0 / jnp.sum(e, axis=0, keepdims=True))).astype(BF)
        probs[0, h] = p
        mixed[0, h * size : (h + 1) * size, :] = dot(v, p, (0, 0)).astype(BF)
    ba = dot(mixed[0], weight(3), (0, 0)) + bias[0:1]
    branch_a[0] = ba
    middle = value[...].astype(F32) + mod[2:3] * ba
    acc[...] = middle
    normed, _ = standard(middle)
    hidden[...] = (normed * (1.0 + mod[4:5]) + mod[3:4]).astype(BF)
    down = None
    for j in range(4):
        cols = slice(j * width, (j + 1) * width)
        pre = dot(hidden[...], weight(4 + j)) + bias[1 + j : 2 + j]
        square = pre * pre
        t = jnp.tanh(pre * (C0 + (C0 * C1) * square))
        half = 0.5 + 0.5 * t
        a = pre * half
        slope[0, :, cols] = (half + a * (1.0 - t) * (C0 + (3.0 * C0 * C1) * square)).astype(BF)
        act[0, :, cols] = a.astype(BF)
        part = dot(act[0, :, cols], weight(8 + j))
        down = part if down is None else down + part
    bb = down + bias[5:6]
    branch_b[0] = bb.astype(BF)
    out = (acc[...] + mod[5:6] * bb).astype(BF)
    value[...] = out
    result[0] = out

    @pl.when(layer == layers - 1)
    def _():
        @pl.loop(0, layers)
        def _(target):
            pltpu.make_async_copy(w.at[target], w_out.at[target], out_sem.at[target]).wait()


def forward(plan, sources, ids, tokens, mods, biases):
    layers = mods.shape[0]
    _, seq, width = tokens.shape
    rows = width // SHARDS

    def per_layer(*shape):
        return pl.BlockSpec((1,) + shape, lambda l: (l,) + (0,) * len(shape))

    def same(*shape):
        return pl.BlockSpec(shape, lambda l: (0,) * len(shape))

    shapes = [
        ((seq, width), BF),
        ((seq, 3 * width), BF),
        ((HEADS, seq, seq), BF),
        ((width, seq), BF),
        ((seq, width), F32),
        ((seq, 4 * width), BF),
        ((seq, 4 * width), BF),
        ((seq, width), BF),
    ]
    hbm = pl.BlockSpec(memory_space=pl.ANY)
    return pl.pallas_call(
        functools.partial(forward_kernel, plan),
        grid=(layers,),
        in_specs=[
            pl.BlockSpec(memory_space=pltpu.SMEM),
            same(1, seq, width),
            same(layers, 6, width),
            same(layers, 6, width),
        ]
        + [hbm] * len(sources),
        out_specs=[same(1, seq, width), hbm] + [per_layer(*s) for s, _ in shapes],
        out_shape=[
            jax.ShapeDtypeStruct((1, seq, width), BF),
            jax.ShapeDtypeStruct((layers, BLOCKS, SHARDS, rows, width), BF),
        ]
        + [jax.ShapeDtypeStruct((layers,) + s, d) for s, d in shapes],
        scratch_shapes=[
            pltpu.VMEM((seq, width), BF),
            pltpu.VMEM((seq, width), BF),
            pltpu.VMEM((seq, width), F32),
            pltpu.VMEM((layers, BLOCKS, SHARDS, rows, width), BF),
            pltpu.SemaphoreType.DMA((layers,)),
            pltpu.SemaphoreType.DMA((layers,)),
        ],
        compiler_params=pltpu.CompilerParams(vmem_limit_bytes=VMEM_LIMIT),
        cost_estimate=pl.CostEstimate(
            flops=layers * 1_740_000_000, bytes_accessed=80_000_000, transcendentals=0
        ),
        name="forward",
    )(ids, tokens, mods, biases, *sources)


def backward_kernel(
    layer, ids, grad, mods, w, xs, qkv, probs, mixed, branch_a, act, slope, branch_b,
    grad_in, kept, sent, vec, gbb, hid, gsum, gmix, gqkv, dqt, halves, sems,
):
    seq, width = gbb.shape
    size = width // HEADS
    section, place, core = ids[0], ids[1], ids[2]
    rows = width // SHARDS

    def weight(j):
        return w[0, j].reshape(width, width)

    def keep(shard, block, value):
        half = jnp.bitwise_xor(core, shard % 2)
        halves[half, jnp.bitwise_xor(place, shard // 2), block] = value

    def keep_front(block, value):
        for shard in range(SHARDS):
            keep(shard, block, value[shard * rows : (shard + 1) * rows])

    def keep_down(j, value):
        for part in range(SHARDS):
            keep(2 * j + part // 4, 8 + part % 4, value[part * rows : (part + 1) * rows])

    mod = mods[jnp.bitwise_xor(section, layer)]
    shift_a, scale_a, gate_a, shift_b, scale_b, gate_b = (mod[i : i + 1] for i in range(6))
    gout = grad[0].astype(F32)
    vec[5:6] = jnp.sum(gout * branch_b[0].astype(F32), 0, keepdims=True)
    gb = (gout * gate_b).astype(BF)
    gbb[...] = gb
    vec[11:12] = jnp.sum(gb.astype(F32), 0, keepdims=True)
    x = xs[0].astype(F32)
    middle = x + gate_a * branch_a[0]
    normed_b, rstd_b = standard(middle)
    hid[...] = (normed_b * (1.0 + scale_b) + shift_b).astype(BF)
    total = None
    for j in range(4):
        cols = slice(j * width, (j + 1) * width)
        keep_down(j, dot(act[0, :, cols], gbb[...], (0, 0)).astype(BF))
        gact = dot(gbb[...], weight(8 + j), (1, 1))
        gpre = (gact * slope[0, :, cols].astype(F32)).astype(BF)
        vec[7 + j : 8 + j] = jnp.sum(gpre.astype(F32), 0, keepdims=True)
        keep_front(4 + j, dot(hid[...], gpre, (0, 0)).astype(BF))
        part = dot(gpre, weight(4 + j), (1, 1))
        total = part if total is None else total + part
    ghb = total
    vec[3:4] = jnp.sum(ghb, 0, keepdims=True)
    vec[4:5] = jnp.sum(ghb * normed_b, 0, keepdims=True)
    gmid = gout + standard_back(ghb * (1.0 + scale_b), normed_b, rstd_b)
    gsum[...] = gmid
    vec[2:3] = jnp.sum(gmid * branch_a[0], 0, keepdims=True)
    gba = (gmid * gate_a).astype(BF)
    gbb[...] = gba
    vec[6:7] = jnp.sum(gba.astype(F32), 0, keepdims=True)
    keep_front(3, dot(mixed[0], gbb[...]).astype(BF))
    gmix[...] = dot(gbb[...], weight(3), (1, 1)).astype(BF)
    factor = size ** -0.5
    for h in range(HEADS):
        q = qkv[0, :, h * size : (h + 1) * size]
        k = qkv[0, :, width + h * size : width + (h + 1) * size]
        v = qkv[0, :, 2 * width + h * size : 2 * width + (h + 1) * size]
        g = gmix[:, h * size : (h + 1) * size]
        p = probs[0, h]
        pf = p.astype(F32)
        dp = dot(v, g, (1, 1))
        inner = jnp.sum(dp * pf, axis=0, keepdims=True)
        ds = (pf * (dp - inner) * factor).astype(BF)
        gqkv[:, 2 * width + h * size : 2 * width + (h + 1) * size] = dot(p, g).astype(BF)
        gqkv[:, width + h * size : width + (h + 1) * size] = dot(ds, q).astype(BF)
        dqt[h * size : (h + 1) * size, :] = dot(k, ds, (0, 0)).astype(BF)
    gqkv[:, :width] = dqt[...].T
    normed_a, rstd_a = standard(xs[0].astype(F32))
    hid[...] = (normed_a * (1.0 + scale_a) + shift_a).astype(BF)
    total = None
    for j in range(3):
        cols = slice(j * width, (j + 1) * width)
        keep_front(j, dot(hid[...], gqkv[:, cols], (0, 0)).astype(BF))
        part = dot(gqkv[:, cols], weight(j), (1, 1))
        total = part if total is None else total + part
    gha = total
    copies = [
        pltpu.make_async_copy(halves.at[1], sent, sems.at[1]),
        pltpu.make_async_copy(halves.at[0], kept, sems.at[0]),
    ]
    for copy in copies:
        copy.start()
    vec[0:1] = jnp.sum(gha, 0, keepdims=True)
    vec[1:2] = jnp.sum(gha * normed_a, 0, keepdims=True)
    grad_in[0] = (gsum[...] + standard_back(gha * (1.0 + scale_a), normed_a, rstd_a)).astype(BF)
    for copy in copies:
        copy.wait()


def backward(layer, ids, grad, mods, w, saved):
    _, seq, width = grad.shape
    rows = width // SHARDS

    def at_layer(a):
        return pl.BlockSpec((1,) + a.shape[1:], lambda i: (layer,) + (0,) * (a.ndim - 1))

    def full(*shape):
        return pl.BlockSpec(shape, lambda i: (0,) * len(shape))

    half = (SHARDS // 2, BLOCKS, rows, width)
    hbm = pl.BlockSpec(memory_space=pl.ANY)
    return pl.pallas_call(
        functools.partial(backward_kernel, layer),
        grid=(1,),
        in_specs=[pl.BlockSpec(memory_space=pltpu.SMEM), full(1, seq, width), full(*mods.shape), at_layer(w)]
        + [at_layer(a) for a in saved],
        out_specs=[full(1, seq, width), hbm, hbm, full(12, width)],
        out_shape=[
            jax.ShapeDtypeStruct((1, seq, width), BF),
            jax.ShapeDtypeStruct(half, BF),
            jax.ShapeDtypeStruct(half, BF),
            jax.ShapeDtypeStruct((12, width), F32),
        ],
        scratch_shapes=[
            pltpu.VMEM((seq, width), BF),
            pltpu.VMEM((seq, width), BF),
            pltpu.VMEM((seq, width), F32),
            pltpu.VMEM((seq, width), BF),
            pltpu.VMEM((seq, 3 * width), BF),
            pltpu.VMEM((width, seq), BF),
            pltpu.VMEM((2,) + half, BF),
            pltpu.SemaphoreType.DMA((2,)),
        ],
        compiler_params=pltpu.CompilerParams(vmem_limit_bytes=VMEM_LIMIT),
        cost_estimate=pl.CostEstimate(
            flops=3_480_000_000, bytes_accessed=20_000_000, transcendentals=0
        ),
        name=f"backward_{layer}",
    )(ids, grad, mods, w, *saved)


def embed_lead(steps, width):
    half = width // 2
    freq = jnp.exp(-math.log(10000.0) * jnp.arange(half, dtype=F32) / half)
    angle = 6.0 * steps.astype(F32)[:, None] * freq[None, :]
    return jnp.concatenate([jnp.sin(angle), jnp.cos(angle)], -1)


def over_core(value):
    return lax.ppermute(value, "batch", [(i, i ^ 1) for i in range(8)])


def over_z(value, away):
    return lax.ppermute(value, "batch", [(i, i ^ (2 * away)) for i in range(8)])


def over_section(value, away):
    return lax.ppermute(value, "section", [(i, i ^ away) for i in range(4)])


def after(value, *others):
    return lax.optimization_barrier((value,) + others)[0]


def gather_shards(w):
    x0, y0, z1 = over_section(w, 1), over_section(w, 2), over_z(w, 1)
    z2 = over_z(w, 2)
    x1, y1 = over_section(z1, 1), over_section(z1, 2)
    z3 = over_z(after(w, z1), 3)
    p0 = over_section(after(y0, z1)[:6], 1)
    q0 = over_section(after(x0, z1)[6:], 2)
    x2, y2 = over_section(after(z2, x1), 1), over_section(after(z2, y1), 2)
    p1, q1 = over_section(y1[:6], 1), over_section(x1[6:], 2)
    x3, y3 = over_section(after(z3, x2), 1), over_section(after(z3, y2), 2)
    p2, q2 = over_section(y2[:6], 1), over_section(x2[6:], 2)
    p3, q3 = over_section(y3[:6], 1), over_section(x3[6:], 2)
    names = {}
    for zx, group in enumerate(
        [(w, x0, y0, p0, q0), (z1, x1, y1, p1, q1), (z2, x2, y2, p2, q2), (z3, x3, y3, p3, q3)]
    ):
        names[0, zx], names[1, zx], names[2, zx] = [(group[0], 0)], [(group[1], 0)], [(group[2], 0)]
        names[3, zx] = [(group[3], 0), (group[4], 6)]
    sources, plan = [], {}
    for keys in (
        [(0, 0), (0, 1), (1, 0), (2, 0), (1, 1), (2, 1), (3, 0)],
        [(0, 2), (0, 3), (3, 1), (1, 2), (2, 2)],
        [(1, 3), (2, 3), (3, 2), (3, 3)],
    ):
        bundle = []
        for key in keys:
            plan[key + (0,)], plan[key + (1,)] = [], []
            for array, low in names[key]:
                plan[key + (0,)].append((len(sources), low, 0))
                sources.append(array)
                bundle.append((key, array, low))
        other = over_core(jnp.concatenate([array for _, array, _ in bundle]))
        start = 0
        for key, array, low in bundle:
            plan[key + (1,)].append((len(sources), low, start))
            start += array.shape[0]
        sources.append(other)
    sizes = {}
    final = {}
    for key, parts in plan.items():
        final[key] = []
        for index, low, start in parts:
            high = BLOCKS if key[0] != 3 else low + 6
            final[key].append((index, start, low, high))
    return final, sources


def sum_shards(parts):
    def add(*values):
        total = values[0].astype(F32)
        for value in values[1:]:
            total = total + value.astype(F32)
        return total

    stage = None
    received = []
    own = None
    p, q = {}, {}

    def corners(zx, gate):
        p[zx] = over_section(after(parts[3, zx][:6], *gate), 1)
        q[zx] = over_section(after(parts[3, zx][6:], *gate), 2)

    corners(3, ())
    corners(2, ())
    gate = ()
    for zx in (3, 2, 1, 0):
        left = parts[1, zx]
        left = jnp.concatenate([left[:6], add(left[6:], q[zx]).astype(BF)])
        right = parts[2, zx]
        right = jnp.concatenate([add(right[:6], p[zx]).astype(BF), right[6:]])
        x, y = over_section(after(left, *gate), 1), over_section(after(right, *gate), 2)
        if zx >= 2:
            corners(zx - 2, (p[zx], q[zx]) + gate)
        total = add(parts[0, zx], x, y)
        gate = (x, y)
        if zx:
            received.append(over_z(total.astype(BF), zx))
        else:
            own = total
    return add(own, *received)


def gather_small(row):
    cores = jnp.stack([row, over_core(row)])
    places = jnp.stack([cores] + [over_z(cores, i) for i in (1, 2, 3)])
    return jnp.stack([places] + [over_section(places, i) for i in (1, 2, 3)])


def body_permuted(
    tokens, levels, lead, w_qkv, w_o, b_o, w_up, b_up, w_down, b_down, w_ada, b_ada, cotangent
):
    section, batch = lax.axis_index("section"), lax.axis_index("batch")
    place, core = batch // 2, batch % 2
    width = tokens.shape[2]
    rows = width // SHARDS
    ids = jnp.stack([section, place, core, levels[0]]).astype(jnp.int32)
    plan, sources = gather_shards(local_shard(w_qkv, w_o, w_up, w_down))

    small = jnp.concatenate([b_o[0], b_up[0], b_down[0], lead.astype(BF)])
    small = jnp.pad(small, (0, width - small.shape[0]))
    smalls = gather_small(small)
    leads = smalls[..., 6 * rows].reshape(-1)
    order = jnp.arange(SHARDS) ^ batch
    smalls = jnp.take(smalls.reshape(4, SHARDS, width), order, axis=1).astype(F32)
    biases = jnp.stack(
        [smalls[:, :, :rows].reshape(4, width)]
        + [
            smalls[:, 2 * j : 2 * j + 2, rows : 5 * rows].reshape(4, width)
            for j in range(4)
        ]
        + [smalls[:, :, 5 * rows : 6 * rows].reshape(4, width)],
        axis=1,
    )
    conds = jax.nn.silu(embed_lead(leads, width))
    mine = lax.dynamic_slice_in_dim(conds, batch * rows, rows, axis=1)
    part = jnp.dot(mine, w_ada[0].astype(F32), precision=HIGH)
    bias = jnp.zeros((6 * width,), F32)
    bias = lax.dynamic_update_slice_in_dim(
        bias, b_ada[0].astype(F32), batch * 6 * rows, axis=0
    )
    part = (part + bias).reshape(4, 4, 2, 6 * width)
    part = part[:, :, 0] + over_core(part[:, :, 1])
    part = part[:, 0] + over_z(part[:, 1], 1) + over_z(part[:, 2], 2) + over_z(part[:, 3], 3)
    mods = jnp.stack([part[0]] + [over_section(part[i], i) for i in (1, 2, 3)])
    mods = mods.reshape(4, 6, width)

    result, w, *saved = forward(plan, sources, ids, tokens, mods, biases)
    grad = cotangent
    sums = jnp.zeros((4, 4, BLOCKS, rows, width), BF)
    vecs = [None] * 4
    for layer in reversed(range(4)):
        grad, kept, sent, vecs[layer] = backward(layer, ids, grad, mods, w, saved)
        both = (kept.astype(F32) + over_core(sent).astype(F32)).astype(BF)
        sums = lax.dynamic_update_index_in_dim(sums, both, section ^ layer, 0)
    total = sum_shards({(i, j): sums[i, j] for i in range(4) for j in range(4)})

    vec = jnp.take(jnp.stack(vecs), jnp.arange(4) ^ section, axis=0)
    vec = jnp.stack([vec[0]] + [over_section(vec[i], i) for i in (1, 2, 3)])
    vec = jnp.stack([vec] + [over_z(vec, i) for i in (1, 2, 3)], axis=1)
    vec = jnp.stack([vec, over_core(vec)], axis=2).reshape(32, 12, width)
    g_ada = jnp.dot(mine.T, vec[:, :6].reshape(32, 6 * width), precision=HIGH)[None]
    flat = jnp.sum(vec, 0)

    def slot(low, high, count):
        return lax.dynamic_slice_in_dim(
            flat[low:high].reshape(-1), batch * count, count, axis=0
        )[None]

    return (
        result,
        grad,
        jnp.concatenate([total[0], total[1], total[2]], axis=1)[None],
        total[3][None],
        slot(6, 7, rows),
        jnp.concatenate([total[4 + j] for j in range(4)], axis=1)[None],
        slot(7, 11, 4 * rows),
        total[8:].reshape(1, 4 * rows, width),
        slot(11, 12, rows),
        g_ada,
        slot(0, 6, 6 * rows),
    )


def local_shard(w_qkv, w_o, w_up, w_down):
    _, rows, width = w_o.shape

    def blocks_of(piece):
        return jnp.stack(jnp.split(piece, piece.shape[1] // width, axis=1))

    return jnp.concatenate(
        [blocks_of(w_qkv[0]), w_o, blocks_of(w_up[0]), w_down[0].reshape(4, rows, width)]
    )


BOTH = ("section", "batch")


def body_general(
    tokens, levels, lead, w_qkv, w_o, b_o, w_up, b_up, w_down, b_down, w_ada, b_ada, cotangent
):
    batch = lax.axis_index("batch")
    sections, batches = lax.axis_size("section"), lax.axis_size("batch")
    width = tokens.shape[2]
    rows, tall = width // batches, width // SHARDS
    zero = jnp.zeros((), jnp.int32)
    ids = jnp.stack([zero, zero, zero, levels[0]])

    shards = lax.all_gather(local_shard(w_qkv, w_o, w_up, w_down), BOTH, axis=0, tiled=False)
    shards = shards.reshape(sections, batches, BLOCKS, rows, width)
    front = jnp.swapaxes(shards[:, :, :8], 1, 2).reshape(sections, 8, SHARDS, tall, width)
    downs = shards[:, :, 8:].reshape(sections, SHARDS, 4, tall, width)
    source = jnp.concatenate([jnp.swapaxes(front, 1, 2), downs], axis=2)
    source = source.reshape(sections * SHARDS * BLOCKS, tall, width)
    plan = {
        (l, z, c): [(0, ((l * 4 + z) * 2 + c) * BLOCKS, 0, BLOCKS)]
        for l in range(4)
        for z in range(4)
        for c in range(2)
    }
    small = jnp.concatenate([b_o[0], b_up[0], b_down[0]])
    smalls = lax.all_gather(small, BOTH, axis=0, tiled=False).reshape(sections, batches, -1)
    smalls = smalls.astype(F32)
    biases = jnp.concatenate(
        [
            smalls[:, :, :rows].reshape(sections, 1, width),
            smalls[:, :, rows : 5 * rows].reshape(sections, 4, width),
            smalls[:, :, 5 * rows :].reshape(sections, 1, width),
        ],
        axis=1,
    )
    leads = lax.all_gather(lead, BOTH, axis=0, tiled=True)
    conds = jax.nn.silu(embed_lead(leads, width))
    mine = lax.dynamic_slice_in_dim(conds, batch * rows, rows, axis=1)
    part = jnp.dot(mine, w_ada[0].astype(F32), precision=HIGH)
    bias = jnp.zeros((6 * width,), F32)
    bias = lax.dynamic_update_slice_in_dim(
        bias, b_ada[0].astype(F32), batch * 6 * rows, axis=0
    )
    part = (part + bias).reshape(sections, batches, 6 * width)
    part = lax.psum_scatter(part, "batch", scatter_dimension=1, tiled=True)
    mods = lax.all_to_all(part[:, 0], "section", 0, 0, tiled=True)
    mods = mods.reshape(sections, 6, width)

    result, w, *saved = forward(plan, [source], ids, tokens, mods, biases)
    grad = cotangent
    grads, vecs = [None] * sections, [None] * sections
    for layer in reversed(range(sections)):
        grad, kept, sent, vecs[layer] = backward(layer, ids, grad, mods, w, saved)
        grads[layer] = jnp.stack([kept, sent], axis=1).reshape(SHARDS, BLOCKS, tall, width)
    grads = jnp.stack(grads)
    front = jnp.swapaxes(grads[:, :, :8], 1, 2).reshape(sections, 8, batches, rows, width)
    downs = grads[:, :, 8:].reshape(sections, batches, 4, rows, width)
    total = jnp.concatenate([jnp.swapaxes(front, 1, 2), downs], axis=2)
    total = total.reshape(sections, batches, BLOCKS * rows, width)
    total = lax.psum_scatter(total, "section", scatter_dimension=0, tiled=True)
    total = lax.psum_scatter(total, "batch", scatter_dimension=1, tiled=True)
    total = total.astype(F32).reshape(BLOCKS, rows, width)

    vec = lax.all_to_all(jnp.stack(vecs), "section", 0, 0, tiled=True)
    vec = lax.all_gather(vec, "batch", axis=1, tiled=False)
    vec = vec.reshape(sections * batches, 12, width)
    g_ada = jnp.dot(mine.T, vec[:, :6].reshape(-1, 6 * width), precision=HIGH)[None]
    flat = jnp.sum(vec, 0)

    def slot(low, high, count):
        return lax.dynamic_slice_in_dim(
            flat[low:high].reshape(-1), batch * count, count, axis=0
        )[None]

    return (
        result,
        grad,
        jnp.concatenate([total[0], total[1], total[2]], axis=1)[None],
        total[3][None],
        slot(6, 7, rows),
        jnp.concatenate([total[4 + j] for j in range(4)], axis=1)[None],
        slot(7, 11, 4 * rows),
        total[8:].reshape(1, 4 * rows, width),
        slot(11, 12, rows),
        g_ada,
        slot(0, 6, 6 * rows),
    )


def solution(mesh):
    in_specs = (
        P(("section", "batch"), None, None),
        P(("section", "batch")),
        P(("section", "batch")),
        P("section", "batch", None),
        P("section", "batch", None),
        P("section", "batch"),
        P("section", "batch", None),
        P("section", "batch"),
        P("section", "batch", None),
        P("section", "batch"),
        P("section", "batch", None),
        P("section", "batch"),
        P(("section", "batch"), None, None),
    )
    out_specs = (
        P(("section", "batch"), None, None),
        P(("section", "batch"), None, None),
        P("section", "batch", None),
        P("section", "batch", None),
        P("section", "batch"),
        P("section", "batch", None),
        P("section", "batch"),
        P("section", "batch", None),
        P("section", "batch"),
        P("section", "batch", None),
        P("section", "batch"),
    )
    permuted = mesh.shape["section"] == 4 and mesh.shape["batch"] == SHARDS
    body = body_permuted if permuted else body_general
    return jax.shard_map(body, mesh=mesh, in_specs=in_specs, out_specs=out_specs, check_vma=False)
```

time: 753 us -> 364 us (0.48)
  the two profiles are of different devices: /device:TPU:0 before, /device:TPU:8 now
where the time goes in v2:
time: 364 us; the launch traced here: 358 us
  waiting for transfers between devices  126 us (35%)
  Pallas kernels  101 us (28%)
  starting transfers between devices  65.6 us (18%)
  local copies, waits for them, and re-layouts  40.6 us (11%)
  other arithmetic  20.4 us (6%)
    pallas_call x4, Pallas kernels, backward(): pl.pallas_call(functools.partial(backward_kernel, layer), grid=(1,), in_s...  64.8 us
    ppermute x15, waiting for transfers between devices, over_z(): return lax.ppermute(value, 'batch', [(i, i ^ 2 * away) for i in range(8)])  63 us
    ppermute x41, waiting for transfers between devices, over_section(): return lax.ppermute(value, 'section', [(i, i ^ away) for i in range(4)])  62.9 us
    ppermute x41, starting transfers between devices, over_section(): return lax.ppermute(value, 'section', [(i, i ^ away) for i in range(4)])  43.2 us
    pallas_call x1, Pallas kernels, forward(): pl.pallas_call(functools.partial(forward_kernel, plan), grid=(layers,), i...  36 us
    unnamed x96, local copies, waits for them, and re-layouts  29 us
    ppermute x15, starting transfers between devices, over_z(): return lax.ppermute(value, 'batch', [(i, i ^ 2 * away) for i in range(8)])  21 us
    dynamic_update_slice x4, other arithmetic, body_permuted(): sums = lax.dynamic_update_index_in_dim(sums, both, section ^ layer, 0)  7.32 us
  transfers between devices with their start and end apart: 66, of which 29 were waited for; matrix products, arithmetic and copies ran while one was open for 11% of the time, Pallas kernels for 14%

profile of v2, /device:TPU:8, one launch (start us, length us, event | category | flops | bytes accessed | tf_op | source)
XLA Modules:
  0.0 358.5 jit_solution(5871221399743496410)
XLA Ops:
  0.7 1.4 constant_dynamic-update-slice_fusion.28
  11.9 1.6 constant_dynamic-update-slice_fusion.20
  13.6 1.9 collective-permute-start.15
  19.4 2.8 collective-permute-start.3
  23.7 3.0 collective-permute-done.2
  27.0 2.3 collective-permute-start.6
  31.6 1.5 collective-permute-start.16
  33.1 1.7 collective-permute-start.22
  38.8 2.8 collective-permute-done.16.refs_3_
  41.7 1.8 collective-permute-start.23
  44.2 1.5 collective-permute-start.18
  48.1 14.9 %collective-permute-done.22.refs_9_ = bf16[12,48,384]{2,1,0:T(8,128)(2,1)} collective-permute-done((bf16[12,48,384]{2,1,0:T(8,128)(2,1)}, bf16[12,48,384]{2,1,0:T(8,128)(2,1)}, u32[]{:S(2)}, u32[]{:S(2)}) %collective-permute-start.22) | collective-permute-done | bytes 442400 | tf_op jit(solution)/shard_map/ppermute | solution.py:346
  63.7 1.8 constant_dynamic-update-slice_fusion.34
  69.1 4.4 %collective-permute-done.23.refs_10_ = bf16[12,48,384]{2,1,0:T(8,128)(2,1)S(1)} collective-permute-done((bf16[12,48,384]{2,1,0:T(8,128)(2,1)}, bf16[12,48,384]{2,1,0:T(8,128)(2,1)S(1)}, u32[]{:S(2)}, u32[]{:S(2)}) %collective-permute-start.23) | collective-permute-done | bytes 442400 | tf_op jit(solution)/shard_map/ppermute | solution.py:346
  76.9 4.9 %collective-permute-done.20.refs_7_ = bf16[6,48,384]{2,1,0:T(8,128)(2,1)S(1)} collective-permute-done((bf16[6,48,384]{2,1,0:T(8,128)(2,1)S(1)}, bf16[6,48,384]{2,1,0:T(8,128)(2,1)S(1)}, u32[]{:S(2)}, u32[]{:S(2)}) %collective-permute-start.20) | collective-permute-done | bytes 221216 | tf_op jit(solution)/shard_map/ppermute | solution.py:350
  84.5 1.5 collective-permute-start.30
  86.7 1.9 collective-permute-done.25.refs_12_
  91.7 5.7 %collective-permute-done.30.refs_17_ = bf16[12,48,384]{2,1,0:T(8,128)(2,1)S(1)} collective-permute-done((bf16[12,48,384]{2,1,0:T(8,128)(2,1)S(1)}, bf16[12,48,384]{2,1,0:T(8,128)(2,1)S(1)}, u32[]{:S(2)}, u32[]{:S(2)}) %collective-permute-start.30) | collective-permute-done | bytes 442400 | tf_op jit(solution)/shard_map/ppermute | solution.py:350
  97.4 1.7 collective-permute-start.31
  101.4 2.8 collective-permute-done.31.refs_18_
  107.9 2.2 collective-permute-done.33.refs_20_
  112.7 3.7 %collective-permute-start.9 = (f32[4,2304]{1,0:T(4,128)S(1)}, f32[4,2304]{1,0:T(4,128)S(1)}, u32[]{:S(2)}, u32[]{:S(2)}) collective-permute-start(f32[4,2304]{1,0:T(4,128)S(1)} %get-tuple-element.152), channel_id=1, source_target_pairs={{0,4},{1,5},{2,6},{3,7},{4,0},{5,1},{6,2},{7,3},{8,12},{9,13},{10,... | collective-permute-start | bytes 110600 | tf_op jit(solution)/shard_map/ppermute | solution.py:346
  116.4 2.1 collective-permute-done.9
  118.5 1.8 collective-permute-done.8
  126.5 2.3 collective-permute-done.13
  129.5 36.0 %forward.1 = (bf16[1,416,384]{2,1,0:T(8,128)(2,1)}, bf16[4,12,8,48,384]{4,3,2,1,0:T(8,128)(2,1)}, bf16[4,416,384]{2,1,0:T(8,128)(2,1)}, bf16[4,416,1152]{2,1,0:T...) custom-call(s32[4]{0:T(128)} %pad_add_fusion.ids, ...), custom_call_target="tpu_custom_call" | custom-call | flops 6960000000 | bytes 80000000 | tf_op jit(solution)/shard_map/forward/pallas_call | solution.py:167
  165.4 16.1 %backward_3.1 = (bf16[1,416,384]{2,1,0:T(8,128)(2,1)}, bf16[4,12,48,384]{3,2,1,0:T(8,128)(2,1)}, bf16[4,12,48,384]{3,2,1,0:T(8,128)(2,1)}, f32[12,384]{1,0:T(8,128)}) custom-call(s32[4]{0:T(128)} %pad_add_fusion.ids, bf16[1,416,384]{2,1,0:T(8,128)(2,1)} %grad.1, f32[4,6,384]{2,1,0:T(8,128)} %copy-done.15, bf16[4,12,8,48,384]{4,3,2,1,0:T(8,128)(2,1)} %get-tuple-element.62.w, ...), custom_call_target="tpu_custom_call" | custom-call | flops 3480000000 | bytes 20000000 | tf_op jit(solution)/shard_map/backward_3/pallas_call | solution.py:304
  181.6 16.3 %backward_2.1 = (bf16[1,416,384]{2,1,0:T(8,128)(2,1)}, bf16[4,12,48,384]{3,2,1,0:T(8,128)(2,1)}, bf16[4,12,48,384]{3,2,1,0:T(8,128)(2,1)}, f32[12,384]{1,0:T(8,128)}) custom-call(s32[4]{0:T(128)} %pad_add_fusion.ids, bf16[1,416,384]{2,1,0:T(8,128)(2,1)} %get-tuple-element.71.grad, f32[4,6,384]{2,1,0:T(8,128)} %copy-done.15, ...), custom_call_target="tpu_custom_call" | custom-call | flops 3480000000 | bytes 20000000 | tf_op jit(solution)/shard_map/backward_2/pallas_call | solution.py:304
  198.5 16.3 %backward_1.1 = (bf16[1,416,384]{2,1,0:T(8,128)(2,1)}, bf16[4,12,48,384]{3,2,1,0:T(8,128)(2,1)}, bf16[4,12,48,384]{3,2,1,0:T(8,128)(2,1)}, f32[12,384]{1,0:T(8,128)}) custom-call(s32[4]{0:T(128)} %pad_add_fusion.ids, bf16[1,416,384]{2,1,0:T(8,128)(2,1)} %get-tuple-element.72.grad, f32[4,6,384]{2,1,0:T(8,128)} %copy-done.15, ...), custom_call_target="tpu_custom_call" | custom-call | flops 3480000000 | bytes 20000000 | tf_op jit(solution)/shard_map/backward_1/pallas_call | solution.py:304
  214.9 16.1 %backward_0.1 = (bf16[1,416,384]{2,1,0:T(8,128)(2,1)}, bf16[4,12,48,384]{3,2,1,0:T(8,128)(2,1)}, bf16[4,12,48,384]{3,2,1,0:T(8,128)(2,1)}, f32[12,384]{1,0:T(8,128)}) custom-call(s32[4]{0:T(128)} %pad_add_fusion.ids, bf16[1,416,384]{2,1,0:T(8,128)(2,1)} %get-tuple-element.73.grad, f32[4,6,384]{2,1,0:T(8,128)} %copy-done.15, ...), custom_call_target="tpu_custom_call" | custom-call | flops 3480000000 | bytes 20000000 | tf_op jit(solution)/shard_map/backward_0/pallas_call | solution.py:304
  235.9 2.2 fusion.3
  238.1 2.3 fusion.5
  240.4 2.2 fusion.7
  245.9 5.4 %collective-permute-done.44 = bf16[6,48,384]{2,1,0:T(8,128)(2,1)S(1)} collective-permute-done((bf16[6,48,384]{2,1,0:T(8,128)(2,1)S(1)}, bf16[6,48,384]{2,1,0:T(8,128)(2,1)S(1)}, u32[]{:S(2)}, u32[]{:S(2)}) %collective-permute-start.44) | collective-permute-done | bytes 221216 | tf_op jit(solution)/shard_map/ppermute | solution.py:350
  253.5 1.7 collective-permute-start.61
  256.0 9.3 %collective-permute-done.61 = f32[12,384]{1,0:T(8,128)S(1)} collective-permute-done((f32[12,384]{1,0:T(8,128)S(1)}, f32[12,384]{1,0:T(8,128)S(1)}, u32[]{:S(2)}, u32[]{:S(2)}) %collective-permute-start.61) | collective-permute-done | bytes 18464 | tf_op jit(solution)/shard_map/ppermute | solution.py:350
  267.5 2.9 collective-permute-done.59
  271.3 2.4 collective-permute-start.63
  278.9 1.6 collective-permute-start.62
  280.5 3.0 collective-permute-done.62
  288.7 9.8 %collective-permute-done.48 = bf16[12,48,384]{2,1,0:T(8,128)(2,1)} collective-permute-done((bf16[12,48,384]{2,1,0:T(8,128)(2,1)}, bf16[12,48,384]{2,1,0:T(8,128)(2,1)}, u32[]{:S(2)}, u32[]{:S(2)}) %collective-permute-start.48) | collective-permute-done | bytes 442400 | tf_op jit(solution)/shard_map/ppermute | solution.py:350
  303.1 7.8 %collective-permute-done.52 = bf16[12,48,384]{2,1,0:T(8,128)(2,1)} collective-permute-done((bf16[12,48,384]{2,1,0:T(8,128)(2,1)}, bf16[12,48,384]{2,1,0:T(8,128)(2,1)}, u32[]{:S(2)}, u32[]{:S(2)}) %collective-permute-start.52) | collective-permute-done | bytes 442400 | tf_op jit(solution)/shard_map/ppermute | solution.py:350
  311.4 2.4 fusion.13
  313.8 1.5 collective-permute-start.58
  315.3 1.6 collective-permute-start.57
  321.5 9.5 %collective-permute-done.58 = bf16[12,48,384]{2,1,0:T(8,128)(2,1)S(1)} collective-permute-done((bf16[12,48,384]{2,1,0:T(8,128)(2,1)S(1)}, bf16[12,48,384]{2,1,0:T(8,128)(2,1)S(1)}, u32[]{:S(2)}, u32[]{:S(2)}) %collective-permute-start.58) | collective-permute-done | bytes 442400 | tf_op jit(solution)/shard_map/ppermute | solution.py:346
  331.0 15.4 %collective-permute-done.57 = bf16[12,48,384]{2,1,0:T(8,128)(2,1)S(1)} collective-permute-done((bf16[12,48,384]{2,1,0:T(8,128)(2,1)S(1)}, bf16[12,48,384]{2,1,0:T(8,128)(2,1)S(1)}, u32[]{:S(2)}, u32[]{:S(2)}) %collective-permute-start.57) | collective-permute-done | bytes 442400 | tf_op jit(solution)/shard_map/ppermute | solution.py:346
  346.4 7.4 %collective-permute-done.56 = bf16[12,48,384]{2,1,0:T(8,128)(2,1)S(1)} collective-permute-done((bf16[12,48,384]{2,1,0:T(8,128)(2,1)S(1)}, bf16[12,48,384]{2,1,0:T(8,128)(2,1)S(1)}, u32[]{:S(2)}, u32[]{:S(2)}) %collective-permute-start.56) | collective-permute-done | bytes 442400 | tf_op jit(solution)/shard_map/ppermute | solution.py:346
  (296 shorter events, 91.8 us)
Async XLA Ops:
  13.6 25.3 %collective-permute-start.14 = (bf16[12,48,384]{2,1,0:T(8,128)(2,1)}, bf16[12,48,384]{2,1,0:T(8,128)(2,1)S(1)}, u32[]{:S(2)}, u32[]{:S(2)}) collective-permute-start(bf16[12,48,384]{2,1,0:T(8,128)(2,1)} %get-tuple-element.56.refs_0_), channel_id=1, source_target_pairs={{0,2},{1,3},{2,0},{3,1},{4,6},{5,7},{6,4},{7,5},{8,10},{9,11},{10,... | collective-permute-start | bytes 1327112 | tf_op jit(solution)/shard_map/ppermute | solution.py:346
  13.6 28.1 %collective-permute-start.15 = (bf16[12,48,384]{2,1,0:T(8,128)(2,1)}, bf16[12,48,384]{2,1,0:T(8,128)(2,1)S(1)}, u32[]{:S(2)}, u32[]{:S(2)}) collective-permute-start(bf16[12,48,384]{2,1,0:T(8,128)(2,1)} %get-tuple-element.56.refs_0_), channel_id=1, source_target_pairs={{0,8},{8,0},{16,24},{24,16},{1,9},{9,1},{17,25},{25,17},{2,10},{10... | collective-permute-start | bytes 1327112 | tf_op jit(solution)/shard_map/ppermute | solution.py:350
  31.6 10.0 %collective-permute-start.16 = (bf16[12,48,384]{2,1,0:T(8,128)(2,1)}, bf16[12,48,384]{2,1,0:T(8,128)(2,1)S(1)}, u32[]{:S(2)}, u32[]{:S(2)}) collective-permute-start(bf16[12,48,384]{2,1,0:T(8,128)(2,1)} %get-tuple-element.56.refs_0_), channel_id=1, source_target_pairs={{0,16},{8,24},{16,0},{24,8},{1,17},{9,25},{17,1},{25,9},{2,18},{10... | collective-permute-start | bytes 1327112 | tf_op jit(solution)/shard_map/ppermute | solution.py:350
  33.1 29.9 %collective-permute-start.22 = (bf16[12,48,384]{2,1,0:T(8,128)(2,1)}, bf16[12,48,384]{2,1,0:T(8,128)(2,1)}, u32[]{:S(2)}, u32[]{:S(2)}) collective-permute-start(bf16[12,48,384]{2,1,0:T(8,128)(2,1)} %get-tuple-element.56.refs_0_), channel_id=1, source_target_pairs={{0,4},{1,5},{2,6},{3,7},{4,0},{5,1},{6,2},{7,3},{8,12},{9,13},{10,... | collective-permute-start | bytes 1327112 | tf_op jit(solution)/shard_map/ppermute | solution.py:346
  37.7 78.7 %collective-permute-start.10 = (f32[4,2304]{1,0:T(4,128)S(1)}, f32[4,2304]{1,0:T(4,128)S(1)}, u32[]{:S(2)}, u32[]{:S(2)}) collective-permute-start(f32[4,2304]{1,0:T(4,128)S(1)} %get-tuple-element.151), channel_id=1, source_target_pairs={{0,6},{1,7},{2,4},{3,5},{4,2},{5,3},{6,0},{7,1},{8,14},{9,15},{10,... | collective-permute-start | bytes 110600 | tf_op jit(solution)/shard_map/ppermute | solution.py:346
  41.7 31.8 %collective-permute-start.23 = (bf16[12,48,384]{2,1,0:T(8,128)(2,1)}, bf16[12,48,384]{2,1,0:T(8,128)(2,1)S(1)}, u32[]{:S(2)}, u32[]{:S(2)}) collective-permute-start(bf16[12,48,384]{2,1,0:T(8,128)(2,1)} %get-tuple-element.56.refs_0_), channel_id=1, source_target_pairs={{0,6},{1,7},{2,4},{3,5},{4,2},{5,3},{6,0},{7,1},{8,14},{9,15},{10,... | collective-permute-start | bytes 1327112 | tf_op jit(solution)/shard_map/ppermute | solution.py:346
  43.5 22.0 %collective-permute-start.17 = (bf16[12,48,384]{2,1,0:T(8,128)(2,1)S(1)}, bf16[12,48,384]{2,1,0:T(8,128)(2,1)S(1)}, u32[]{:S(2)}, u32[]{:S(2)}) collective-permute-start(bf16[12,48,384]{2,1,0:T(8,128)(2,1)S(1)} %collective-permute-done.14.refs_1_), channel_id=1, source_target_pairs={{0,8},{8,0},{16,24},{24,16},{1,9},{9,1},{17,25},{25,17},{2,10},{10... | collective-permute-start | bytes 1327112 | tf_op jit(solution)/shard_map/ppermute | solution.py:350
  44.2 22.7 %collective-permute-start.18 = (bf16[12,48,384]{2,1,0:T(8,128)(2,1)S(1)}, bf16[12,48,384]{2,1,0:T(8,128)(2,1)S(1)}, u32[]{:S(2)}, u32[]{:S(2)}) collective-permute-start(bf16[12,48,384]{2,1,0:T(8,128)(2,1)S(1)} %collective-permute-done.14.refs_1_), channel_id=1, source_target_pairs={{0,16},{8,24},{16,0},{24,8},{1,17},{9,25},{17,1},{25,9},{2,18},{10... | collective-permute-start | bytes 1327112 | tf_op jit(solution)/shard_map/ppermute | solution.py:350
  63.1 11.8 %collective-permute-start.19 = (bf16[6,48,384]{2,1,0:T(8,128)(2,1)S(1)}, bf16[6,48,384]{2,1,0:T(8,128)(2,1)S(1)}, u32[]{:S(2)}, u32[]{:S(2)}) collective-permute-start(bf16[6,48,384]{2,1,0:T(8,128)(2,1)S(1)} %slice.322), channel_id=1, source_target_pairs={{0,8},{8,0},{16,24},{24,16},{1,9},{9,1},{17,25},{25,17},{2,10},{10... | collective-permute-start | bytes 663560 | tf_op jit(solution)/shard_map/ppermute | solution.py:350
  65.5 17.5 %collective-permute-start.26 = (bf16[12,48,384]{2,1,0:T(8,128)(2,1)}, bf16[12,48,384]{2,1,0:T(8,128)(2,1)S(1)}, u32[]{:S(2)}, u32[]{:S(2)}) collective-permute-start(bf16[12,48,384]{2,1,0:T(8,128)(2,1)} %collective-permute-done.22.refs_9_), channel_id=1, source_target_pairs={{0,8},{8,0},{16,24},{24,16},{1,9},{9,1},{17,25},{25,17},{2,10},{10... | collective-permute-start | bytes 1327112 | tf_op jit(solution)/shard_map/ppermute | solution.py:350
  66.9 16.1 %collective-permute-start.27 = (bf16[12,48,384]{2,1,0:T(8,128)(2,1)}, bf16[12,48,384]{2,1,0:T(8,128)(2,1)S(1)}, u32[]{:S(2)}, u32[]{:S(2)}) collective-permute-start(bf16[12,48,384]{2,1,0:T(8,128)(2,1)} %collective-permute-done.22.refs_9_), channel_id=1, source_target_pairs={{0,16},{8,24},{16,0},{24,8},{1,17},{9,25},{17,1},{25,9},{2,18},{10... | collective-permute-start | bytes 1327112 | tf_op jit(solution)/shard_map/ppermute | solution.py:350
  73.5 8.3 %collective-permute-start.20 = (bf16[6,48,384]{2,1,0:T(8,128)(2,1)S(1)}, bf16[6,48,384]{2,1,0:T(8,128)(2,1)S(1)}, u32[]{:S(2)}, u32[]{:S(2)}) collective-permute-start(bf16[6,48,384]{2,1,0:T(8,128)(2,1)S(1)} %slice.323), channel_id=1, source_target_pairs={{0,16},{8,24},{16,0},{24,8},{1,17},{9,25},{17,1},{25,9},{2,18},{10... | collective-permute-start | bytes 663560 | tf_op jit(solution)/shard_map/ppermute | solution.py:350
  74.8 9.6 %collective-permute-start.24 = (bf16[6,48,384]{2,1,0:T(8,128)(2,1)S(1)}, bf16[6,48,384]{2,1,0:T(8,128)(2,1)S(1)}, u32[]{:S(2)}, u32[]{:S(2)}) collective-permute-start(bf16[6,48,384]{2,1,0:T(8,128)(2,1)S(1)} %slice.412), channel_id=1, source_target_pairs={{0,8},{8,0},{16,24},{24,16},{1,9},{9,1},{17,25},{25,17},{2,10},{10... | collective-permute-start | bytes 663560 | tf_op jit(solution)/shard_map/ppermute | solution.py:350
  81.8 6.8 %collective-permute-start.25 = (bf16[6,48,384]{2,1,0:T(8,128)(2,1)S(1)}, bf16[6,48,384]{2,1,0:T(8,128)(2,1)S(1)}, u32[]{:S(2)}, u32[]{:S(2)}) collective-permute-start(bf16[6,48,384]{2,1,0:T(8,128)(2,1)S(1)} %slice.413), channel_id=1, source_target_pairs={{0,16},{8,24},{16,0},{24,8},{1,17},{9,25},{17,1},{25,9},{2,18},{10... | collective-permute-start | bytes 663560 | tf_op jit(solution)/shard_map/ppermute | solution.py:350
  83.0 45.9 %collective-permute-start.21 = (bf16[84,48,384]{2,1,0:T(8,128)(2,1)}, bf16[84,48,384]{2,1,0:T(8,128)(2,1)}, u32[]{:S(2)}, u32[]{:S(2)}) collective-permute-start(bf16[84,48,384]{2,1,0:T(8,128)(2,1)} %constant_dynamic-update-slice_fusion.13), channel_id=1, source_target_pairs={{0,1},{1,0},{2,3},{3,2},{4,5},{5,4},{6,7},{7,6},{8,9},{9,8},{10,11... | collective-permute-start | bytes 9289736 | tf_op jit(solution)/shard_map/ppermute | solution.py:342
  83.0 16.1 %collective-permute-start.29 = (bf16[12,48,384]{2,1,0:T(8,128)(2,1)S(1)}, bf16[12,48,384]{2,1,0:T(8,128)(2,1)S(1)}, u32[]{:S(2)}, u32[]{:S(2)}) collective-permute-start(bf16[12,48,384]{2,1,0:T(8,128)(2,1)S(1)} %collective-permute-done.23.refs_10_), channel_id=1, source_target_pairs={{0,8},{8,0},{16,24},{24,16},{1,9},{9,1},{17,25},{25,17},{2,10},{10... | collective-permute-start | bytes 1327112 | tf_op jit(solution)/shard_map/ppermute | solution.py:350
  84.5 13.0 %collective-permute-start.30 = (bf16[12,48,384]{2,1,0:T(8,128)(2,1)S(1)}, bf16[12,48,384]{2,1,0:T(8,128)(2,1)S(1)}, u32[]{:S(2)}, u32[]{:S(2)}) collective-permute-start(bf16[12,48,384]{2,1,0:T(8,128)(2,1)S(1)} %collective-permute-done.23.refs_10_), channel_id=1, source_target_pairs={{0,16},{8,24},{16,0},{24,8},{1,17},{9,25},{17,1},{25,9},{2,18},{10... | collective-permute-start | bytes 1327112 | tf_op jit(solution)/shard_map/ppermute | solution.py:350
  91.7 37.2 %collective-permute-start.28 = (bf16[60,48,384]{2,1,0:T(8,128)(2,1)}, bf16[60,48,384]{2,1,0:T(8,128)(2,1)}, u32[]{:S(2)}, u32[]{:S(2)}) collective-permute-start(bf16[60,48,384]{2,1,0:T(8,128)(2,1)} %constant_dynamic-update-slice_fusion.29), channel_id=1, source_target_pairs={{0,1},{1,0},{2,3},{3,2},{4,5},{5,4},{6,7},{7,6},{8,9},{9,8},{10,11... | collective-permute-start | bytes 6635528 | tf_op jit(solution)/shard_map/ppermute | solution.py:342
  97.4 6.8 %collective-permute-start.31 = (bf16[6,48,384]{2,1,0:T(8,128)(2,1)S(1)}, bf16[6,48,384]{2,1,0:T(8,128)(2,1)S(1)}, u32[]{:S(2)}, u32[]{:S(2)}) collective-permute-start(bf16[6,48,384]{2,1,0:T(8,128)(2,1)S(1)} %slice.414), channel_id=1, source_target_pairs={{0,8},{8,0},{16,24},{24,16},{1,9},{9,1},{17,25},{25,17},{2,10},{10... | collective-permute-start | bytes 663560 | tf_op jit(solution)/shard_map/ppermute | solution.py:350
  99.2 6.6 %collective-permute-start.32 = (bf16[6,48,384]{2,1,0:T(8,128)(2,1)S(1)}, bf16[6,48,384]{2,1,0:T(8,128)(2,1)S(1)}, u32[]{:S(2)}, u32[]{:S(2)}) collective-permute-start(bf16[6,48,384]{2,1,0:T(8,128)(2,1)S(1)} %slice.415), channel_id=1, source_target_pairs={{0,16},{8,24},{16,0},{24,8},{1,17},{9,25},{17,1},{25,9},{2,18},{10... | collective-permute-start | bytes 663560 | tf_op jit(solution)/shard_map/ppermute | solution.py:350
  112.6 16.3 %collective-permute-start.35 = (bf16[48,48,384]{2,1,0:T(8,128)(2,1)}, bf16[48,48,384]{2,1,0:T(8,128)(2,1)}, u32[]{:S(2)}, u32[]{:S(2)}) collective-permute-start(bf16[48,48,384]{2,1,0:T(8,128)(2,1)} %constant_dynamic-update-slice_fusion.35), channel_id=1, source_target_pairs={{0,1},{1,0},{2,3},{3,2},{4,5},{5,4},{6,7},{7,6},{8,9},{9,8},{10,11... | collective-permute-start | bytes 5308424 | tf_op jit(solution)/shard_map/ppermute | solution.py:342
  181.5 51.4 %collective-permute-start.36 = (bf16[4,12,48,384]{3,2,1,0:T(8,128)(2,1)}, bf16[4,12,48,384]{3,2,1,0:T(8,128)(2,1)S(1)}, u32[]{:S(2)}, u32[]{:S(2)}) collective-permute-start(bf16[4,12,48,384]{3,2,1,0:T(8,128)(2,1)} %get-tuple-element.76), channel_id=1, source_target_pairs={{0,1},{1,0},{2,3},{3,2},{4,5},{5,4},{6,7},{7,6},{8,9},{9,8},{10,11... | collective-permute-start | bytes 5308424 | tf_op jit(solution)/shard_map/ppermute | solution.py:342
  197.9 37.1 %collective-permute-start.37 = (bf16[4,12,48,384]{3,2,1,0:T(8,128)(2,1)}, bf16[4,12,48,384]{3,2,1,0:T(8,128)(2,1)}, u32[]{:S(2)}, u32[]{:S(2)}) collective-permute-start(bf16[4,12,48,384]{3,2,1,0:T(8,128)(2,1)} %get-tuple-element.78), channel_id=1, source_target_pairs={{0,1},{1,0},{2,3},{3,2},{4,5},{5,4},{6,7},{7,6},{8,9},{9,8},{10,11... | collective-permute-start | bytes 5308424 | tf_op jit(solution)/shard_map/ppermute | solution.py:342
  214.8 23.3 %collective-permute-start.38 = (bf16[4,12,48,384]{3,2,1,0:T(8,128)(2,1)}, bf16[4,12,48,384]{3,2,1,0:T(8,128)(2,1)}, u32[]{:S(2)}, u32[]{:S(2)}) collective-permute-start(bf16[4,12,48,384]{3,2,1,0:T(8,128)(2,1)} %get-tuple-element.80), channel_id=1, source_target_pairs={{0,1},{1,0},{2,3},{3,2},{4,5},{5,4},{6,7},{7,6},{8,9},{9,8},{10,11... | collective-permute-start | bytes 5308424 | tf_op jit(solution)/shard_map/ppermute | solution.py:342
  231.0 9.4 %collective-permute-start.39 = (bf16[4,12,48,384]{3,2,1,0:T(8,128)(2,1)}, bf16[4,12,48,384]{3,2,1,0:T(8,128)(2,1)}, u32[]{:S(2)}, u32[]{:S(2)}) collective-permute-start(bf16[4,12,48,384]{3,2,1,0:T(8,128)(2,1)} %get-tuple-element.82), channel_id=1, source_target_pairs={{0,1},{1,0},{2,3},{3,2},{4,5},{5,4},{6,7},{7,6},{8,9},{9,8},{10,11... | collective-permute-start | bytes 5308424 | tf_op jit(solution)/shard_map/ppermute | solution.py:342
  243.0 8.4 %collective-permute-start.44 = (bf16[6,48,384]{2,1,0:T(8,128)(2,1)S(1)}, bf16[6,48,384]{2,1,0:T(8,128)(2,1)S(1)}, u32[]{:S(2)}, u32[]{:S(2)}) collective-permute-start(bf16[6,48,384]{2,1,0:T(8,128)(2,1)S(1)} %get-tuple-element.111), channel_id=1, source_target_pairs={{0,8},{8,0},{16,24},{24,16},{1,9},{9,1},{17,25},{25,17},{2,10},{10... | collective-permute-start | bytes 663560 | tf_op jit(solution)/shard_map/ppermute | solution.py:350
  244.0 7.4 %collective-permute-start.42 = (bf16[6,48,384]{2,1,0:T(8,128)(2,1)S(1)}, bf16[6,48,384]{2,1,0:T(8,128)(2,1)S(1)}, u32[]{:S(2)}, u32[]{:S(2)}) collective-permute-start(bf16[6,48,384]{2,1,0:T(8,128)(2,1)S(1)} %get-tuple-element.112), channel_id=1, source_target_pairs={{0,16},{8,24},{16,0},{24,8},{1,17},{9,25},{17,1},{25,9},{2,18},{10... | collective-permute-start | bytes 663560 | tf_op jit(solution)/shard_map/ppermute | solution.py:350
  244.9 26.3 %collective-permute-start.40 = (bf16[6,48,384]{2,1,0:T(8,128)(2,1)S(1)}, bf16[6,48,384]{2,1,0:T(8,128)(2,1)S(1)}, u32[]{:S(2)}, u32[]{:S(2)}) collective-permute-start(bf16[6,48,384]{2,1,0:T(8,128)(2,1)S(1)} %get-tuple-element.115), channel_id=1, source_target_pairs={{0,8},{8,0},{16,24},{24,16},{1,9},{9,1},{17,25},{25,17},{2,10},{10... | collective-permute-start | bytes 663560 | tf_op jit(solution)/shard_map/ppermute | solution.py:350
  251.5 23.1 %collective-permute-start.45 = (bf16[12,48,384]{2,1,0:T(8,128)(2,1)S(1)}, bf16[12,48,384]{2,1,0:T(8,128)(2,1)S(1)}, u32[]{:S(2)}, u32[]{:S(2)}) collective-permute-start(bf16[12,48,384]{2,1,0:T(8,128)(2,1)S(1)} %pad_maximum_fusion.2), channel_id=1, source_target_pairs={{0,16},{8,24},{16,0},{24,8},{1,17},{9,25},{17,1},{25,9},{2,18},{10... | collective-permute-start | bytes 1327112 | tf_op jit(solution)/shard_map/ppermute | solution.py:350
  252.3 23.2 %collective-permute-start.43 = (bf16[12,48,384]{2,1,0:T(8,128)(2,1)S(1)}, bf16[12,48,384]{2,1,0:T(8,128)(2,1)S(1)}, u32[]{:S(2)}, u32[]{:S(2)}) collective-permute-start(bf16[12,48,384]{2,1,0:T(8,128)(2,1)S(1)} %pad_maximum_fusion.1), channel_id=1, source_target_pairs={{0,8},{8,0},{16,24},{24,16},{1,9},{9,1},{17,25},{25,17},{2,10},{10... | collective-permute-start | bytes 1327112 | tf_op jit(solution)/shard_map/ppermute | solution.py:350
  253.5 11.8 %collective-permute-start.61 = (f32[12,384]{1,0:T(8,128)S(1)}, f32[12,384]{1,0:T(8,128)S(1)}, u32[]{:S(2)}, u32[]{:S(2)}) collective-permute-start(f32[12,384]{1,0:T(8,128)S(1)} %get-tuple-element.162), channel_id=1, source_target_pairs={{0,24},{8,16},{16,8},{24,0},{1,25},{9,17},{17,9},{25,1},{2,26},{10... | collective-permute-start | bytes 55304 | tf_op jit(solution)/shard_map/ppermute | solution.py:350
  255.2 11.4 %collective-permute-start.60 = (f32[12,384]{1,0:T(8,128)S(1)}, f32[12,384]{1,0:T(8,128)S(1)}, u32[]{:S(2)}, u32[]{:S(2)}) collective-permute-start(f32[12,384]{1,0:T(8,128)S(1)} %get-tuple-element.163), channel_id=1, source_target_pairs={{0,16},{8,24},{16,0},{24,8},{1,17},{9,25},{17,1},{25,9},{2,18},{10... | collective-permute-start | bytes 55304 | tf_op jit(solution)/shard_map/ppermute | solution.py:350
  265.3 8.4 %collective-permute-start.41 = (bf16[6,48,384]{2,1,0:T(8,128)(2,1)S(1)}, bf16[6,48,384]{2,1,0:T(8,128)(2,1)S(1)}, u32[]{:S(2)}, u32[]{:S(2)}) collective-permute-start(bf16[6,48,384]{2,1,0:T(8,128)(2,1)S(1)} %get-tuple-element.114), channel_id=1, source_target_pairs={{0,16},{8,24},{16,0},{24,8},{1,17},{9,25},{17,1},{25,9},{2,18},{10... | collective-permute-start | bytes 663560 | tf_op jit(solution)/shard_map/ppermute | solution.py:350
  270.5 7.5 %collective-permute-start.64 = (f32[4,12,384]{2,1,0:T(8,128)S(1)}, f32[4,12,384]{2,1,0:T(8,128)S(1)}, u32[]{:S(2)}, u32[]{:S(2)}) collective-permute-start(f32[4,12,384]{2,1,0:T(8,128)S(1)} %get-tuple-element.160), channel_id=1, source_target_pairs={{0,6},{1,7},{2,4},{3,5},{4,2},{5,3},{6,0},{7,1},{8,14},{9,15},{10,... | collective-permute-start | bytes 221192 | tf_op jit(solution)/shard_map/ppermute | solution.py:346
  271.3 7.6 %collective-permute-start.63 = (f32[4,12,384]{2,1,0:T(8,128)S(1)}, f32[4,12,384]{2,1,0:T(8,128)S(1)}, u32[]{:S(2)}, u32[]{:S(2)}) collective-permute-start(f32[4,12,384]{2,1,0:T(8,128)S(1)} %get-tuple-element.160), channel_id=1, source_target_pairs={{0,4},{1,5},{2,6},{3,7},{4,0},{5,1},{6,2},{7,3},{8,12},{9,13},{10,... | collective-permute-start | bytes 221192 | tf_op jit(solution)/shard_map/ppermute | solution.py:346
  273.7 10.7 %collective-permute-start.51 = (bf16[6,48,384]{2,1,0:T(8,128)(2,1)S(1)}, bf16[6,48,384]{2,1,0:T(8,128)(2,1)S(1)}, u32[]{:S(2)}, u32[]{:S(2)}) collective-permute-start(bf16[6,48,384]{2,1,0:T(8,128)(2,1)S(1)} %get-tuple-element.88), channel_id=1, source_target_pairs={{0,8},{8,0},{16,24},{24,16},{1,9},{9,1},{17,25},{25,17},{2,10},{10... | collective-permute-start | bytes 663560 | tf_op jit(solution)/shard_map/ppermute | solution.py:350
  274.6 9.7 %collective-permute-start.47 = (bf16[6,48,384]{2,1,0:T(8,128)(2,1)S(1)}, bf16[6,48,384]{2,1,0:T(8,128)(2,1)S(1)}, u32[]{:S(2)}, u32[]{:S(2)}) collective-permute-start(bf16[6,48,384]{2,1,0:T(8,128)(2,1)S(1)} %get-tuple-element.84), channel_id=1, source_target_pairs={{0,16},{8,24},{16,0},{24,8},{1,17},{9,25},{17,1},{25,9},{2,18},{10... | collective-permute-start | bytes 663560 | tf_op jit(solution)/shard_map/ppermute | solution.py:350
  275.5 8.8 %collective-permute-start.46 = (bf16[6,48,384]{2,1,0:T(8,128)(2,1)S(1)}, bf16[6,48,384]{2,1,0:T(8,128)(2,1)S(1)}, u32[]{:S(2)}, u32[]{:S(2)}) collective-permute-start(bf16[6,48,384]{2,1,0:T(8,128)(2,1)S(1)} %get-tuple-element.83), channel_id=1, source_target_pairs={{0,16},{8,24},{16,0},{24,8},{1,17},{9,25},{17,1},{25,9},{2,18},{10... | collective-permute-start | bytes 663560 | tf_op jit(solution)/shard_map/ppermute | solution.py:350
  278.0 6.4 %collective-permute-start.54 = (bf16[6,48,384]{2,1,0:T(8,128)(2,1)S(1)}, bf16[6,48,384]{2,1,0:T(8,128)(2,1)S(1)}, u32[]{:S(2)}, u32[]{:S(2)}) collective-permute-start(bf16[6,48,384]{2,1,0:T(8,128)(2,1)S(1)} %get-tuple-element.91), channel_id=1, source_target_pairs={{0,8},{8,0},{16,24},{24,16},{1,9},{9,1},{17,25},{25,17},{2,10},{10... | collective-permute-start | bytes 663560 | tf_op jit(solution)/shard_map/ppermute | solution.py:350
  285.6 12.9 %collective-permute-start.48 = (bf16[12,48,384]{2,1,0:T(8,128)(2,1)}, bf16[12,48,384]{2,1,0:T(8,128)(2,1)}, u32[]{:S(2)}, u32[]{:S(2)}) collective-permute-start(bf16[12,48,384]{2,1,0:T(8,128)(2,1)} %get-tuple-element.85), channel_id=1, source_target_pairs={{0,8},{8,0},{16,24},{24,16},{1,9},{9,1},{17,25},{25,17},{2,10},{10... | collective-permute-start | bytes 1327112 | tf_op jit(solution)/shard_map/ppermute | solution.py:350
  286.8 12.4 %collective-permute-start.49 = (bf16[12,48,384]{2,1,0:T(8,128)(2,1)S(1)}, bf16[12,48,384]{2,1,0:T(8,128)(2,1)}, u32[]{:S(2)}, u32[]{:S(2)}) collective-permute-start(bf16[12,48,384]{2,1,0:T(8,128)(2,1)S(1)} %get-tuple-element.86), channel_id=1, source_target_pairs={{0,16},{8,24},{16,0},{24,8},{1,17},{9,25},{17,1},{25,9},{2,18},{10... | collective-permute-start | bytes 1327112 | tf_op jit(solution)/shard_map/ppermute | solution.py:350
  299.2 11.8 %collective-permute-start.52 = (bf16[12,48,384]{2,1,0:T(8,128)(2,1)}, bf16[12,48,384]{2,1,0:T(8,128)(2,1)}, u32[]{:S(2)}, u32[]{:S(2)}) collective-permute-start(bf16[12,48,384]{2,1,0:T(8,128)(2,1)} %get-tuple-element.89), channel_id=1, source_target_pairs={{0,16},{8,24},{16,0},{24,8},{1,17},{9,25},{17,1},{25,9},{2,18},{10... | collective-permute-start | bytes 1327112 | tf_op jit(solution)/shard_map/ppermute | solution.py:350
  299.9 11.5 %collective-permute-start.50 = (bf16[12,48,384]{2,1,0:T(8,128)(2,1)}, bf16[12,48,384]{2,1,0:T(8,128)(2,1)}, u32[]{:S(2)}, u32[]{:S(2)}) collective-permute-start(bf16[12,48,384]{2,1,0:T(8,128)(2,1)} %get-tuple-element.87), channel_id=1, source_target_pairs={{0,8},{8,0},{16,24},{24,16},{1,9},{9,1},{17,25},{25,17},{2,10},{10... | collective-permute-start | bytes 1327112 | tf_op jit(solution)/shard_map/ppermute | solution.py:350
  313.8 17.2 %collective-permute-start.58 = (bf16[12,48,384]{2,1,0:T(8,128)(2,1)S(1)}, bf16[12,48,384]{2,1,0:T(8,128)(2,1)S(1)}, u32[]{:S(2)}, u32[]{:S(2)}) collective-permute-start(bf16[12,48,384]{2,1,0:T(8,128)(2,1)S(1)} %get-tuple-element.124), channel_id=1, source_target_pairs={{0,2},{1,3},{2,0},{3,1},{4,6},{5,7},{6,4},{7,5},{8,10},{9,11},{10,... | collective-permute-start | bytes 1327112 | tf_op jit(solution)/shard_map/ppermute | solution.py:346
  315.3 31.2 %collective-permute-start.57 = (bf16[12,48,384]{2,1,0:T(8,128)(2,1)S(1)}, bf16[12,48,384]{2,1,0:T(8,128)(2,1)S(1)}, u32[]{:S(2)}, u32[]{:S(2)}) collective-permute-start(bf16[12,48,384]{2,1,0:T(8,128)(2,1)S(1)} %get-tuple-element.125), channel_id=1, source_target_pairs={{0,4},{1,5},{2,6},{3,7},{4,0},{5,1},{6,2},{7,3},{8,12},{9,13},{10,... | collective-permute-start | bytes 1327112 | tf_op jit(solution)/shard_map/ppermute | solution.py:346
  316.8 37.0 %collective-permute-start.56 = (bf16[12,48,384]{2,1,0:T(8,128)(2,1)S(1)}, bf16[12,48,384]{2,1,0:T(8,128)(2,1)S(1)}, u32[]{:S(2)}, u32[]{:S(2)}) collective-permute-start(bf16[12,48,384]{2,1,0:T(8,128)(2,1)S(1)} %get-tuple-element.123), channel_id=1, source_target_pairs={{0,6},{1,7},{2,4},{3,5},{4,2},{5,3},{6,0},{7,1},{8,14},{9,15},{10,... | collective-permute-start | bytes 1327112 | tf_op jit(solution)/shard_map/ppermute | solution.py:346
  317.3 36.5 %collective-permute-start.55 = (bf16[12,48,384]{2,1,0:T(8,128)(2,1)S(1)}, bf16[12,48,384]{2,1,0:T(8,128)(2,1)S(1)}, u32[]{:S(2)}, u32[]{:S(2)}) collective-permute-start(bf16[12,48,384]{2,1,0:T(8,128)(2,1)S(1)} %get-tuple-element.92), channel_id=1, source_target_pairs={{0,16},{8,24},{16,0},{24,8},{1,17},{9,25},{17,1},{25,9},{2,18},{10... | collective-permute-start | bytes 1327112 | tf_op jit(solution)/shard_map/ppermute | solution.py:350
  318.6 35.2 %collective-permute-start.53 = (bf16[12,48,384]{2,1,0:T(8,128)(2,1)S(1)}, bf16[12,48,384]{2,1,0:T(8,128)(2,1)S(1)}, u32[]{:S(2)}, u32[]{:S(2)}) collective-permute-start(bf16[12,48,384]{2,1,0:T(8,128)(2,1)S(1)} %get-tuple-element.90), channel_id=1, source_target_pairs={{0,8},{8,0},{16,24},{24,16},{1,9},{9,1},{17,25},{25,17},{2,10},{10... | collective-permute-start | bytes 1327112 | tf_op jit(solution)/shard_map/ppermute | solution.py:350
  (51 other events, 708.9 us)

commit v3 on v2

--- a/solution.py
+++ b/solution.py
@@ -17,6 +17,7 @@
 BF = jnp.bfloat16
 F32 = jnp.float32
 HIGH = lax.Precision.HIGHEST
+BOTH = ("section", "batch")
 C0 = math.sqrt(2.0 / math.pi)
 C1 = 0.044715
 VMEM_LIMIT = 60 * 2**20
@@ -89,9 +90,8 @@
     def weight(j):
         return w[layer, j].reshape(width, width)
 
-    here = jnp.bitwise_xor(section, layer)
-    mod = mods[here]
-    bias = biases[here]
+    mod = mods[layer]
+    bias = biases[layer]
     xs[0] = value[...]
     x = value[...].astype(F32)
     normed, _ = standard(x)
@@ -202,7 +202,7 @@
 ):
     seq, width = gbb.shape
     size = width // HEADS
-    section, place, core = ids[0], ids[1], ids[2]
+    place, core = ids[1], ids[2]
     rows = width // SHARDS
 
     def weight(j):
@@ -220,7 +220,7 @@
         for part in range(SHARDS):
             keep(2 * j + part // 4, 8 + part % 4, value[part * rows : (part + 1) * rows])
 
-    mod = mods[jnp.bitwise_xor(section, layer)]
+    mod = mods[layer]
     shift_a, scale_a, gate_a, shift_b, scale_b, gate_b = (mod[i : i + 1] for i in range(6))
     gout = grad[0].astype(F32)
     vec[5:6] = jnp.sum(gout * branch_b[0].astype(F32), 0, keepdims=True)
@@ -354,17 +354,21 @@
     return lax.optimization_barrier((value,) + others)[0]
 
 
-def gather_shards(w):
+def gather_shards(w, small, exchange):
     x0, y0, z1 = over_section(w, 1), over_section(w, 2), over_z(w, 1)
     z2 = over_z(w, 2)
+    z1, small = lax.optimization_barrier((z1, small))
+    small = lax.all_to_all(small, BOTH, 0, 0, tiled=True)
     x1, y1 = over_section(z1, 1), over_section(z1, 2)
-    z3 = over_z(after(w, z1), 3)
-    p0 = over_section(after(y0, z1)[:6], 1)
-    q0 = over_section(after(x0, z1)[6:], 2)
-    x2, y2 = over_section(after(z2, x1), 1), over_section(after(z2, y1), 2)
+    z3 = over_z(z2, 1)
+    p0, q0 = over_section(y0[:6], 1), over_section(x0[6:], 2)
+    x1, small = lax.optimization_barrier((x1, small))
+    part = exchange(small)
+    x2, y2 = over_section(z2, 1), over_section(z2, 2)
     p1, q1 = over_section(y1[:6], 1), over_section(x1[6:], 2)
-    x3, y3 = over_section(after(z3, x2), 1), over_section(after(z3, y2), 2)
+    x3, y3 = over_section(z3, 1), over_section(z3, 2)
     p2, q2 = over_section(y2[:6], 1), over_section(x2[6:], 2)
+    x3, part = lax.optimization_barrier((x3, part))
     p3, q3 = over_section(y3[:6], 1), over_section(x3[6:], 2)
     names = {}
     for zx, group in enumerate(
@@ -391,56 +395,50 @@
             plan[key + (1,)].append((len(sources), low, start))
             start += array.shape[0]
         sources.append(other)
-    sizes = {}
     final = {}
     for key, parts in plan.items():
         final[key] = []
         for index, low, start in parts:
             high = BLOCKS if key[0] != 3 else low + 6
             final[key].append((index, start, low, high))
-    return final, sources
-
-
-def sum_shards(parts):
+    return final, sources, small, part
+
+
+def sum_shards(parts, vec):
     def add(*values):
         total = values[0].astype(F32)
         for value in values[1:]:
             total = total + value.astype(F32)
         return total
 
-    stage = None
-    received = []
-    own = None
-    p, q = {}, {}
-
-    def corners(zx, gate):
-        p[zx] = over_section(after(parts[3, zx][:6], *gate), 1)
-        q[zx] = over_section(after(parts[3, zx][6:], *gate), 2)
-
-    corners(3, ())
-    corners(2, ())
-    gate = ()
-    for zx in (3, 2, 1, 0):
-        left = parts[1, zx]
-        left = jnp.concatenate([left[:6], add(left[6:], q[zx]).astype(BF)])
-        right = parts[2, zx]
-        right = jnp.concatenate([add(right[:6], p[zx]).astype(BF), right[6:]])
-        x, y = over_section(after(left, *gate), 1), over_section(after(right, *gate), 2)
-        if zx >= 2:
-            corners(zx - 2, (p[zx], q[zx]) + gate)
-        total = add(parts[0, zx], x, y)
-        gate = (x, y)
-        if zx:
-            received.append(over_z(total.astype(BF), zx))
-        else:
-            own = total
-    return add(own, *received)
-
-
-def gather_small(row):
-    cores = jnp.stack([row, over_core(row)])
-    places = jnp.stack([cores] + [over_z(cores, i) for i in (1, 2, 3)])
-    return jnp.stack([places] + [over_section(places, i) for i in (1, 2, 3)])
+    def joined(zx, p, q):
+        left = jnp.concatenate([parts[1, zx][:6], add(parts[1, zx][6:], q).astype(BF)])
+        right = jnp.concatenate([add(parts[2, zx][:6], p).astype(BF), parts[2, zx][6:]])
+        return left, right
+
+    p3, q3 = over_section(parts[3, 3][:6], 1), over_section(parts[3, 3][6:], 2)
+    d2, d1 = over_section(parts[3, 2], 1), over_section(parts[3, 1], 2)
+    left, right = joined(3, p3, q3)
+    x3, y3 = over_section(left, 1), over_section(right, 2)
+    p0, q0 = over_section(parts[3, 0][:6], 1), over_section(parts[3, 0][6:], 2)
+    left, right = parts[1, 2], add(parts[2, 2], d2).astype(BF)
+    x3, vec = lax.optimization_barrier((x3, vec))
+    vec = lax.all_to_all(vec, BOTH, 0, 0, tiled=True)
+    total = add(parts[0, 3], x3, y3).astype(BF)
+    left, right, total = lax.optimization_barrier((left, right, total))
+    z3 = over_z(total, 1)
+    x2, y2 = over_section(left, 1), over_section(right, 2)
+    left, right = add(parts[1, 1], d1).astype(BF), parts[2, 1]
+    total = add(parts[0, 2], x2, y2, z3).astype(BF)
+    left, right, total = lax.optimization_barrier((left, right, total))
+    z2, s2 = over_z(total[:6], 2), over_z(total[6:], 2)
+    x1, y1 = over_section(left, 1), over_section(right, 2)
+    left, right = joined(0, p0, q0)
+    total = add(parts[0, 1], x1, y1).astype(BF)
+    left, right, total, z2 = lax.optimization_barrier((left, right, total, z2))
+    x0, y0 = over_section(left, 1), over_section(right, 2)
+    z1 = over_z(total, 1)
+    return unpacked(parts[0, 0], x0, y0, z1, z2, s2), vec
 
 
 def body_permuted(
@@ -451,36 +449,31 @@
     width = tokens.shape[2]
     rows = width // SHARDS
     ids = jnp.stack([section, place, core, levels[0]]).astype(jnp.int32)
-    plan, sources = gather_shards(local_shard(w_qkv, w_o, w_up, w_down))
-
-    small = jnp.concatenate([b_o[0], b_up[0], b_down[0], lead.astype(BF)])
-    small = jnp.pad(small, (0, width - small.shape[0]))
-    smalls = gather_small(small)
-    leads = smalls[..., 6 * rows].reshape(-1)
-    order = jnp.arange(SHARDS) ^ batch
-    smalls = jnp.take(smalls.reshape(4, SHARDS, width), order, axis=1).astype(F32)
-    biases = jnp.stack(
-        [smalls[:, :, :rows].reshape(4, width)]
-        + [
-            smalls[:, 2 * j : 2 * j + 2, rows : 5 * rows].reshape(4, width)
-            for j in range(4)
-        ]
-        + [smalls[:, :, 5 * rows : 6 * rows].reshape(4, width)],
+    shard, small = packed(lead, w_qkv, w_o, w_up, w_down, b_o, b_up, b_down)
+    mine = []
+
+    def exchange(smalls):
+        conds = jax.nn.silu(embed_lead(smalls[:, 512], width))
+        mine.append(lax.dynamic_slice_in_dim(conds, batch * rows, rows, axis=1))
+        part = jnp.dot(mine[0], w_ada[0].astype(F32), precision=HIGH)
+        bias = jnp.zeros((6 * width,), F32)
+        bias = lax.dynamic_update_slice_in_dim(
+            bias, b_ada[0].astype(F32), batch * 6 * rows, axis=0
+        )
+        return lax.all_to_all(part + bias, BOTH, 0, 0, tiled=True)
+
+    plan, sources, smalls, part = gather_shards(shard, small, exchange)
+    mine = mine[0]
+    mods = jnp.sum(part.reshape(4, SHARDS, 6 * width), axis=1).reshape(4, 6, width)
+    vectors = smalls.reshape(4, SHARDS, 640).astype(F32)
+    biases = jnp.concatenate(
+        [
+            vectors[:, :, :rows].reshape(4, 1, width),
+            vectors[:, :, 128 : 128 + 4 * rows].reshape(4, 4, width),
+            vectors[:, :, 384 : 384 + rows].reshape(4, 1, width),
+        ],
         axis=1,
     )
-    conds = jax.nn.silu(embed_lead(leads, width))
-    mine = lax.dynamic_slice_in_dim(conds, batch * rows, rows, axis=1)
-    part = jnp.dot(mine, w_ada[0].astype(F32), precision=HIGH)
-    bias = jnp.zeros((6 * width,), F32)
-    bias = lax.dynamic_update_slice_in_dim(
-        bias, b_ada[0].astype(F32), batch * 6 * rows, axis=0
-    )
-    part = (part + bias).reshape(4, 4, 2, 6 * width)
-    part = part[:, :, 0] + over_core(part[:, :, 1])
-    part = part[:, 0] + over_z(part[:, 1], 1) + over_z(part[:, 2], 2) + over_z(part[:, 3], 3)
-    mods = jnp.stack([part[0]] + [over_section(part[i], i) for i in (1, 2, 3)])
-    mods = mods.reshape(4, 6, width)
-
     result, w, *saved = forward(plan, sources, ids, tokens, mods, biases)
     grad = cotangent
     sums = jnp.zeros((4, 4, BLOCKS, rows, width), BF)
@@ -489,12 +482,10 @@
         grad, kept, sent, vecs[layer] = backward(layer, ids, grad, mods, w, saved)
         both = (kept.astype(F32) + over_core(sent).astype(F32)).astype(BF)
         sums = lax.dynamic_update_index_in_dim(sums, both, section ^ layer, 0)
-    total = sum_shards({(i, j): sums[i, j] for i in range(4) for j in range(4)})
-
-    vec = jnp.take(jnp.stack(vecs), jnp.arange(4) ^ section, axis=0)
-    vec = jnp.stack([vec[0]] + [over_section(vec[i], i) for i in (1, 2, 3)])
-    vec = jnp.stack([vec] + [over_z(vec, i) for i in (1, 2, 3)], axis=1)
-    vec = jnp.stack([vec, over_core(vec)], axis=2).reshape(32, 12, width)
+    vec = jnp.stack(vecs)[:, None].astype(BF)
+    vec = jnp.broadcast_to(vec, (4, SHARDS) + vec.shape[2:]).reshape(32, 12 * width)
+    totals, vec = sum_shards({(i, j): sums[i, j] for i in range(4) for j in range(4)}, vec)
+    vec = vec.astype(F32).reshape(32, 12, width)
     g_ada = jnp.dot(mine.T, vec[:, :6].reshape(32, 6 * width), precision=HIGH)[None]
     flat = jnp.sum(vec, 0)
 
@@ -506,18 +497,79 @@
     return (
         result,
         grad,
-        jnp.concatenate([total[0], total[1], total[2]], axis=1)[None],
-        total[3][None],
+        totals[0],
+        totals[1],
         slot(6, 7, rows),
-        jnp.concatenate([total[4 + j] for j in range(4)], axis=1)[None],
+        totals[2],
         slot(7, 11, 4 * rows),
-        total[8:].reshape(1, 4 * rows, width),
+        totals[3],
         slot(11, 12, rows),
         g_ada,
         slot(0, 6, 6 * rows),
     )
 
 
+def pack_kernel(lead, w_qkv, w_o, w_up, w_down, b_o, b_up, b_down, out, small):
+    _, rows, width = w_o.shape
+    for j in range(3):
+        out[j] = w_qkv[0, :, j * width : (j + 1) * width]
+    out[3] = w_o[0]
+    for j in range(4):
+        out[4 + j] = w_up[0, :, j * width : (j + 1) * width]
+        out[8 + j] = w_down[0, j * rows : (j + 1) * rows]
+    peers = small.shape[0]
+    small[...] = jnp.full(small.shape, lead[0].astype(F32), F32).astype(BF)
+    for start, bias in zip((0, 128, 384), (b_o, b_up, b_down)):
+        count = bias.shape[1]
+        small[:, start : start + count] = jnp.broadcast_to(
+            bias[...].astype(F32), (peers, count)
+        ).astype(BF)
+
+
+def packed(lead, w_qkv, w_o, w_up, w_down, b_o, b_up, b_down):
+    _, rows, width = w_o.shape
+    vmem = pl.BlockSpec(memory_space=pltpu.VMEM)
+    return pl.pallas_call(
+        pack_kernel,
+        in_specs=[pl.BlockSpec(memory_space=pltpu.SMEM)] + [vmem] * 7,
+        out_shape=[
+            jax.ShapeDtypeStruct((BLOCKS, rows, width), BF),
+            jax.ShapeDtypeStruct((32, 640), BF),
+        ],
+        name="pack",
+    )(lead, w_qkv, w_o, w_up, w_down, b_o, b_up, b_down)
+
+
+def unpack_kernel(own, x, y, z, low, high, g_qkv, g_o, g_up, g_down):
+    _, rows, width = g_o.shape
+    for j in range(BLOCKS):
+        last = low[j] if j < 6 else high[j - 6]
+        total = own[j].astype(F32) + x[j].astype(F32) + y[j].astype(F32)
+        total = total + z[j].astype(F32) + last.astype(F32)
+        if j < 3:
+            g_qkv[0, :, j * width : (j + 1) * width] = total
+        elif j == 3:
+            g_o[0] = total
+        elif j < 8:
+            g_up[0, :, (j - 4) * width : (j - 3) * width] = total
+        else:
+            g_down[0, (j - 8) * rows : (j - 7) * rows] = total
+
+
+def unpacked(own, x, y, z, low, high):
+    _, rows, width = own.shape
+    return pl.pallas_call(
+        unpack_kernel,
+        out_shape=[
+            jax.ShapeDtypeStruct((1, rows, 3 * width), F32),
+            jax.ShapeDtypeStruct((1, rows, width), F32),
+            jax.ShapeDtypeStruct((1, rows, 4 * width), F32),
+            jax.ShapeDtypeStruct((1, 4 * rows, width), F32),
+        ],
+        name="unpack",
+    )(own, x, y, z, low, high)
+
+
 def local_shard(w_qkv, w_o, w_up, w_down):
     _, rows, width = w_o.shape
 
@@ -527,9 +579,6 @@
     return jnp.concatenate(
         [blocks_of(w_qkv[0]), w_o, blocks_of(w_up[0]), w_down[0].reshape(4, rows, width)]
     )
-
-
-BOTH = ("section", "batch")
 
 
 def body_general(

time: 364 us -> 293 us (0.80)
  the two profiles are of different devices: /device:TPU:8 before, /device:TPU:0 now
where the time goes in v3:
time: 293 us; the launch traced here: 290 us
  Pallas kernels  105 us (36%)
  waiting for transfers between devices  67 us (23%)
  starting transfers between devices  58.5 us (20%)
  local copies, waits for them, and re-layouts  34.2 us (12%)
  other arithmetic  20.3 us (7%)
  between operations  3.06 us (1%)
    pallas_call x4, Pallas kernels, backward(): pl.pallas_call(functools.partial(backward_kernel, layer), grid=(1,), in_s...  64.7 us
    ppermute x30, waiting for transfers between devices, over_section(): return lax.ppermute(value, 'section', [(i, i ^ away) for i in range(4)])  48 us
    pallas_call x1, Pallas kernels, forward(): pl.pallas_call(functools.partial(forward_kernel, plan), grid=(layers,), i...  35.9 us
    ppermute x30, starting transfers between devices, over_section(): return lax.ppermute(value, 'section', [(i, i ^ away) for i in range(4)])  35.3 us
    unnamed x96, local copies, waits for them, and re-layouts  19.4 us
    ppermute x7, waiting for transfers between devices, over_z(): return lax.ppermute(value, 'batch', [(i, i ^ 2 * away) for i in range(8)])  17.8 us
    ppermute x7, starting transfers between devices, over_z(): return lax.ppermute(value, 'batch', [(i, i ^ 2 * away) for i in range(8)])  11.3 us
    dynamic_update_slice x4, other arithmetic, body_permuted(): sums = lax.dynamic_update_index_in_dim(sums, both, section ^ layer, 0)  7.45 us
  transfers between devices with their start and end apart: 47, of which 20 were waited for; matrix products, arithmetic and copies ran while one was open for 18% of the time, Pallas kernels for 17%

profile of v3, /device:TPU:0, one launch (start us, length us, event | category | flops | bytes accessed | tf_op | source)
XLA Modules:
  0.0 289.6 jit_solution(6450563799978004266)
XLA Ops:
  1.3 1.9 pack.1
  3.2 3.0 %collective-permute-start.3 = (bf16[12,48,384]{2,1,0:T(8,128)(2,1)}, bf16[12,48,384]{2,1,0:T(8,128)(2,1)S(1)}, u32[]{:S(2)}, u32[]{:S(2)}) collective-permute-start(bf16[12,48,384]{2,1,0:T(8,128)(2,1)} %get-tuple-element.61.refs_0_), channel_id=1, source_target_pairs={{0,2},{1,3},{2,0},{3,1},{4,6},{5,7},{6,4},{7,5},{8,10},{9,11},{10,... | collective-permute-start | bytes 1327112 | tf_op jit(solution)/shard_map/ppermute | solution.py:346
  6.3 1.5 collective-permute-start.6
  7.8 1.5 collective-permute-start.5
  9.3 2.6 collective-permute-start
  12.9 1.9 constant_dynamic-update-slice_fusion.7
  14.7 8.8 %collective-permute-done.3.refs_1_ = bf16[12,48,384]{2,1,0:T(8,128)(2,1)S(1)} collective-permute-done((bf16[12,48,384]{2,1,0:T(8,128)(2,1)}, bf16[12,48,384]{2,1,0:T(8,128)(2,1)S(1)}, u32[]{:S(2)}, u32[]{:S(2)}) %collective-permute-start.3) | collective-permute-done | bytes 442400 | tf_op jit(solution)/shard_map/ppermute | solution.py:346
  23.5 2.6 collective-permute-start.4
  26.1 2.5 collective-permute-start.7
  29.2 1.4 reduce.6
  31.4 2.9 all-to-all-start
  35.0 1.8 collective-permute-start.8
  37.6 1.5 collective-permute-start.9
  39.0 1.5 collective-permute-start.1
  49.1 1.5 collective-permute-start.11
  53.0 3.9 %all-to-all-start.1 = ((f32[32,1,2304]{2,1,0:T(1,128)}), f32[32,1,2304]{2,1,0:T(1,128)S(1)}, u32[]{:S(2)}, u32[]{:S(2)}) async-start(f32[32,1,2304]{2,1,0:T(1,128)} %copy.28), calls=%async_computation.1 | async-start | bytes 589824 | tf_op jit(solution)/shard_map/all_to_all | solution.py:463
  57.0 1.9 collective-permute-start.12
  59.6 1.5 collective-permute-start.17
  62.4 1.8 constant_dynamic-update-slice_fusion.12
  65.1 2.9 collective-permute-done.12.refs_12_
  68.0 1.3 collective-permute-start.18
  71.7 6.1 %collective-permute-done.16.refs_17_ = bf16[12,48,384]{2,1,0:T(8,128)(2,1)S(1)} collective-permute-done((bf16[12,48,384]{2,1,0:T(8,128)(2,1)}, bf16[12,48,384]{2,1,0:T(8,128)(2,1)S(1)}, u32[]{:S(2)}, u32[]{:S(2)}) %collective-permute-start.16) | collective-permute-done | bytes 442400 | tf_op jit(solution)/shard_map/ppermute | solution.py:350
  83.4 2.4 collective-permute-done.19.refs_20_
  86.6 1.9 collective-permute-done.20.refs_21_
  93.3 35.9 %forward.1 = (bf16[1,416,384]{2,1,0:T(8,128)(2,1)}, bf16[4,12,8,48,384]{4,3,2,1,0:T(8,128)(2,1)}, bf16[4,416,384]{2,1,0:T(8,128)(2,1)}, bf16[4,416,1152]{2,1,0:T...) custom-call(s32[4]{0:T(128)} %pad_add_fusion.ids, ...), custom_call_target="tpu_custom_call" | custom-call | flops 6960000000 | bytes 80000000 | tf_op jit(solution)/shard_map/forward/pallas_call | solution.py:167
  129.2 16.2 %backward_3.1 = (bf16[1,416,384]{2,1,0:T(8,128)(2,1)}, bf16[4,12,48,384]{3,2,1,0:T(8,128)(2,1)}, bf16[4,12,48,384]{3,2,1,0:T(8,128)(2,1)}, f32[12,384]{1,0:T(8,128)}) custom-call(s32[4]{0:T(128)} %pad_add_fusion.ids, bf16[1,416,384]{2,1,0:T(8,128)(2,1)} %grad.1, f32[4,6,384]{2,1,0:T(8,128)} %reshape.158.mods, ...), custom_call_target="tpu_custom_call" | custom-call | flops 3480000000 | bytes 20000000 | tf_op jit(solution)/shard_map/backward_3/pallas_call | solution.py:304
  145.5 16.2 %backward_2.1 = (bf16[1,416,384]{2,1,0:T(8,128)(2,1)}, bf16[4,12,48,384]{3,2,1,0:T(8,128)(2,1)}, bf16[4,12,48,384]{3,2,1,0:T(8,128)(2,1)}, f32[12,384]{1,0:T(8,128)}) custom-call(s32[4]{0:T(128)} %pad_add_fusion.ids, bf16[1,416,384]{2,1,0:T(8,128)(2,1)} %get-tuple-element.79.grad, f32[4,6,384]{2,1,0:T(8,128)} %reshape.158.mods, ...), custom_call_target="tpu_custom_call" | custom-call | flops 3480000000 | bytes 20000000 | tf_op jit(solution)/shard_map/backward_2/pallas_call | solution.py:304
  162.2 16.3 %backward_1.1 = (bf16[1,416,384]{2,1,0:T(8,128)(2,1)}, bf16[4,12,48,384]{3,2,1,0:T(8,128)(2,1)}, bf16[4,12,48,384]{3,2,1,0:T(8,128)(2,1)}, f32[12,384]{1,0:T(8,128)}) custom-call(s32[4]{0:T(128)} %pad_add_fusion.ids, bf16[1,416,384]{2,1,0:T(8,128)(2,1)} %get-tuple-element.80.grad, f32[4,6,384]{2,1,0:T(8,128)} %reshape.158.mods, ...), custom_call_target="tpu_custom_call" | custom-call | flops 3480000000 | bytes 20000000 | tf_op jit(solution)/shard_map/backward_1/pallas_call | solution.py:304
  178.7 16.1 %backward_0.1 = (bf16[1,416,384]{2,1,0:T(8,128)(2,1)}, bf16[4,12,48,384]{3,2,1,0:T(8,128)(2,1)}, bf16[4,12,48,384]{3,2,1,0:T(8,128)(2,1)}, f32[12,384]{1,0:T(8,128)}) custom-call(s32[4]{0:T(128)} %pad_add_fusion.ids, bf16[1,416,384]{2,1,0:T(8,128)(2,1)} %get-tuple-element.81.grad, f32[4,6,384]{2,1,0:T(8,128)} %reshape.158.mods, ...), custom_call_target="tpu_custom_call" | custom-call | flops 3480000000 | bytes 20000000 | tf_op jit(solution)/shard_map/backward_0/pallas_call | solution.py:304
  198.2 2.3 fusion.4
  200.5 2.3 fusion.6
  202.8 2.2 fusion.8
  211.2 2.4 collective-permute-done.30
  214.5 4.7 %collective-permute-done.27 = bf16[6,48,384]{2,1,0:T(8,128)(2,1)S(1)} collective-permute-done((bf16[6,48,384]{2,1,0:T(8,128)(2,1)S(1)}, bf16[6,48,384]{2,1,0:T(8,128)(2,1)S(1)}, u32[]{:S(2)}, u32[]{:S(2)}) %collective-permute-start.27) | collective-permute-done | bytes 221216 | tf_op jit(solution)/shard_map/ppermute | solution.py:350
  222.9 14.2 %collective-permute-done.31 = bf16[12,48,384]{2,1,0:T(8,128)(2,1)S(1)} collective-permute-done((bf16[12,48,384]{2,1,0:T(8,128)(2,1)S(1)}, bf16[12,48,384]{2,1,0:T(8,128)(2,1)S(1)}, u32[]{:S(2)}, u32[]{:S(2)}) %collective-permute-start.31) | collective-permute-done | bytes 442400 | tf_op jit(solution)/shard_map/ppermute | solution.py:350
  238.4 1.3 collective-permute-start.36
  239.7 1.3 collective-permute-start.35
  243.4 3.8 %all-to-all-start.2 = ((bf16[32,2,2304]{2,1,0:T(2,128)(2,1)}), bf16[32,2,2304]{2,1,0:T(2,128)(2,1)S(1)}, u32[]{:S(2)}, u32[]{:S(2)}) async-start(bf16[32,2,2304]{2,1,0:T(2,128)(2,1)} %reshape.181), calls=%async_computation.2 | async-start | bytes 589824 | tf_op jit(solution)/shard_map/all_to_all | solution.py:426
  247.2 2.7 collective-permute-done.36
  251.1 2.0 collective-permute-done.34
  253.1 2.8 fusion.14
  257.9 2.4 collective-permute-start.39
  261.1 1.8 reduce.3
  265.8 1.4 fusion.17
  267.3 5.2 %collective-permute-done.39.low = bf16[6,48,384]{2,1,0:T(8,128)(2,1)S(1)} collective-permute-done((bf16[6,48,384]{2,1,0:T(8,128)(2,1)S(1)}, bf16[6,48,384]{2,1,0:T(8,128)(2,1)S(1)}, u32[]{:S(2)}, u32[]{:S(2)}) %collective-permute-start.39) | collective-permute-done | bytes 221216 | tf_op jit(solution)/shard_map/ppermute | solution.py:346
  273.1 1.7 collective-permute-start.41
  276.6 7.1 %collective-permute-done.40.x = bf16[12,48,384]{2,1,0:T(8,128)(2,1)S(1)} collective-permute-done((bf16[12,48,384]{2,1,0:T(8,128)(2,1)S(1)}, bf16[12,48,384]{2,1,0:T(8,128)(2,1)S(1)}, u32[]{:S(2)}, u32[]{:S(2)}) %collective-permute-start.40) | collective-permute-done | bytes 442400 | tf_op jit(solution)/shard_map/ppermute | solution.py:350
  286.7 2.5 unpack.1
  (214 shorter events, 61.3 us)
Async XLA Ops:
  0.6 50.2 %copy-start = (bf16[1,48,2304]{2,1,0:T(8,128)(2,1)S(1)}, bf16[1,48,2304]{2,1,0:T(8,128)(2,1)}, u32[]{:S(2)}) copy-start(bf16[1,48,2304]{2,1,0:T(8,128)(2,1)} %param.23) | copy-start | bytes 663556
  3.2 20.3 %collective-permute-start.3 = (bf16[12,48,384]{2,1,0:T(8,128)(2,1)}, bf16[12,48,384]{2,1,0:T(8,128)(2,1)S(1)}, u32[]{:S(2)}, u32[]{:S(2)}) collective-permute-start(bf16[12,48,384]{2,1,0:T(8,128)(2,1)} %get-tuple-element.61.refs_0_), channel_id=1, source_target_pairs={{0,2},{1,3},{2,0},{3,1},{4,6},{5,7},{6,4},{7,5},{8,10},{9,11},{10,... | collective-permute-start | bytes 1327112 | tf_op jit(solution)/shard_map/ppermute | solution.py:346
  6.3 28.0 %collective-permute-start.6 = (bf16[12,48,384]{2,1,0:T(8,128)(2,1)}, bf16[12,48,384]{2,1,0:T(8,128)(2,1)S(1)}, u32[]{:S(2)}, u32[]{:S(2)}) collective-permute-start(bf16[12,48,384]{2,1,0:T(8,128)(2,1)} %get-tuple-element.61.refs_0_), channel_id=1, source_target_pairs={{0,16},{8,24},{16,0},{24,8},{1,17},{9,25},{17,1},{25,9},{2,18},{10... | collective-permute-start | bytes 1327112 | tf_op jit(solution)/shard_map/ppermute | solution.py:350
  7.8 29.0 %collective-permute-start.5 = (bf16[12,48,384]{2,1,0:T(8,128)(2,1)}, bf16[12,48,384]{2,1,0:T(8,128)(2,1)S(1)}, u32[]{:S(2)}, u32[]{:S(2)}) collective-permute-start(bf16[12,48,384]{2,1,0:T(8,128)(2,1)} %get-tuple-element.61.refs_0_), channel_id=1, source_target_pairs={{0,8},{8,0},{16,24},{24,16},{1,9},{9,1},{17,25},{25,17},{2,10},{10... | collective-permute-start | bytes 1327112 | tf_op jit(solution)/shard_map/ppermute | solution.py:350
  9.3 29.8 %collective-permute-start = (bf16[12,48,384]{2,1,0:T(8,128)(2,1)}, bf16[12,48,384]{2,1,0:T(8,128)(2,1)S(1)}, u32[]{:S(2)}, u32[]{:S(2)}) collective-permute-start(bf16[12,48,384]{2,1,0:T(8,128)(2,1)} %get-tuple-element.61.refs_0_), channel_id=1, source_target_pairs={{0,4},{1,5},{2,6},{3,7},{4,0},{5,1},{6,2},{7,3},{8,12},{9,13},{10,... | collective-permute-start | bytes 1327112 | tf_op jit(solution)/shard_map/ppermute | solution.py:346
  23.5 20.4 %collective-permute-start.4 = (bf16[12,48,384]{2,1,0:T(8,128)(2,1)S(1)}, bf16[12,48,384]{2,1,0:T(8,128)(2,1)S(1)}, u32[]{:S(2)}, u32[]{:S(2)}) collective-permute-start(bf16[12,48,384]{2,1,0:T(8,128)(2,1)S(1)} %collective-permute-done.3.refs_1_), channel_id=1, source_target_pairs={{0,8},{8,0},{16,24},{24,16},{1,9},{9,1},{17,25},{25,17},{2,10},{10... | collective-permute-start | bytes 1327112 | tf_op jit(solution)/shard_map/ppermute | solution.py:350
  26.1 19.3 %collective-permute-start.7 = (bf16[12,48,384]{2,1,0:T(8,128)(2,1)S(1)}, bf16[12,48,384]{2,1,0:T(8,128)(2,1)S(1)}, u32[]{:S(2)}, u32[]{:S(2)}) collective-permute-start(bf16[12,48,384]{2,1,0:T(8,128)(2,1)S(1)} %collective-permute-done.3.refs_1_), channel_id=1, source_target_pairs={{0,16},{8,24},{16,0},{24,8},{1,17},{9,25},{17,1},{25,9},{2,18},{10... | collective-permute-start | bytes 1327112 | tf_op jit(solution)/shard_map/ppermute | solution.py:350
  31.4 12.4 %all-to-all-start = ((bf16[32,2,320]{2,1,0:T(2,128)(2,1)}), bf16[32,2,320]{2,1,0:T(2,128)(2,1)S(1)}, u32[]{:S(2)}, u32[]{:S(2)}) async-start(bf16[32,2,320]{2,1,0:T(2,128)(2,1)} %reshape.179), calls=%async_computation | async-start | bytes 98304 | tf_op jit(solution)/shard_map/all_to_all | solution.py:361
  35.0 11.8 %collective-permute-start.8 = (bf16[6,48,384]{2,1,0:T(8,128)(2,1)}, bf16[6,48,384]{2,1,0:T(8,128)(2,1)S(1)}, u32[]{:S(2)}, u32[]{:S(2)}) collective-permute-start(bf16[6,48,384]{2,1,0:T(8,128)(2,1)} %slice.225), channel_id=1, source_target_pairs={{0,8},{8,0},{16,24},{24,16},{1,9},{9,1},{17,25},{25,17},{2,10},{10... | collective-permute-start | bytes 663560 | tf_op jit(solution)/shard_map/ppermute | solution.py:350
  37.6 10.0 %collective-permute-start.9 = (bf16[6,48,384]{2,1,0:T(8,128)(2,1)}, bf16[6,48,384]{2,1,0:T(8,128)(2,1)S(1)}, u32[]{:S(2)}, u32[]{:S(2)}) collective-permute-start(bf16[6,48,384]{2,1,0:T(8,128)(2,1)} %slice.226), channel_id=1, source_target_pairs={{0,16},{8,24},{16,0},{24,8},{1,17},{9,25},{17,1},{25,9},{2,18},{10... | collective-permute-start | bytes 663560 | tf_op jit(solution)/shard_map/ppermute | solution.py:350
  39.0 20.6 %collective-permute-start.1 = (bf16[12,48,384]{2,1,0:T(8,128)(2,1)S(1)}, bf16[12,48,384]{2,1,0:T(8,128)(2,1)}, u32[]{:S(2)}, u32[]{:S(2)}) collective-permute-start(bf16[12,48,384]{2,1,0:T(8,128)(2,1)S(1)} %collective-permute-done.refs_9_), channel_id=1, source_target_pairs={{0,2},{1,3},{2,0},{3,1},{4,6},{5,7},{6,4},{7,5},{8,10},{9,11},{10,... | collective-permute-start | bytes 1327112 | tf_op jit(solution)/shard_map/ppermute | solution.py:346
  44.0 17.1 %collective-permute-start.13 = (bf16[12,48,384]{2,1,0:T(8,128)(2,1)S(1)}, bf16[12,48,384]{2,1,0:T(8,128)(2,1)S(1)}, u32[]{:S(2)}, u32[]{:S(2)}) collective-permute-start(bf16[12,48,384]{2,1,0:T(8,128)(2,1)S(1)} %collective-permute-done.refs_9_), channel_id=1, source_target_pairs={{0,8},{8,0},{16,24},{24,16},{1,9},{9,1},{17,25},{25,17},{2,10},{10... | collective-permute-start | bytes 1327112 | tf_op jit(solution)/shard_map/ppermute | solution.py:350
  45.4 11.5 %collective-permute-start.14 = (bf16[12,48,384]{2,1,0:T(8,128)(2,1)S(1)}, bf16[12,48,384]{2,1,0:T(8,128)(2,1)S(1)}, u32[]{:S(2)}, u32[]{:S(2)}) collective-permute-start(bf16[12,48,384]{2,1,0:T(8,128)(2,1)S(1)} %collective-permute-done.refs_9_), channel_id=1, source_target_pairs={{0,16},{8,24},{16,0},{24,8},{1,17},{9,25},{17,1},{25,9},{2,18},{10... | collective-permute-start | bytes 1327112 | tf_op jit(solution)/shard_map/ppermute | solution.py:350
  48.4 44.9 %collective-permute-start.10 = (bf16[84,48,384]{2,1,0:T(8,128)(2,1)}, bf16[84,48,384]{2,1,0:T(8,128)(2,1)}, u32[]{:S(2)}, u32[]{:S(2)}) collective-permute-start(bf16[84,48,384]{2,1,0:T(8,128)(2,1)} %constant_dynamic-update-slice_fusion), channel_id=1, source_target_pairs={{0,1},{1,0},{2,3},{3,2},{4,5},{5,4},{6,7},{7,6},{8,9},{9,8},{10,11... | collective-permute-start | bytes 9289736 | tf_op jit(solution)/shard_map/ppermute | solution.py:342
  49.1 15.1 %collective-permute-start.11 = (bf16[6,48,384]{2,1,0:T(8,128)(2,1)}, bf16[6,48,384]{2,1,0:T(8,128)(2,1)S(1)}, u32[]{:S(2)}, u32[]{:S(2)}) collective-permute-start(bf16[6,48,384]{2,1,0:T(8,128)(2,1)} %slice.227), channel_id=1, source_target_pairs={{0,8},{8,0},{16,24},{24,16},{1,9},{9,1},{17,25},{25,17},{2,10},{10... | collective-permute-start | bytes 663560 | tf_op jit(solution)/shard_map/ppermute | solution.py:350
  53.0 24.9 %all-to-all-start.1 = ((f32[32,1,2304]{2,1,0:T(1,128)}), f32[32,1,2304]{2,1,0:T(1,128)S(1)}, u32[]{:S(2)}, u32[]{:S(2)}) async-start(f32[32,1,2304]{2,1,0:T(1,128)} %copy.28), calls=%async_computation.1 | async-start | bytes 589824 | tf_op jit(solution)/shard_map/all_to_all | solution.py:463
  57.0 11.0 %collective-permute-start.12 = (bf16[6,48,384]{2,1,0:T(8,128)(2,1)}, bf16[6,48,384]{2,1,0:T(8,128)(2,1)S(1)}, u32[]{:S(2)}, u32[]{:S(2)}) collective-permute-start(bf16[6,48,384]{2,1,0:T(8,128)(2,1)} %slice.180), channel_id=1, source_target_pairs={{0,16},{8,24},{16,0},{24,8},{1,17},{9,25},{17,1},{25,9},{2,18},{10... | collective-permute-start | bytes 663560 | tf_op jit(solution)/shard_map/ppermute | solution.py:350
  59.6 21.3 %collective-permute-start.17 = (bf16[6,48,384]{2,1,0:T(8,128)(2,1)}, bf16[6,48,384]{2,1,0:T(8,128)(2,1)S(1)}, u32[]{:S(2)}, u32[]{:S(2)}) collective-permute-start(bf16[6,48,384]{2,1,0:T(8,128)(2,1)} %slice.228), channel_id=1, source_target_pairs={{0,8},{8,0},{16,24},{24,16},{1,9},{9,1},{17,25},{25,17},{2,10},{10... | collective-permute-start | bytes 663560 | tf_op jit(solution)/shard_map/ppermute | solution.py:350
  61.1 17.1 %collective-permute-start.2 = (bf16[12,48,384]{2,1,0:T(8,128)(2,1)}, bf16[12,48,384]{2,1,0:T(8,128)(2,1)S(1)}, u32[]{:S(2)}, u32[]{:S(2)}) collective-permute-start(bf16[12,48,384]{2,1,0:T(8,128)(2,1)} %collective-permute-done.1.refs_10_), channel_id=1, source_target_pairs={{0,8},{8,0},{16,24},{24,16},{1,9},{9,1},{17,25},{25,17},{2,10},{10... | collective-permute-start | bytes 1327112 | tf_op jit(solution)/shard_map/ppermute | solution.py:350
  64.2 13.6 %collective-permute-start.16 = (bf16[12,48,384]{2,1,0:T(8,128)(2,1)}, bf16[12,48,384]{2,1,0:T(8,128)(2,1)S(1)}, u32[]{:S(2)}, u32[]{:S(2)}) collective-permute-start(bf16[12,48,384]{2,1,0:T(8,128)(2,1)} %collective-permute-done.1.refs_10_), channel_id=1, source_target_pairs={{0,16},{8,24},{16,0},{24,8},{1,17},{9,25},{17,1},{25,9},{2,18},{10... | collective-permute-start | bytes 1327112 | tf_op jit(solution)/shard_map/ppermute | solution.py:350
  68.0 14.6 %collective-permute-start.18 = (bf16[6,48,384]{2,1,0:T(8,128)(2,1)}, bf16[6,48,384]{2,1,0:T(8,128)(2,1)S(1)}, u32[]{:S(2)}, u32[]{:S(2)}) collective-permute-start(bf16[6,48,384]{2,1,0:T(8,128)(2,1)} %slice.229), channel_id=1, source_target_pairs={{0,16},{8,24},{16,0},{24,8},{1,17},{9,25},{17,1},{25,9},{2,18},{10... | collective-permute-start | bytes 663560 | tf_op jit(solution)/shard_map/ppermute | solution.py:350
  77.8 14.4 %collective-permute-start.15 = (bf16[60,48,384]{2,1,0:T(8,128)(2,1)}, bf16[60,48,384]{2,1,0:T(8,128)(2,1)}, u32[]{:S(2)}, u32[]{:S(2)}) collective-permute-start(bf16[60,48,384]{2,1,0:T(8,128)(2,1)} %constant_dynamic-update-slice_fusion.8), channel_id=1, source_target_pairs={{0,1},{1,0},{2,3},{3,2},{4,5},{5,4},{6,7},{7,6},{8,9},{9,8},{10,11... | collective-permute-start | bytes 6635528 | tf_op jit(solution)/shard_map/ppermute | solution.py:342
  78.2 7.7 %collective-permute-start.19 = (bf16[6,48,384]{2,1,0:T(8,128)(2,1)S(1)}, bf16[6,48,384]{2,1,0:T(8,128)(2,1)S(1)}, u32[]{:S(2)}, u32[]{:S(2)}) collective-permute-start(bf16[6,48,384]{2,1,0:T(8,128)(2,1)S(1)} %slice.230), channel_id=1, source_target_pairs={{0,8},{8,0},{16,24},{24,16},{1,9},{9,1},{17,25},{25,17},{2,10},{10... | collective-permute-start | bytes 663560 | tf_op jit(solution)/shard_map/ppermute | solution.py:350
  80.9 7.5 %collective-permute-start.20 = (bf16[6,48,384]{2,1,0:T(8,128)(2,1)S(1)}, bf16[6,48,384]{2,1,0:T(8,128)(2,1)S(1)}, u32[]{:S(2)}, u32[]{:S(2)}) collective-permute-start(bf16[6,48,384]{2,1,0:T(8,128)(2,1)S(1)} %slice.184), channel_id=1, source_target_pairs={{0,16},{8,24},{16,0},{24,8},{1,17},{9,25},{17,1},{25,9},{2,18},{10... | collective-permute-start | bytes 663560 | tf_op jit(solution)/shard_map/ppermute | solution.py:350
  89.2 4.0 %collective-permute-start.21 = (bf16[48,48,384]{2,1,0:T(8,128)(2,1)}, bf16[48,48,384]{2,1,0:T(8,128)(2,1)}, u32[]{:S(2)}, u32[]{:S(2)}) collective-permute-start(bf16[48,48,384]{2,1,0:T(8,128)(2,1)} %constant_dynamic-update-slice_fusion.14), channel_id=1, source_target_pairs={{0,1},{1,0},{2,3},{3,2},{4,5},{5,4},{6,7},{7,6},{8,9},{9,8},{10,11... | collective-permute-start | bytes 5308424 | tf_op jit(solution)/shard_map/ppermute | solution.py:342
  145.4 49.9 %collective-permute-start.22 = (bf16[4,12,48,384]{3,2,1,0:T(8,128)(2,1)}, bf16[4,12,48,384]{3,2,1,0:T(8,128)(2,1)S(1)}, u32[]{:S(2)}, u32[]{:S(2)}) collective-permute-start(bf16[4,12,48,384]{3,2,1,0:T(8,128)(2,1)} %get-tuple-element.84), channel_id=1, source_target_pairs={{0,1},{1,0},{2,3},{3,2},{4,5},{5,4},{6,7},{7,6},{8,9},{9,8},{10,11... | collective-permute-start | bytes 5308424 | tf_op jit(solution)/shard_map/ppermute | solution.py:342
  161.8 35.6 %collective-permute-start.23 = (bf16[4,12,48,384]{3,2,1,0:T(8,128)(2,1)}, bf16[4,12,48,384]{3,2,1,0:T(8,128)(2,1)}, u32[]{:S(2)}, u32[]{:S(2)}) collective-permute-start(bf16[4,12,48,384]{3,2,1,0:T(8,128)(2,1)} %get-tuple-element.86), channel_id=1, source_target_pairs={{0,1},{1,0},{2,3},{3,2},{4,5},{5,4},{6,7},{7,6},{8,9},{9,8},{10,11... | collective-permute-start | bytes 5308424 | tf_op jit(solution)/shard_map/ppermute | solution.py:342
  178.5 22.0 %collective-permute-start.24 = (bf16[4,12,48,384]{3,2,1,0:T(8,128)(2,1)}, bf16[4,12,48,384]{3,2,1,0:T(8,128)(2,1)}, u32[]{:S(2)}, u32[]{:S(2)}) collective-permute-start(bf16[4,12,48,384]{3,2,1,0:T(8,128)(2,1)} %get-tuple-element.88), channel_id=1, source_target_pairs={{0,1},{1,0},{2,3},{3,2},{4,5},{5,4},{6,7},{7,6},{8,9},{9,8},{10,11... | collective-permute-start | bytes 5308424 | tf_op jit(solution)/shard_map/ppermute | solution.py:342
  194.7 8.1 %collective-permute-start.25 = (bf16[4,12,48,384]{3,2,1,0:T(8,128)(2,1)}, bf16[4,12,48,384]{3,2,1,0:T(8,128)(2,1)}, u32[]{:S(2)}, u32[]{:S(2)}) collective-permute-start(bf16[4,12,48,384]{3,2,1,0:T(8,128)(2,1)} %get-tuple-element.90), channel_id=1, source_target_pairs={{0,1},{1,0},{2,3},{3,2},{4,5},{5,4},{6,7},{7,6},{8,9},{9,8},{10,11... | collective-permute-start | bytes 5308424 | tf_op jit(solution)/shard_map/ppermute | solution.py:342
  205.2 8.3 %collective-permute-start.30 = (bf16[6,48,384]{2,1,0:T(8,128)(2,1)S(1)}, bf16[6,48,384]{2,1,0:T(8,128)(2,1)S(1)}, u32[]{:S(2)}, u32[]{:S(2)}) collective-permute-start(bf16[6,48,384]{2,1,0:T(8,128)(2,1)S(1)} %get-tuple-element.118), channel_id=1, source_target_pairs={{0,16},{8,24},{16,0},{24,8},{1,17},{9,25},{17,1},{25,9},{2,18},{10... | collective-permute-start | bytes 663560 | tf_op jit(solution)/shard_map/ppermute | solution.py:350
  206.2 8.3 %collective-permute-start.32 = (bf16[6,48,384]{2,1,0:T(8,128)(2,1)S(1)}, bf16[6,48,384]{2,1,0:T(8,128)(2,1)S(1)}, u32[]{:S(2)}, u32[]{:S(2)}) collective-permute-start(bf16[6,48,384]{2,1,0:T(8,128)(2,1)S(1)} %get-tuple-element.117), channel_id=1, source_target_pairs={{0,8},{8,0},{16,24},{24,16},{1,9},{9,1},{17,25},{25,17},{2,10},{10... | collective-permute-start | bytes 663560 | tf_op jit(solution)/shard_map/ppermute | solution.py:350
  207.2 12.1 %collective-permute-start.27 = (bf16[6,48,384]{2,1,0:T(8,128)(2,1)S(1)}, bf16[6,48,384]{2,1,0:T(8,128)(2,1)S(1)}, u32[]{:S(2)}, u32[]{:S(2)}) collective-permute-start(bf16[6,48,384]{2,1,0:T(8,128)(2,1)S(1)} %get-tuple-element.120), channel_id=1, source_target_pairs={{0,8},{8,0},{16,24},{24,16},{1,9},{9,1},{17,25},{25,17},{2,10},{10... | collective-permute-start | bytes 663560 | tf_op jit(solution)/shard_map/ppermute | solution.py:350
  208.2 11.0 %collective-permute-start.26 = (bf16[6,48,384]{2,1,0:T(8,128)(2,1)S(1)}, bf16[6,48,384]{2,1,0:T(8,128)(2,1)S(1)}, u32[]{:S(2)}, u32[]{:S(2)}) collective-permute-start(bf16[6,48,384]{2,1,0:T(8,128)(2,1)S(1)} %get-tuple-element.121), channel_id=1, source_target_pairs={{0,16},{8,24},{16,0},{24,8},{1,17},{9,25},{17,1},{25,9},{2,18},{10... | collective-permute-start | bytes 663560 | tf_op jit(solution)/shard_map/ppermute | solution.py:350
  210.4 26.7 %collective-permute-start.29 = (bf16[12,48,384]{2,1,0:T(8,128)(2,1)S(1)}, bf16[12,48,384]{2,1,0:T(8,128)(2,1)S(1)}, u32[]{:S(2)}, u32[]{:S(2)}) collective-permute-start(bf16[12,48,384]{2,1,0:T(8,128)(2,1)S(1)} %get-tuple-element.127), channel_id=1, source_target_pairs={{0,8},{8,0},{16,24},{24,16},{1,9},{9,1},{17,25},{25,17},{2,10},{10... | collective-permute-start | bytes 1327112 | tf_op jit(solution)/shard_map/ppermute | solution.py:350
  219.5 17.6 %collective-permute-start.33 = (bf16[12,48,384]{2,1,0:T(8,128)(2,1)S(1)}, bf16[12,48,384]{2,1,0:T(8,128)(2,1)S(1)}, u32[]{:S(2)}, u32[]{:S(2)}) collective-permute-start(bf16[12,48,384]{2,1,0:T(8,128)(2,1)S(1)} %pad_maximum_fusion.3), channel_id=1, source_target_pairs={{0,16},{8,24},{16,0},{24,8},{1,17},{9,25},{17,1},{25,9},{2,18},{10... | collective-permute-start | bytes 1327112 | tf_op jit(solution)/shard_map/ppermute | solution.py:350
  220.8 16.3 %collective-permute-start.31 = (bf16[12,48,384]{2,1,0:T(8,128)(2,1)S(1)}, bf16[12,48,384]{2,1,0:T(8,128)(2,1)S(1)}, u32[]{:S(2)}, u32[]{:S(2)}) collective-permute-start(bf16[12,48,384]{2,1,0:T(8,128)(2,1)S(1)} %pad_maximum_fusion.2), channel_id=1, source_target_pairs={{0,8},{8,0},{16,24},{24,16},{1,9},{9,1},{17,25},{25,17},{2,10},{10... | collective-permute-start | bytes 1327112 | tf_op jit(solution)/shard_map/ppermute | solution.py:350
  221.7 25.5 %collective-permute-start.28 = (bf16[12,48,384]{2,1,0:T(8,128)(2,1)S(1)}, bf16[12,48,384]{2,1,0:T(8,128)(2,1)}, u32[]{:S(2)}, u32[]{:S(2)}) collective-permute-start(bf16[12,48,384]{2,1,0:T(8,128)(2,1)S(1)} %get-tuple-element.130), channel_id=1, source_target_pairs={{0,16},{8,24},{16,0},{24,8},{1,17},{9,25},{17,1},{25,9},{2,18},{10... | collective-permute-start | bytes 1327112 | tf_op jit(solution)/shard_map/ppermute | solution.py:350
  238.4 11.5 %collective-permute-start.36 = (bf16[12,48,384]{2,1,0:T(8,128)(2,1)}, bf16[12,48,384]{2,1,0:T(8,128)(2,1)}, u32[]{:S(2)}, u32[]{:S(2)}) collective-permute-start(bf16[12,48,384]{2,1,0:T(8,128)(2,1)} %get-tuple-element.98), channel_id=1, source_target_pairs={{0,2},{1,3},{2,0},{3,1},{4,6},{5,7},{6,4},{7,5},{8,10},{9,11},{10,... | collective-permute-start | bytes 1327112 | tf_op jit(solution)/shard_map/ppermute | solution.py:346
  239.7 11.4 %collective-permute-start.35 = (bf16[12,48,384]{2,1,0:T(8,128)(2,1)}, bf16[12,48,384]{2,1,0:T(8,128)(2,1)}, u32[]{:S(2)}, u32[]{:S(2)}) collective-permute-start(bf16[12,48,384]{2,1,0:T(8,128)(2,1)} %get-tuple-element.97), channel_id=1, source_target_pairs={{0,16},{8,24},{16,0},{24,8},{1,17},{9,25},{17,1},{25,9},{2,18},{10... | collective-permute-start | bytes 1327112 | tf_op jit(solution)/shard_map/ppermute | solution.py:350
  241.0 12.1 %collective-permute-start.34 = (bf16[12,48,384]{2,1,0:T(8,128)(2,1)S(1)}, bf16[12,48,384]{2,1,0:T(8,128)(2,1)}, u32[]{:S(2)}, u32[]{:S(2)}) collective-permute-start(bf16[12,48,384]{2,1,0:T(8,128)(2,1)S(1)} %get-tuple-element.96), channel_id=1, source_target_pairs={{0,8},{8,0},{16,24},{24,16},{1,9},{9,1},{17,25},{25,17},{2,10},{10... | collective-permute-start | bytes 1327112 | tf_op jit(solution)/shard_map/ppermute | solution.py:350
  243.4 17.4 %all-to-all-start.2 = ((bf16[32,2,2304]{2,1,0:T(2,128)(2,1)}), bf16[32,2,2304]{2,1,0:T(2,128)(2,1)S(1)}, u32[]{:S(2)}, u32[]{:S(2)}) async-start(bf16[32,2,2304]{2,1,0:T(2,128)(2,1)} %reshape.181), calls=%async_computation.2 | async-start | bytes 589824 | tf_op jit(solution)/shard_map/all_to_all | solution.py:426
  255.9 9.3 %collective-permute-start.38 = (bf16[12,48,384]{2,1,0:T(8,128)(2,1)S(1)}, bf16[12,48,384]{2,1,0:T(8,128)(2,1)}, u32[]{:S(2)}, u32[]{:S(2)}) collective-permute-start(bf16[12,48,384]{2,1,0:T(8,128)(2,1)S(1)} %get-tuple-element.100), channel_id=1, source_target_pairs={{0,16},{8,24},{16,0},{24,8},{1,17},{9,25},{17,1},{25,9},{2,18},{10... | collective-permute-start | bytes 1327112 | tf_op jit(solution)/shard_map/ppermute | solution.py:350
  256.1 9.8 %collective-permute-start.37 = (bf16[12,48,384]{2,1,0:T(8,128)(2,1)}, bf16[12,48,384]{2,1,0:T(8,128)(2,1)}, u32[]{:S(2)}, u32[]{:S(2)}) collective-permute-start(bf16[12,48,384]{2,1,0:T(8,128)(2,1)} %get-tuple-element.99), channel_id=1, source_target_pairs={{0,8},{8,0},{16,24},{24,16},{1,9},{9,1},{17,25},{25,17},{2,10},{10... | collective-permute-start | bytes 1327112 | tf_op jit(solution)/shard_map/ppermute | solution.py:350
  257.9 14.6 %collective-permute-start.39 = (bf16[6,48,384]{2,1,0:T(8,128)(2,1)S(1)}, bf16[6,48,384]{2,1,0:T(8,128)(2,1)S(1)}, u32[]{:S(2)}, u32[]{:S(2)}) collective-permute-start(bf16[6,48,384]{2,1,0:T(8,128)(2,1)S(1)} %get-tuple-element.133), channel_id=1, source_target_pairs={{0,4},{1,5},{2,6},{3,7},{4,0},{5,1},{6,2},{7,3},{8,12},{9,13},{10,... | collective-permute-start | bytes 663560 | tf_op jit(solution)/shard_map/ppermute | solution.py:346
  260.3 16.3 %collective-permute-start.43 = (bf16[6,48,384]{2,1,0:T(8,128)(2,1)}, bf16[6,48,384]{2,1,0:T(8,128)(2,1)S(1)}, u32[]{:S(2)}, u32[]{:S(2)}) collective-permute-start(bf16[6,48,384]{2,1,0:T(8,128)(2,1)} %get-tuple-element.132), channel_id=1, source_target_pairs={{0,4},{1,5},{2,6},{3,7},{4,0},{5,1},{6,2},{7,3},{8,12},{9,13},{10,... | collective-permute-start | bytes 663560 | tf_op jit(solution)/shard_map/ppermute | solution.py:346
  272.5 11.2 %collective-permute-start.40 = (bf16[12,48,384]{2,1,0:T(8,128)(2,1)S(1)}, bf16[12,48,384]{2,1,0:T(8,128)(2,1)S(1)}, u32[]{:S(2)}, u32[]{:S(2)}) collective-permute-start(bf16[12,48,384]{2,1,0:T(8,128)(2,1)S(1)} %get-tuple-element.102), channel_id=1, source_target_pairs={{0,8},{8,0},{16,24},{24,16},{1,9},{9,1},{17,25},{25,17},{2,10},{10... | collective-permute-start | bytes 1327112 | tf_op jit(solution)/shard_map/ppermute | solution.py:350
  273.1 11.7 %collective-permute-start.41 = (bf16[12,48,384]{2,1,0:T(8,128)(2,1)S(1)}, bf16[12,48,384]{2,1,0:T(8,128)(2,1)S(1)}, u32[]{:S(2)}, u32[]{:S(2)}) collective-permute-start(bf16[12,48,384]{2,1,0:T(8,128)(2,1)S(1)} %get-tuple-element.103), channel_id=1, source_target_pairs={{0,16},{8,24},{16,0},{24,8},{1,17},{9,25},{17,1},{25,9},{2,18},{10... | collective-permute-start | bytes 1327112 | tf_op jit(solution)/shard_map/ppermute | solution.py:350
  274.8 11.1 %collective-permute-start.42 = (bf16[12,48,384]{2,1,0:T(8,128)(2,1)S(1)}, bf16[12,48,384]{2,1,0:T(8,128)(2,1)S(1)}, u32[]{:S(2)}, u32[]{:S(2)}) collective-permute-start(bf16[12,48,384]{2,1,0:T(8,128)(2,1)S(1)} %fusion.17), channel_id=1, source_target_pairs={{0,2},{1,3},{2,0},{3,1},{4,6},{5,7},{6,4},{7,5},{8,10},{9,11},{10,... | collective-permute-start | bytes 1327112 | tf_op jit(solution)/shard_map/ppermute | solution.py:346
  (35 other events, 354.9 us)
